TPU v7x, 32 devices: a whole 2x2x4 slice. The times are simulated.
32 devices in a mesh: dp: 4 (over y, core), fsdp: 8 (over z, x).
Axes of the slice: x: 2, y: 2, z: 4, core: 2. Of those that a mesh axis runs over, the one named last changes fastest.
Arguments:
- history: bfloat16 [9, 8192, 2048], P(None, ('dp', 'fsdp')), may hold values from -6 to 6
- out_grad: bfloat16 [8192, 2048], P(('dp', 'fsdp')), may hold values from -6 to 6
- doc_lengths: int32 [32, 3], P(('dp', 'fsdp')), may hold values from 1 to 170, 256 in all within a row
- doc_domain: int32 [32, 3], P(('dp', 'fsdp')), may hold values from 0 to 21
- domain_weight: int32 [22], replicated, may hold values from 64 to 511
- attn_weight: bfloat16 [4, 2048, 2048], P(None, 'fsdp')
- attn_master: float32 [4, 2048, 2048], P(None, 'fsdp', 'dp')
- attn_moment: float32 [4, 2048, 2048], P(None, 'fsdp', 'dp'), may hold values from -240 to 240
- mlp_weight: bfloat16 [2, 2048, 8192], P(None, 'fsdp'), may hold values from -0.125 to 0.125
- mlp_master: float32 [2, 2048, 8192], P(None, 'fsdp', 'dp'), may hold values from -0.125 to 0.125
- mlp_moment: float32 [2, 2048, 8192], P(None, 'fsdp', 'dp'), may hold values from -360 to 360
- params: float32 [53, 2048], P(None, 'fsdp')
- params_m: float32 [53, 2048], P(None, 'fsdp'), may hold values from -12 to 12
- params_v: float32 [53, 2048], P(None, 'fsdp'), may hold values from 4 to 400
- mix_out: float32 [37, 36], replicated, may hold values from -0.9 to 0.9
- mix_out_m: float32 [37, 36], replicated, may hold values from -12 to 12
- mix_out_v: float32 [37, 36], replicated, may hold values from 4 to 400
Outputs:
- layer_out: bfloat16 [8192, 2048], P(('dp', 'fsdp'))
- history_grad: bfloat16 [9, 8192, 2048], P(None, ('dp', 'fsdp'))
- attn_grad: float32 [4, 2048, 2048], P(None, 'fsdp', 'dp')
- attn_moment_new: float32 [4, 2048, 2048], P(None, 'fsdp', 'dp')
- attn_master_new: float32 [4, 2048, 2048], P(None, 'fsdp', 'dp')
- attn_copy: bfloat16 [4, 2048, 2048], P(None, 'fsdp')
- mlp_grad: float32 [2, 2048, 8192], P(None, 'fsdp', 'dp')
- mlp_moment_new: float32 [2, 2048, 8192], P(None, 'fsdp', 'dp')
- mlp_master_new: float32 [2, 2048, 8192], P(None, 'fsdp', 'dp')
- mlp_copy: bfloat16 [2, 2048, 8192], P(None, 'fsdp')
- params_grad: float32 [53, 2048], P(None, 'fsdp')
- residual_bias_grad: float32 [2, 2048], P(None, 'fsdp')
- params_m_new: float32 [53, 2048], P(None, 'fsdp')
- params_v_new: float32 [53, 2048], P(None, 'fsdp')
- params_new: float32 [53, 2048], P(None, 'fsdp')
- mix_out_grad: float32 [37, 36], replicated
- mix_out_m_new: float32 [37, 36], replicated
- mix_out_v_new: float32 [37, 36], replicated
- mix_out_new: float32 [37, 36], replicated
Inputs may be any that keep to these rules, and one draw needn't show every extreme that they name: `doc_lengths`: each packed row holds 3 document lengths that sum to 256; the longest is exactly 170.
All inputs are finite; a program needn't handle non-finite values.
Results may differ from a plain program's by a relative error of at most 0.007.
The roundings to bfloat16 on the way count: a program that leaves them out, or rounds other values in their place, can miss the bound.
Values may be sent and summed in bfloat16 or wider, within the bound.
No kernel may reach another device: no remote copies, remote signals or barrier semaphores. Data moves between devices by JAX's collectives and lax.ppermute only.
A program may use at most 704 MiB of HBM per device.

v0:
```python
import math

import jax
import jax.numpy as jnp
from jax import lax
from jax.sharding import PartitionSpec as P

HEADS = 16
HEAD = 128
FF = 8192
ROT = 32
MIXW = 36
DOCS = 3
NDOM = 22
STEP = 6


NS_A = 3.4445
NS_B = -4.775
NS_C = 2.0315
ROPE_BASE = 10000.0
LR_MUON = 0.1
LR_ADAM = 0.03
DECAY = 0.01
MOMENTUM = 0.95
BETA_ONE = 0.9
BETA_TWO = 0.95
HIGHEST = lax.Precision.HIGHEST


def rounded(values):
    return lax.optimization_barrier(values.astype(jnp.bfloat16)).astype(jnp.float32)


def exact_gelu(values):
    return jax.nn.gelu(values, approximate=False)


def rope_tables(tok_count):
    half_rot = ROT // 2
    inverse_freq = ROPE_BASE ** (-(2.0 * jnp.arange(half_rot, dtype=jnp.float32)) / ROT)
    angles = jnp.arange(tok_count, dtype=jnp.float32)[:, None] * inverse_freq[None, :]
    return (jnp.cos(angles)[:, None, :], jnp.sin(angles)[:, None, :])


def rotate(values, cosine, sine_tab):
    half_rot = cosine.shape[-1]
    first_half = values[..., :half_rot]
    second_half = values[..., half_rot : 2 * half_rot]
    remain = values[..., 2 * half_rot :]
    return jnp.concatenate(
        [
            first_half * cosine - second_half * sine_tab,
            second_half * cosine + first_half * sine_tab,
            remain,
        ],
        -1,
    )


def layer_norm(values, gain_row, shift_row):
    centred = values - jnp.mean(values, -1, keepdims=True)
    inv_std = lax.rsqrt(jnp.mean(centred * centred, -1, keepdims=True) + 1e-05)
    normed = centred * inv_std
    return (normed * gain_row + shift_row, normed, inv_std)


def norm_back(grad_out, normed, inv_std, gain_row):
    scaled = grad_out * gain_row
    grad_in = inv_std * (
        scaled
        - jnp.mean(scaled, -1, keepdims=True)
        - normed * jnp.mean(scaled * normed, -1, keepdims=True)
    )
    return (grad_in, jnp.sum(grad_out * normed, 0), jnp.sum(grad_out, 0))


def product_nt(left_side, right_side):
    return lax.dot_general(
        left_side, right_side, (((1,), (1,)), ((), ())), preferred_element_type=jnp.float32
    )


def product_tn(left_side, right_side):
    return lax.dot_general(
        left_side, right_side, (((0,), (0,)), ((), ())), preferred_element_type=jnp.float32
    )


def pack_info(lengths, domains, weight_table, tok_count):
    doc_ends = jnp.cumsum(lengths)
    positions = jnp.arange(tok_count, dtype=jnp.int32)
    doc_of = jnp.sum((positions[:, None] >= doc_ends[None, :]).astype(jnp.int32), 1)
    allowed = (doc_of[:, None] == doc_of[None, :]) & (positions[:, None] >= positions[None, :])
    domain = jnp.sum(
        jnp.where(
            doc_of[:, None] == jnp.arange(DOCS, dtype=jnp.int32)[None, :], domains[None, :], 0
        ),
        1,
    )
    weight = jnp.sum(
        jnp.where(
            domain[:, None] == jnp.arange(NDOM, dtype=jnp.int32)[None, :], weight_table[None, :], 0
        ),
        1,
    )
    return (allowed, weight.astype(jnp.float32) / 256.0)


def col_term(left_side, right_side):
    return product_tn(right_side, left_side)


def gram_of(blocks):
    return jnp.einsum("mik,mjk->mij", blocks, blocks, precision=HIGHEST)


def newton_step(current, gram_mat):
    poly_mat = NS_B * gram_mat + NS_C * jnp.einsum(
        "mij,mjk->mik", gram_mat, gram_mat, precision=HIGHEST
    )
    return NS_A * current + jnp.einsum("mij,mjk->mik", poly_mat, current, precision=HIGHEST)


def adamw(current, grad_in, moment_one, moment_two):
    one_new = BETA_ONE * moment_one + (1.0 - BETA_ONE) * grad_in
    two_new = BETA_TWO * moment_two + (1.0 - BETA_TWO) * grad_in * grad_in
    one_hat = one_new / (1.0 - BETA_ONE**STEP)
    two_hat = two_new / (1.0 - BETA_TWO**STEP)
    updated = current * (1.0 - LR_ADAM * DECAY) - LR_ADAM * one_hat / (jnp.sqrt(two_hat) + 1e-08)
    return (one_new, two_new, updated)


def body(
    history,
    out_grad,
    doc_lengths,
    doc_domain,
    domain_weight,
    attn_weight,
    attn_master,
    attn_moment,
    mlp_weight,
    mlp_master,
    mlp_moment,
    params,
    params_m,
    params_v,
    mix_out,
    mix_out_m,
    mix_out_v,
):
    hist_count, tok_count, model_width = history.shape
    head_scale = 1.0 / math.sqrt(HEAD)
    full_attn, full_mlp, full_params = (
        lax.all_gather(attn_weight, "fsdp", axis=1, tiled=True),
        lax.all_gather(mlp_weight, "fsdp", axis=1, tiled=True),
        lax.all_gather(params.astype(jnp.bfloat16), "fsdp", axis=1, tiled=True),
    )
    param_vals = full_params.astype(jnp.float32)
    mix_weight = full_params[17:]
    mixing = rounded(mix_out)
    allowed, tok_weight = pack_info(doc_lengths[0], doc_domain[0], domain_weight, tok_count)
    last_hist = history[hist_count - 1].astype(jnp.float32)
    inv_rms = lax.rsqrt(jnp.mean(last_hist * last_hist, -1, keepdims=True) + 1e-06)
    unit_rms = last_hist * inv_rms
    unit_low = unit_rms.astype(jnp.bfloat16)
    inner_pre = product_nt(unit_low, mix_weight)
    hidden, gelu_inner = jax.vjp(exact_gelu, inner_pre)
    coeffs = (
        jnp.dot(hidden, mixing[:MIXW], precision=HIGHEST, preferred_element_type=jnp.float32)
        + mixing[MIXW]
    ).reshape(tok_count, 4, hist_count)
    streams = []
    for member in range(4):
        running = coeffs[:, member, 0, None] * history[0].astype(jnp.float32)
        for source in range(1, hist_count):
            running = running + coeffs[:, member, source, None] * history[source].astype(
                jnp.float32
            )
        streams.append(running)
    normed_low = []
    norm_keep = []
    for member in range(4):
        result, normed, inv_std = layer_norm(
            streams[member], param_vals[member], param_vals[4 + member]
        )
        normed_low.append(result.astype(jnp.bfloat16))
        norm_keep.append((normed, inv_std))
    cosine, sine_tab = rope_tables(tok_count)
    q_pre = jnp.dot(normed_low[0], full_attn[0], preferred_element_type=jnp.float32) + param_vals[8]
    k_pre = jnp.dot(normed_low[1], full_attn[1], preferred_element_type=jnp.float32) + param_vals[9]
    value_low = (
        (jnp.dot(normed_low[2], full_attn[2], preferred_element_type=jnp.float32) + param_vals[10])
        .astype(jnp.bfloat16)
        .reshape(tok_count, HEADS, HEAD)
    )
    query_low = rotate(q_pre.reshape(tok_count, HEADS, HEAD), cosine, sine_tab).astype(jnp.bfloat16)
    key_low = rotate(k_pre.reshape(tok_count, HEADS, HEAD), cosine, sine_tab).astype(jnp.bfloat16)
    scores = (
        jnp.einsum("qhd,khd->hqk", query_low, key_low, preferred_element_type=jnp.float32)
        * head_scale
    )
    scores = jnp.where(allowed[None], scores, -1000000000.0)
    top_score = jnp.max(scores, -1, keepdims=True)
    log_total = top_score + jnp.log(jnp.sum(jnp.exp(scores - top_score), -1, keepdims=True))
    probs_low = jnp.exp(scores - log_total).astype(jnp.bfloat16)
    context = jnp.einsum(
        "hqk,khd->qhd", probs_low, value_low, preferred_element_type=jnp.float32
    ).reshape(tok_count, model_width)
    context_low = context.astype(jnp.bfloat16)
    attn_out = (
        jnp.dot(context_low, full_attn[3], preferred_element_type=jnp.float32) + param_vals[11]
    )
    up_pre = jnp.dot(normed_low[3], full_mlp[0], preferred_element_type=jnp.float32) + param_vals[
        13:17
    ].reshape(-1)
    act_val, gelu_up = jax.vjp(exact_gelu, up_pre)
    act_low = act_val.astype(jnp.bfloat16)
    mlp_out = product_nt(act_low, full_mlp[1]) + param_vals[12]
    layer_out = (streams[3] + attn_out + mlp_out).astype(jnp.bfloat16)
    back_attn, back_mlp = (
        lax.all_gather(attn_weight, "fsdp", axis=1, tiled=True),
        lax.all_gather(mlp_weight, "fsdp", axis=1, tiled=True),
    )
    out_cot = out_grad.astype(jnp.float32) * tok_weight[:, None]
    cot_low = out_cot.astype(jnp.bfloat16)
    act_grad = jnp.dot(cot_low, back_mlp[1], preferred_element_type=jnp.float32)
    up_grad = gelu_up(act_grad)[0].astype(jnp.bfloat16)
    mlp_in_grad = product_nt(up_grad, back_mlp[0])
    stream_three, gain_three, shift_three = norm_back(
        mlp_in_grad, norm_keep[3][0], norm_keep[3][1], param_vals[3]
    )
    stream_three = out_cot + stream_three
    ctx_grad = (
        product_nt(cot_low, back_attn[3]).astype(jnp.bfloat16).reshape(tok_count, HEADS, HEAD)
    )
    scores_again = (
        jnp.einsum("qhd,khd->hqk", query_low, key_low, preferred_element_type=jnp.float32)
        * head_scale
    )
    scores_again = jnp.where(allowed[None], scores_again, -1000000000.0)
    probs_again = jnp.exp(scores_again - log_total)
    prob_grad = jnp.einsum("qhd,khd->hqk", ctx_grad, value_low, preferred_element_type=jnp.float32)
    score_grad = (
        probs_again * (prob_grad - jnp.sum(probs_again * prob_grad, -1, keepdims=True))
    ).astype(jnp.bfloat16)
    value_grad = (
        jnp.einsum(
            "hqk,qhd->khd",
            probs_again.astype(jnp.bfloat16),
            ctx_grad,
            preferred_element_type=jnp.float32,
        )
        .reshape(tok_count, model_width)
        .astype(jnp.bfloat16)
    )
    query_grad = (
        jnp.einsum("hqk,khd->qhd", score_grad, key_low, preferred_element_type=jnp.float32)
        * head_scale
    )
    key_grad = (
        jnp.einsum("hqk,qhd->khd", score_grad, query_low, preferred_element_type=jnp.float32)
        * head_scale
    )
    query_back = (
        rotate(query_grad, cosine, -sine_tab).reshape(tok_count, model_width).astype(jnp.bfloat16)
    )
    key_back = (
        rotate(key_grad, cosine, -sine_tab).reshape(tok_count, model_width).astype(jnp.bfloat16)
    )
    proj_grads = (query_back, key_back, value_grad)
    stream_grads = []
    gain_list = []
    shift_list = []
    for member in range(3):
        in_grad = product_nt(proj_grads[member], back_attn[member])
        grad_stream, gain_part, shift_part = norm_back(
            in_grad, norm_keep[member][0], norm_keep[member][1], param_vals[member]
        )
        stream_grads.append(grad_stream)
        gain_list.append(gain_part)
        shift_list.append(shift_part)
    stream_grads.append(stream_three)
    gain_list.append(gain_three)
    shift_list.append(shift_three)
    stream_stack = jnp.stack(stream_grads)
    coef_cols = []
    for source in range(hist_count):
        coef_cols.append(
            jnp.einsum(
                "sd,ksd->sk", history[source].astype(jnp.float32), stream_stack, precision=HIGHEST
            )
        )
    coef_grad = jnp.stack(coef_cols, -1)
    coef_flat = coef_grad.reshape(tok_count, 4 * hist_count)
    mixing_grad = jnp.concatenate(
        [
            jnp.dot(hidden.T, coef_flat, precision=HIGHEST, preferred_element_type=jnp.float32),
            jnp.sum(coef_flat, 0)[None],
        ],
        0,
    )
    hidden_grad = jnp.dot(
        coef_flat, mixing[:MIXW].T, precision=HIGHEST, preferred_element_type=jnp.float32
    )
    inner_grad = gelu_inner(hidden_grad)[0].astype(jnp.bfloat16)
    mix_weight_grad = product_tn(inner_grad, unit_low)
    unit_grad = jnp.dot(inner_grad, mix_weight, preferred_element_type=jnp.float32)
    last_grad = inv_rms * (unit_grad - unit_rms * jnp.mean(unit_grad * unit_rms, -1, keepdims=True))
    hist_parts = []
    for source in range(hist_count):
        running = coeffs[:, 0, source, None] * stream_grads[0]
        for member in range(1, 4):
            running = running + coeffs[:, member, source, None] * stream_grads[member]
        if source == hist_count - 1:
            running = running + last_grad
        hist_parts.append(running.astype(jnp.bfloat16))
    history_grad = jnp.stack(hist_parts)
    out_bias_grad = jnp.sum(cot_low.astype(jnp.float32), 0)
    param_grad = jnp.concatenate(
        [
            jnp.stack(gain_list),
            jnp.stack(shift_list),
            jnp.stack(
                [
                    jnp.sum(query_back.astype(jnp.float32), 0),
                    jnp.sum(key_back.astype(jnp.float32), 0),
                    jnp.sum(value_grad.astype(jnp.float32), 0),
                ]
            ),
            out_bias_grad[None],
            out_bias_grad[None],
            jnp.sum(up_grad.astype(jnp.float32), 0).reshape(4, model_width),
            mix_weight_grad,
        ],
        0,
    )
    lefts = (normed_low[0], normed_low[1], normed_low[2], context_low, normed_low[3], cot_low)
    rights = (query_back, key_back, value_grad, cot_low, up_grad, act_low)
    col_parts = []
    for member in range(6):
        col_parts.append(
            lax.psum_scatter(
                col_term(lefts[member], rights[member]), "dp", scatter_dimension=0, tiled=True
            )
        )
    summed = (
        lax.psum_scatter(col_parts[0], "fsdp", scatter_dimension=1, tiled=True),
        lax.psum_scatter(col_parts[1], "fsdp", scatter_dimension=1, tiled=True),
        lax.psum_scatter(col_parts[2], "fsdp", scatter_dimension=1, tiled=True),
        lax.psum_scatter(col_parts[3], "fsdp", scatter_dimension=1, tiled=True),
        lax.psum_scatter(col_parts[4], "fsdp", scatter_dimension=1, tiled=True),
        lax.psum_scatter(col_parts[5], "fsdp", scatter_dimension=1, tiled=True),
        lax.psum_scatter(param_grad, "fsdp", scatter_dimension=1, tiled=True),
    )
    param_part = lax.psum(summed[6], "dp")
    pieces = [summed[member].T for member in range(6)]
    attn_grad = jnp.stack(pieces[:4])
    mlp_grad = jnp.stack(pieces[4:])
    mixing_grad = lax.psum(mixing_grad, ("dp", "fsdp"))
    attn_mom = MOMENTUM * attn_moment + attn_grad
    mlp_mom = MOMENTUM * mlp_moment + mlp_grad
    attn_cur = attn_mom
    mlp_cur = mlp_mom
    for ns_section in range(5):
        attn_gram, mlp_gram = lax.psum((gram_of(attn_cur), gram_of(mlp_cur)), "dp")
        if ns_section == 0:
            attn_norm = jnp.sqrt(jnp.trace(attn_gram, axis1=1, axis2=2)) + 1e-07
            mlp_norm = jnp.sqrt(jnp.trace(mlp_gram, axis1=1, axis2=2)) + 1e-07
            attn_cur = attn_cur / attn_norm[:, None, None]
            mlp_cur = mlp_cur / mlp_norm[:, None, None]
            attn_gram = attn_gram / (attn_norm * attn_norm)[:, None, None]
            mlp_gram = mlp_gram / (mlp_norm * mlp_norm)[:, None, None]
        attn_cur = newton_step(attn_cur, attn_gram)
        mlp_cur = newton_step(mlp_cur, mlp_gram)
    attn_new = (
        attn_master * (1.0 - LR_MUON * DECAY) - LR_MUON * 0.2 * math.sqrt(model_width) * attn_cur
    )
    mlp_new = mlp_master * (1.0 - LR_MUON * DECAY) - LR_MUON * 0.2 * math.sqrt(FF) * mlp_cur
    attn_copy, mlp_copy = (
        lax.all_gather(attn_new.astype(jnp.bfloat16), "dp", axis=2, tiled=True),
        lax.all_gather(mlp_new.astype(jnp.bfloat16), "dp", axis=2, tiled=True),
    )
    params_m_new, params_v_new, params_new = adamw(params, param_part, params_m, params_v)
    mix_out_m_new, mix_out_v_new, mix_out_new = adamw(mix_out, mixing_grad, mix_out_m, mix_out_v)
    return (
        layer_out,
        history_grad,
        attn_grad,
        attn_mom,
        attn_new,
        attn_copy,
        mlp_grad,
        mlp_mom,
        mlp_new,
        mlp_copy,
        param_part,
        param_part[11:13],
        params_m_new,
        params_v_new,
        params_new,
        mixing_grad,
        mix_out_m_new,
        mix_out_v_new,
        mix_out_new,
    )


def solution(mesh):
    in_specs = (
        P(None, ("dp", "fsdp"), None),
        P(("dp", "fsdp"), None),
        P(("dp", "fsdp"), None),
        P(("dp", "fsdp"), None),
        P(),
        P(None, "fsdp", None),
        P(None, "fsdp", "dp"),
        P(None, "fsdp", "dp"),
        P(None, "fsdp", None),
        P(None, "fsdp", "dp"),
        P(None, "fsdp", "dp"),
        P(None, "fsdp"),
        P(None, "fsdp"),
        P(None, "fsdp"),
        P(),
        P(),
        P(),
    )
    out_specs = (
        P(("dp", "fsdp"), None),
        P(None, ("dp", "fsdp"), None),
        P(None, "fsdp", "dp"),
        P(None, "fsdp", "dp"),
        P(None, "fsdp", "dp"),
        P(None, "fsdp", None),
        P(None, "fsdp", "dp"),
        P(None, "fsdp", "dp"),
        P(None, "fsdp", "dp"),
        P(None, "fsdp", None),
        P(None, "fsdp"),
        P(None, "fsdp"),
        P(None, "fsdp"),
        P(None, "fsdp"),
        P(None, "fsdp"),
        P(),
        P(),
        P(),
        P(),
    )
    return jax.shard_map(body, mesh=mesh, in_specs=in_specs, out_specs=out_specs, check_vma=False)
```

profile of v0, /device:TPU:1, one launch (start us, length us, event | category | flops | bytes accessed | tf_op | source)
XLA Modules:
  0.0 4777.8 jit_solution(15959519052930822974)
XLA Ops:
  8.8 68.2 %all_gather.17 = bf16[53,2048]{1,0:T(8,128)(2,1)S(1)} all-gather(bf16[53,256]{1,0:T(8,128)(2,1)S(1)} %convert_element_type.335), channel_id=1, replica_groups=mesh['dp'=4,'fsdp'=8] {'fsdp'}, dimensions={1}, use_global_device_ids=true | all-gather | bytes 244224 | tf_op jit(solution)/shard_map/all_gather | solution.py:158
  111.1 541.9 %all-gather.5.cloned.1.call-done = bf16[4,2048,2048]{2,1,0:T(8,128)(2,1)} async-done(((bf16[4,256,2048]{2,1,0:T(8,128)(2,1)}), bf16[4,2048,2048]{2,1,0:T(8,128)(2,1)}) %all-gather.5.cloned.1.call-update) | async-done | bytes 33554448 | tf_op jit(solution)/shard_map/all_gather | solution.py:156
  771.3 1149.8 %all-gather.7.cloned.1.call-done = bf16[2,2048,8192]{2,1,0:T(8,128)(2,1)} async-done(((bf16[2,256,8192]{2,1,0:T(8,128)(2,1)}), bf16[2,2048,8192]{2,1,0:T(8,128)(2,1)}) %all-gather.7.cloned.1.call-update) | async-done | bytes 67108880 | tf_op jit(solution)/shard_map/all_gather | solution.py:157
  1921.1 26.9 fusion.4
  1948.0 34.4 fusion.270
  1982.6 34.0 convert_reduce_fusion
  2016.6 26.0 fusion.175
  2049.8 128.7 %reduce-scatter.18.cloned.1.call-done = f32[512,2048]{1,0:T(8,128)} async-done(((f32[2048,2048]{1,0:T(8,128)}), f32[512,2048]{1,0:T(8,128)}) %reduce-scatter.18.cloned.1.call-update) | async-done | bytes 4194320 | tf_op jit(solution)/shard_map/reduce_scatter | solution.py:344
  2178.6 128.5 %reduce-scatter.22.cloned.1.call-done = f32[512,2048]{1,0:T(8,128)} async-done(((f32[2048,2048]{1,0:T(8,128)}), f32[512,2048]{1,0:T(8,128)}) %reduce-scatter.22.cloned.1.call-update) | async-done | bytes 4194320 | tf_op jit(solution)/shard_map/reduce_scatter | solution.py:344
  2307.2 128.7 %reduce-scatter.30.cloned.1.call-done = f32[512,2048]{1,0:T(8,128)} async-done(((f32[2048,2048]{1,0:T(8,128)}), f32[512,2048]{1,0:T(8,128)}) %reduce-scatter.30.cloned.1.call-update) | async-done | bytes 4194320 | tf_op jit(solution)/shard_map/reduce_scatter | solution.py:344
  2435.9 454.9 %reduce-scatter.42.cloned.1.call-done = f32[2048,2048]{1,0:T(8,128)} async-done(((f32[8192,2048]{1,0:T(8,128)}), f32[2048,2048]{1,0:T(8,128)}) %reduce-scatter.42.cloned.1.call-update) | async-done | bytes 16777232
  2909.4 436.6 %reduce-scatter.40.cloned.1.call-done = f32[2048,2048]{1,0:T(8,128)} async-done(((f32[8192,2048]{1,0:T(8,128)}), f32[2048,2048]{1,0:T(8,128)}) %reduce-scatter.40.cloned.1.call-update) | async-done | bytes 16777232
  3400.3 37.9 reduce-scatter.28.cloned.1.call-done
  3438.2 92.2 %reduce-scatter.20.cloned.1.call-done = f32[512,256]{1,0:T(8,128)} async-done(((f32[512,2048]{1,0:T(8,128)}), f32[512,256]{1,0:T(8,128)}) %reduce-scatter.20.cloned.1.call-update) | async-done | bytes 524304 | tf_op jit(solution)/shard_map/reduce_scatter | solution.py:349
  3530.4 91.9 %reduce-scatter.24.cloned.1.call-done = f32[512,256]{1,0:T(8,128)} async-done(((f32[512,2048]{1,0:T(8,128)}), f32[512,256]{1,0:T(8,128)}) %reduce-scatter.24.cloned.1.call-update) | async-done | bytes 524304 | tf_op jit(solution)/shard_map/reduce_scatter | solution.py:350
  3622.3 92.2 %reduce-scatter.32.cloned.1.call-done = f32[512,256]{1,0:T(8,128)} async-done(((f32[512,2048]{1,0:T(8,128)}), f32[512,256]{1,0:T(8,128)}) %reduce-scatter.32.cloned.1.call-update) | async-done | bytes 524304 | tf_op jit(solution)/shard_map/reduce_scatter | solution.py:352
  3852.7 148.1 %reduce-scatter.36.cloned.1.call-done = f32[2048,256]{0,1:T(8,128)} async-done(((f32[2048,2048]{0,1:T(8,128)}), f32[2048,256]{0,1:T(8,128)}) %reduce-scatter.36.cloned.1.call-update) | async-done | bytes 2097168 | tf_op jit(solution)/shard_map/reduce_scatter | solution.py:354
  4000.8 285.9 %reduce-scatter.34.cloned.1.call-done = f32[2048,256]{0,1:T(8,128)} async-done(((f32[2048,2048]{0,1:T(8,128)}), f32[2048,256]{0,1:T(8,128)}) %reduce-scatter.34.cloned.1.call-update) | async-done | bytes 2097168 | tf_op jit(solution)/shard_map/reduce_scatter | solution.py:353
  4300.3 25.7 fusion.131
  4367.5 25.7 fusion.133
  4431.4 25.7 fusion.135
  4494.6 25.7 fusion.137
  4624.3 39.9 psum.95
  4701.2 30.9 fusion.31
  (650 shorter events, 679.9 us)
Async XLA Ops:
  7.2 645.8 %all-gather.5.cloned.1.call-start = ((), (), s32[]{:S(2)}) async-start(), calls=%async_computation.13 | async-start | bytes 37748736 | tf_op jit(solution)/shard_map/all_gather | solution.py:156
  7.9 1913.1 %all-gather.7.cloned.1.call-start = ((), (), s32[]{:S(2)}) async-start(), calls=%async_computation.14 | async-start | bytes 75497472 | tf_op jit(solution)/shard_map/all_gather | solution.py:157
  8.7 2041.1 %reduce-scatter.26.cloned.1.call-start = ((), (), s32[]{:S(2)}) async-start(), calls=%async_computation.19 | async-start | bytes 20971520 | tf_op jit(solution)/shard_map/reduce_scatter | solution.py:344
  101.3 1819.8 %copy-start.106 = (f32[1,2048]{1,0:T(1,128)}, f32[1,2048]{1,0:T(1,128)S(1)}, u32[]{:S(2)}) copy-start(f32[1,2048]{1,0:T(1,128)S(1)} %get-tuple-element.173) | copy-start | bytes 24580
  101.3 1819.8 %copy-start.114 = (f32[1,2048]{1,0:T(1,128)}, f32[1,2048]{1,0:T(1,128)S(1)}, u32[]{:S(2)}) copy-start(f32[1,2048]{1,0:T(1,128)S(1)} %get-tuple-element.174) | copy-start | bytes 24580
  707.7 1470.8 %reduce-scatter.18.cloned.1.call-start = ((), (), s32[]{:S(2)}) async-start(), calls=%async_computation.15 | async-start | bytes 20971520 | tf_op jit(solution)/shard_map/reduce_scatter | solution.py:344
  737.9 1569.1 %reduce-scatter.22.cloned.1.call-start = ((), (), s32[]{:S(2)}) async-start(), calls=%async_computation.17 | async-start | bytes 20971520 | tf_op jit(solution)/shard_map/reduce_scatter | solution.py:344
  750.5 1685.3 %reduce-scatter.30.cloned.1.call-start = ((), (), s32[]{:S(2)}) async-start(), calls=%async_computation.21 | async-start | bytes 20971520 | tf_op jit(solution)/shard_map/reduce_scatter | solution.py:344
  764.4 2126.4 %reduce-scatter.42.cloned.1.call-start = ((), (), s32[]{:S(2)}) async-start(), calls=%async_computation.29 | async-start | bytes 83886080
  1982.6 1363.5 %reduce-scatter.40.cloned.1.call-start = ((), (), s32[]{:S(2)}) async-start(), calls=%async_computation.28 | async-start | bytes 83886080
  2042.6 1395.6 %reduce-scatter.28.cloned.1.call-start = ((), (), s32[]{:S(2)}) async-start(), calls=%async_computation.20 | async-start | bytes 4718592 | tf_op jit(solution)/shard_map/reduce_scatter | solution.py:351
  2049.8 1480.6 %reduce-scatter.20.cloned.1.call-start = ((), (), s32[]{:S(2)}) async-start(), calls=%async_computation.16 | async-start | bytes 4718592 | tf_op jit(solution)/shard_map/reduce_scatter | solution.py:349
  2178.5 1443.7 %reduce-scatter.24.cloned.1.call-start = ((), (), s32[]{:S(2)}) async-start(), calls=%async_computation.18 | async-start | bytes 4718592 | tf_op jit(solution)/shard_map/reduce_scatter | solution.py:350
  2307.1 1407.3 %reduce-scatter.32.cloned.1.call-start = ((), (), s32[]{:S(2)}) async-start(), calls=%async_computation.22 | async-start | bytes 4718592 | tf_op jit(solution)/shard_map/reduce_scatter | solution.py:352
  2435.9 1564.9 %reduce-scatter.36.cloned.1.call-start = ((), (), s32[]{:S(2)}) async-start(), calls=%async_computation.25 | async-start | bytes 18874368 | tf_op jit(solution)/shard_map/reduce_scatter | solution.py:354
  2909.4 1377.4 %reduce-scatter.34.cloned.1.call-start = ((), (), s32[]{:S(2)}) async-start(), calls=%async_computation.24 | async-start | bytes 18874368 | tf_op jit(solution)/shard_map/reduce_scatter | solution.py:353
  3363.7 978.5 %all-reduce.21.cloned.1.call-start = ((), (), s32[]{:S(2)}) async-start(), calls=%async_computation.34 | async-start | bytes 3145728 | tf_op jit(solution)/shard_map/psum | solution.py:367
  4300.3 110.3 %all-reduce.19.cloned.1.call-start = ((), (), s32[]{:S(2)}) async-start(), calls=%async_computation.33 | async-start | bytes 3145728 | tf_op jit(solution)/shard_map/psum | solution.py:367
  4367.4 107.1 %all-reduce.17.cloned.1.call-start = ((), (), s32[]{:S(2)}) async-start(), calls=%async_computation.32 | async-start | bytes 3145728 | tf_op jit(solution)/shard_map/psum | solution.py:367
  4431.3 106.4 %all-reduce.15.cloned.1.call-start = ((), (), s32[]{:S(2)}) async-start(), calls=%async_computation.31 | async-start | bytes 3145728 | tf_op jit(solution)/shard_map/psum | solution.py:367
  4494.5 106.5 %all-reduce.13.cloned.1.call-start = ((), (), s32[]{:S(2)}) async-start(), calls=%async_computation.30 | async-start | bytes 3145728 | tf_op jit(solution)/shard_map/psum | solution.py:367
  4557.8 174.4 %reduce-scatter.38.cloned.1.call-start = ((), (), s32[]{:S(2)}) async-start(), calls=%async_computation.27 | async-start | bytes 516096 | tf_op jit(solution)/shard_map/reduce_scatter | solution.py:355
  4597.9 151.4 %all-gather.9.cloned.1.call-start = ((), (), s32[]{:S(2)}) async-start(), calls=%async_computation.23 | async-start | bytes 5242880 | tf_op jit(solution)/shard_map/all_gather | solution.py:382
  4610.3 152.5 %all-gather.11.cloned.1.call-start = ((), (), s32[]{:S(2)}) async-start(), calls=%async_computation.26 | async-start | bytes 10485760 | tf_op jit(solution)/shard_map/all_gather | solution.py:383
  (204 other events, 7009.7 us)
Sparse Core Ops, SparseCore 0:
  9.6 643.3 all-gather.4
  654.5 1266.5 all-gather.6
  1923.7 126.0 reduce-scatter.25
  2052.4 126.0 reduce-scatter.17
  2180.9 126.1 reduce-scatter.21
  2309.7 126.0 reduce-scatter.29
  2438.4 452.3 reduce-scatter.41
  2893.6 452.3 reduce-scatter.39
  3349.7 88.4 reduce-scatter.27
  3442.1 88.2 reduce-scatter.19
  3534.0 88.1 reduce-scatter.23
  3626.2 88.2 reduce-scatter.31
  3718.2 282.5 reduce-scatter.35
  4004.9 281.7 reduce-scatter.33
  4300.4 41.8 all-reduce.20
  4367.5 43.0 all-reduce.18
  4431.4 43.0 all-reduce.16
  4494.6 43.0 all-reduce.14
  4557.9 43.0 all-reduce.12
  4604.1 60.1 reduce-scatter.37
  4666.0 35.7 all-gather.8
  4703.4 59.3 all-gather.10
where the time goes:
time: 4790 us; the launch traced here: 4780 us
  waiting for transfers between devices  3800 us (79%)
  matrix products  627 us (13%)
  blocking collectives  122 us (3%)
  local copies, waits for them, and re-layouts  114 us (2%)
  other arithmetic  94.8 us (2%)
    all_gather x1, waiting for transfers between devices, body(): lax.all_gather(mlp_weight, 'fsdp', axis=1, tiled=True)  1150 us
    unnamed x24, waiting for transfers between devices  893 us
    all_gather x1, waiting for transfers between devices, body(): lax.all_gather(attn_weight, 'fsdp', axis=1, tiled=True)  542 us
    reduce_scatter x4, waiting for transfers between devices, body(): lax.psum_scatter(col_term(lefts[member], rights[member]), 'dp', scatter_d...  393 us
    reduce_scatter x1, waiting for transfers between devices, body(): lax.psum_scatter(col_parts[4], 'fsdp', scatter_dimension=1, tiled=True)  286 us
    dot_general x9, matrix products, body(): jnp.einsum('sd,ksd->sk', history[source].astype(jnp.float32), stream_stac...  225 us
    reduce_scatter x1, waiting for transfers between devices, body(): lax.psum_scatter(col_parts[5], 'fsdp', scatter_dimension=1, tiled=True)  148 us
    dot_general x7, matrix products, product_tn(): lax.dot_general(left_side, right_side, (((0,), (0,)), ((), ())), preferre...  96.3 us
  transfers between devices with their start and end apart: 22, of which 20 were waited for; matrix products, arithmetic and copies ran while one was open for 15% of the time, Pallas kernels for 0%

commit v1 on v0

v1 whole, which is shorter than its diff:
```python
import math

import jax
import jax.numpy as jnp
from jax import lax
from jax.sharding import PartitionSpec as P

HEADS = 16
HEAD = 128
FF = 8192
ROT = 32
MIXW = 36
DOCS = 3
NDOM = 22
STEP = 6


NS_A = 3.4445
NS_B = -4.775
NS_C = 2.0315
ROPE_BASE = 10000.0
LR_MUON = 0.1
LR_ADAM = 0.03
DECAY = 0.01
MOMENTUM = 0.95
BETA_ONE = 0.9
BETA_TWO = 0.95
HIGHEST = lax.Precision.HIGHEST


def exact_gelu(values):
    return jax.nn.gelu(values, approximate=False)


def rope_tables(tok_count):
    half_rot = ROT // 2
    inverse_freq = ROPE_BASE ** (-(2.0 * jnp.arange(half_rot, dtype=jnp.float32)) / ROT)
    angles = jnp.arange(tok_count, dtype=jnp.float32)[:, None] * inverse_freq[None, :]
    return (jnp.cos(angles)[:, None, :], jnp.sin(angles)[:, None, :])


def rotate(values, cosine, sine_tab):
    half_rot = cosine.shape[-1]
    first_half = values[..., :half_rot]
    second_half = values[..., half_rot : 2 * half_rot]
    remain = values[..., 2 * half_rot :]
    return jnp.concatenate(
        [
            first_half * cosine - second_half * sine_tab,
            second_half * cosine + first_half * sine_tab,
            remain,
        ],
        -1,
    )


def layer_norm(values, gain_row, shift_row):
    centred = values - jnp.mean(values, -1, keepdims=True)
    inv_std = lax.rsqrt(jnp.mean(centred * centred, -1, keepdims=True) + 1e-05)
    normed = centred * inv_std
    return (normed * gain_row + shift_row, normed, inv_std)


def norm_back(grad_out, normed, inv_std, gain_row):
    scaled = grad_out * gain_row
    grad_in = inv_std * (
        scaled
        - jnp.mean(scaled, -1, keepdims=True)
        - normed * jnp.mean(scaled * normed, -1, keepdims=True)
    )
    return (grad_in, jnp.sum(grad_out * normed, 0), jnp.sum(grad_out, 0))


def product_nt(left_side, right_side):
    return lax.dot_general(
        left_side, right_side, (((1,), (1,)), ((), ())), preferred_element_type=jnp.float32
    )


def product_tn(left_side, right_side):
    return lax.dot_general(
        left_side, right_side, (((0,), (0,)), ((), ())), preferred_element_type=jnp.float32
    )


def pack_info(lengths, domains, weight_table, tok_count):
    doc_ends = jnp.cumsum(lengths)
    positions = jnp.arange(tok_count, dtype=jnp.int32)
    doc_of = jnp.sum((positions[:, None] >= doc_ends[None, :]).astype(jnp.int32), 1)
    allowed = (doc_of[:, None] == doc_of[None, :]) & (positions[:, None] >= positions[None, :])
    domain = jnp.sum(
        jnp.where(
            doc_of[:, None] == jnp.arange(DOCS, dtype=jnp.int32)[None, :], domains[None, :], 0
        ),
        1,
    )
    weight = jnp.sum(
        jnp.where(
            domain[:, None] == jnp.arange(NDOM, dtype=jnp.int32)[None, :], weight_table[None, :], 0
        ),
        1,
    )
    return (allowed, weight.astype(jnp.float32) / 256.0)


def swap_core(values):
    return lax.ppermute(values, "dp", [(at, at ^ 1) for at in range(4)])


def swap_y(values):
    return lax.ppermute(values, "dp", [(at, at ^ 2) for at in range(4)])


def swap_x(values):
    count = lax.axis_size("fsdp")
    return lax.ppermute(values, "fsdp", [(at, at ^ 1) for at in range(count)])


def shift_z(values, hops):
    count = lax.axis_size("fsdp")
    return lax.ppermute(values, "fsdp", [(at, (at + 2 * hops) % count) for at in range(count)])


def gather_rows(shard):
    depth = lax.axis_size("fsdp") // 2
    z_at = lax.axis_index("fsdp") // 2
    x_at = lax.axis_index("fsdp") % 2
    ring = [shard] + [shift_z(shard, hops) for hops in range(1, depth)]
    whole = jnp.zeros((depth, 2) + shard.shape, shard.dtype)
    rest = (0,) * shard.ndim
    for hops in range(depth):
        owner = (z_at + depth - hops) % depth
        whole = lax.dynamic_update_slice(whole, ring[hops][None, None], (owner, x_at) + rest)
        other = swap_x(ring[hops])
        whole = lax.dynamic_update_slice(whole, other[None, None], (owner, 1 - x_at) + rest)
    return whole.reshape((2 * depth,) + shard.shape)


def scatter_rows(whole, link_type):
    count = lax.axis_size("fsdp")
    depth = count // 2
    z_at = lax.axis_index("fsdp") // 2
    x_at = lax.axis_index("fsdp") % 2
    paired = whole.reshape((depth, 2) + whole.shape[1:])

    def half(which):
        return lax.dynamic_index_in_dim(paired, which, 1, keepdims=False)

    arrived = swap_x(half(1 - x_at).astype(link_type))
    summed = half(x_at).astype(jnp.float32) + arrived.astype(jnp.float32)
    total = lax.dynamic_index_in_dim(summed, z_at, 0, keepdims=False)
    low_sum = summed.astype(link_type)
    for hops in range(1, depth):
        outgoing = lax.dynamic_index_in_dim(low_sum, (z_at + hops) % depth, 0, keepdims=False)
        total = total + shift_z(outgoing, hops).astype(jnp.float32)
    return total


def gather_group(values):
    across = swap_y(values)
    return [values, swap_core(values), across, swap_core(across)]


def scatter_group(parts):
    first = parts[0] + swap_core(parts[1].astype(jnp.bfloat16)).astype(jnp.float32)
    second = parts[2] + swap_core(parts[3].astype(jnp.bfloat16)).astype(jnp.float32)
    return first + swap_y(second.astype(jnp.bfloat16)).astype(jnp.float32)


def flip(values, step):
    blocks = values.reshape((4, values.shape[0] // 4) + values.shape[1:])
    return jnp.stack([blocks[at ^ step] for at in range(4)]).reshape(values.shape)


def gather_columns(values):
    across = flip(swap_y(values), 2)
    return [values, flip(swap_core(values), 1), across, flip(swap_core(across), 1)]


def scatter_columns(parts):
    first = parts[0] + swap_core(flip(parts[1].astype(jnp.bfloat16), 1)).astype(jnp.float32)
    second = parts[2] + swap_core(flip(parts[3].astype(jnp.bfloat16), 1)).astype(jnp.float32)
    return first + swap_y(flip(second.astype(jnp.bfloat16), 2)).astype(jnp.float32)


def sum_group(values):
    values = values + swap_core(values)
    return values + swap_y(values)


def sum_all(values):
    values = sum_group(values)
    count = lax.axis_size("fsdp")
    step = 1
    while step < count:
        values = values + lax.ppermute(
            values, "fsdp", [(at, at ^ step) for at in range(count)]
        )
        step *= 2
    return values


def by_member(parts, member):
    odd_core = member % 2 == 1
    high_y = member >= 2
    near = [jnp.where(odd_core, parts[1], parts[0]), jnp.where(odd_core, parts[0], parts[1])]
    far = [jnp.where(odd_core, parts[3], parts[2]), jnp.where(odd_core, parts[2], parts[3])]
    low_pair = [jnp.where(high_y, b, a) for a, b in zip(near, far)]
    high_pair = [jnp.where(high_y, a, b) for a, b in zip(near, far)]
    return low_pair + high_pair


def high_dot(equation, left_side, right_side):
    return jnp.einsum(
        equation, left_side, right_side, precision=HIGHEST, preferred_element_type=jnp.float32
    )


def orthogonal(moments):
    gram = jnp.concatenate([high_dot("mik,mjk->mij", part, part) for part in moments], 0)
    gram = sum_group(gram)
    norm = jnp.sqrt(jnp.trace(gram, axis1=1, axis2=2)) + 1e-07
    gram = gram / (norm * norm)[:, None, None]
    eye = jnp.eye(gram.shape[-1], dtype=jnp.float32)[None]
    chain = None
    for turn in range(5):
        square = high_dot("mij,mjk->mik", gram, gram)
        factor = NS_A * eye + NS_B * gram + NS_C * square
        chain = factor if chain is None else high_dot("mij,mjk->mik", factor, chain)
        if turn < 4:
            gram = high_dot("mij,mjk->mik", high_dot("mij,mjk->mik", factor, gram), factor)
    chain = chain / norm[:, None, None]
    results = []
    start = 0
    for part in moments:
        count = part.shape[0]
        results.append(high_dot("mij,mjk->mik", chain[start : start + count], part))
        start += count
    return results


def adamw(current, grad_in, moment_one, moment_two):
    one_new = BETA_ONE * moment_one + (1.0 - BETA_ONE) * grad_in
    two_new = BETA_TWO * moment_two + (1.0 - BETA_TWO) * grad_in * grad_in
    one_hat = one_new / (1.0 - BETA_ONE**STEP)
    two_hat = two_new / (1.0 - BETA_TWO**STEP)
    updated = current * (1.0 - LR_ADAM * DECAY) - LR_ADAM * one_hat / (jnp.sqrt(two_hat) + 1e-08)
    return (one_new, two_new, updated)


def columns_of(values, member, width, axis):
    return lax.dynamic_slice_in_dim(values, member * width, width, axis)


def body(
    history,
    out_grad,
    doc_lengths,
    doc_domain,
    domain_weight,
    attn_weight,
    attn_master,
    attn_moment,
    mlp_weight,
    mlp_master,
    mlp_moment,
    params,
    params_m,
    params_v,
    mix_out,
    mix_out_m,
    mix_out_v,
):
    hist_count, tok_count, model_width = history.shape
    members = lax.axis_size("fsdp")
    rows = attn_weight.shape[1]
    group = lax.axis_size("dp")
    member = lax.axis_index("dp")
    attn_cols = attn_weight.shape[2] // group
    mlp_cols = mlp_weight.shape[2] // group
    heads = HEADS // group
    group_tok = group * tok_count
    head_scale = 1.0 / math.sqrt(HEAD)

    param_pieces = gather_rows(params.astype(jnp.bfloat16))
    param_vals_low = jnp.moveaxis(param_pieces, 0, 1).reshape(params.shape[0], model_width)
    param_vals = param_vals_low.astype(jnp.float32)
    mix_weight = param_vals_low[17:]
    full_up = gather_rows(columns_of(mlp_weight[0], member, mlp_cols, 1)).reshape(
        model_width, mlp_cols
    )
    full_down = gather_rows(columns_of(mlp_weight[1], member, mlp_cols, 1)).reshape(
        model_width, mlp_cols
    )
    full_attn = gather_rows(columns_of(attn_weight, member, attn_cols, 2))
    full_attn = jnp.moveaxis(full_attn, 0, 1).reshape(4, model_width, attn_cols)

    mixing = lax.optimization_barrier(mix_out.astype(jnp.bfloat16)).astype(jnp.float32)
    _, tok_weight = pack_info(doc_lengths[0], doc_domain[0], domain_weight, tok_count)
    group_lengths = gather_group(doc_lengths)
    allowed = jnp.stack(
        [
            pack_info(lengths[0], doc_domain[0], domain_weight, tok_count)[0]
            for lengths in group_lengths
        ]
    )
    out_cot = out_grad.astype(jnp.float32) * tok_weight[:, None]
    cot_low = out_cot.astype(jnp.bfloat16)
    group_cot = jnp.concatenate(gather_group(cot_low), 0)

    last_hist = history[hist_count - 1].astype(jnp.float32)
    inv_rms = lax.rsqrt(jnp.mean(last_hist * last_hist, -1, keepdims=True) + 1e-06)
    unit_rms = last_hist * inv_rms
    unit_low = unit_rms.astype(jnp.bfloat16)
    inner_pre = product_nt(unit_low, mix_weight)
    hidden, gelu_inner = jax.vjp(exact_gelu, inner_pre)
    coeffs = (
        jnp.dot(hidden, mixing[:MIXW], precision=HIGHEST, preferred_element_type=jnp.float32)
        + mixing[MIXW]
    ).reshape(tok_count, 4, hist_count)
    streams = []
    for index in range(4):
        running = coeffs[:, index, 0, None] * history[0].astype(jnp.float32)
        for source in range(1, hist_count):
            running = running + coeffs[:, index, source, None] * history[source].astype(
                jnp.float32
            )
        streams.append(running)
    norm_keep = []
    group_normed = []
    for index in (3, 0, 1, 2):
        result, normed, inv_std = layer_norm(
            streams[index], param_vals[index], param_vals[4 + index]
        )
        group_normed.append(
            jnp.concatenate(gather_group(result.astype(jnp.bfloat16)), 0)
        )
        norm_keep.append((normed, inv_std))
    group_normed = group_normed[1:] + group_normed[:1]
    norm_keep = norm_keep[1:] + norm_keep[:1]

    up_bias = lax.dynamic_index_in_dim(param_vals, 13 + member, 0)
    up_pre = jnp.dot(group_normed[3], full_up, preferred_element_type=jnp.float32) + up_bias
    act_val, gelu_up = jax.vjp(exact_gelu, up_pre)
    act_low = act_val.astype(jnp.bfloat16)
    act_grad = jnp.dot(group_cot, full_down, preferred_element_type=jnp.float32)
    up_grad = gelu_up(act_grad)[0].astype(jnp.bfloat16)
    down_weight_grad = scatter_rows(
        product_tn(group_cot, act_low).astype(jnp.bfloat16).reshape(members, rows, mlp_cols),
        jnp.bfloat16,
    )
    up_weight_grad = scatter_rows(
        product_tn(group_normed[3], up_grad)
        .astype(jnp.bfloat16)
        .reshape(members, rows, mlp_cols),
        jnp.bfloat16,
    )
    mlp_in_grad = product_nt(up_grad, full_up)
    mlp_part = product_nt(act_low, full_down)

    def scatter_tokens(part):
        return scatter_group(
            [part[at * tok_count : (at + 1) * tok_count] for at in range(group)]
        )

    in_grads = [None, None, None, scatter_tokens(mlp_in_grad)]

    cosine, sine_tab = rope_tables(tok_count)

    def split_heads(values):
        return values.reshape(group, tok_count, heads, HEAD)

    def bias_piece(row):
        return lax.dynamic_slice(param_vals, (row, member * attn_cols), (1, attn_cols))

    q_pre = jnp.dot(group_normed[0], full_attn[0], preferred_element_type=jnp.float32) + bias_piece(8)
    k_pre = jnp.dot(group_normed[1], full_attn[1], preferred_element_type=jnp.float32) + bias_piece(9)
    value_low = split_heads(
        (
            jnp.dot(group_normed[2], full_attn[2], preferred_element_type=jnp.float32)
            + bias_piece(10)
        ).astype(jnp.bfloat16)
    )
    query_low = rotate(split_heads(q_pre), cosine, sine_tab).astype(jnp.bfloat16)
    key_low = rotate(split_heads(k_pre), cosine, sine_tab).astype(jnp.bfloat16)

    def pair(left_side, right_side):
        return jnp.einsum(
            "bqhd,bkhd->bhqk", left_side, right_side, preferred_element_type=jnp.float32
        )

    def take(weights, right_side):
        return jnp.einsum(
            "bhqk,bkhd->bqhd", weights, right_side, preferred_element_type=jnp.float32
        )

    def give(weights, right_side):
        return jnp.einsum(
            "bhqk,bqhd->bkhd", weights, right_side, preferred_element_type=jnp.float32
        )

    scores = jnp.where(allowed[:, None], pair(query_low, key_low) * head_scale, -1000000000.0)
    top_score = jnp.max(scores, -1, keepdims=True)
    log_total = top_score + jnp.log(jnp.sum(jnp.exp(scores - top_score), -1, keepdims=True))
    probs = jnp.exp(scores - log_total)
    probs_low = probs.astype(jnp.bfloat16)
    context_low = (
        take(probs_low, value_low).reshape(group_tok, attn_cols).astype(jnp.bfloat16)
    )
    group_context = jnp.concatenate(by_member(gather_columns(context_low), member), 1)
    attn_out = jnp.dot(group_context, full_attn[3], preferred_element_type=jnp.float32)
    out_part = lax.dynamic_update_slice(
        mlp_part,
        columns_of(mlp_part, member, attn_cols, 1) + attn_out,
        (0, member * attn_cols),
    )
    layer_out = (
        streams[3] + scatter_tokens(out_part) + (param_vals[11] + param_vals[12])
    ).astype(jnp.bfloat16)

    cot_cols = columns_of(group_cot, member, attn_cols, 1)
    context_grad_part = product_nt(cot_cols, full_attn[3])
    context_grad = split_heads(
        scatter_columns(
            [columns_of(context_grad_part, member ^ at, attn_cols, 1) for at in range(group)]
        ).astype(jnp.bfloat16)
    )
    prob_grad = pair(context_grad, value_low)
    score_grad = (
        probs * (prob_grad - jnp.sum(probs * prob_grad, -1, keepdims=True))
    ).astype(jnp.bfloat16)
    value_grad = give(probs_low, context_grad).reshape(group_tok, attn_cols).astype(jnp.bfloat16)
    query_grad = take(score_grad, key_low) * head_scale
    key_grad = give(score_grad, query_low) * head_scale
    query_back = (
        rotate(query_grad, cosine, -sine_tab).reshape(group_tok, attn_cols).astype(jnp.bfloat16)
    )
    key_back = (
        rotate(key_grad, cosine, -sine_tab).reshape(group_tok, attn_cols).astype(jnp.bfloat16)
    )
    proj_grads = (query_back, key_back, value_grad)
    for index in range(3):
        in_grads[index] = scatter_tokens(product_nt(proj_grads[index], full_attn[index]))
    lefts = (group_normed[0], group_normed[1], group_normed[2], group_context)
    rights = (query_back, key_back, value_grad, cot_cols)
    attn_grads = [
        scatter_rows(
            product_tn(left_side, right_side)
            .astype(jnp.bfloat16)
            .reshape(members, rows, attn_cols),
            jnp.bfloat16,
        )
        for left_side, right_side in zip(lefts, rights)
    ]

    stream_grads = []
    gain_list = []
    shift_list = []
    for index in range(4):
        grad_stream, gain_part, shift_part = norm_back(
            in_grads[index], norm_keep[index][0], norm_keep[index][1], param_vals[index]
        )
        stream_grads.append(grad_stream)
        gain_list.append(gain_part)
        shift_list.append(shift_part)
    stream_grads[3] = stream_grads[3] + out_cot
    coef_grad = jnp.stack(
        [
            jnp.stack(
                [
                    jnp.sum(history[source].astype(jnp.float32) * stream_grads[index], -1)
                    for source in range(hist_count)
                ],
                -1,
            )
            for index in range(4)
        ],
        1,
    )
    coef_flat = coef_grad.reshape(tok_count, 4 * hist_count)
    mixing_grad = jnp.concatenate(
        [
            jnp.dot(hidden.T, coef_flat, precision=HIGHEST, preferred_element_type=jnp.float32),
            jnp.sum(coef_flat, 0)[None],
        ],
        0,
    )
    hidden_grad = jnp.dot(
        coef_flat, mixing[:MIXW].T, precision=HIGHEST, preferred_element_type=jnp.float32
    )
    inner_grad = gelu_inner(hidden_grad)[0].astype(jnp.bfloat16)
    mix_weight_grad = product_tn(inner_grad, unit_low)
    unit_grad = jnp.dot(inner_grad, mix_weight, preferred_element_type=jnp.float32)
    last_grad = inv_rms * (unit_grad - unit_rms * jnp.mean(unit_grad * unit_rms, -1, keepdims=True))
    hist_parts = []
    for source in range(hist_count):
        running = coeffs[:, 0, source, None] * stream_grads[0]
        for index in range(1, 4):
            running = running + coeffs[:, index, source, None] * stream_grads[index]
        if source == hist_count - 1:
            running = running + last_grad
        hist_parts.append(running.astype(jnp.bfloat16))
    history_grad = jnp.stack(hist_parts)
    out_bias_grad = jnp.sum(cot_low.astype(jnp.float32), 0)

    def placed(values, width, at, total):
        return lax.dynamic_update_slice(
            jnp.zeros((total,), jnp.float32),
            jnp.sum(values.astype(jnp.float32), 0),
            (at * width,),
        )

    param_grad = jnp.concatenate(
        [
            jnp.stack(gain_list),
            jnp.stack(shift_list),
            jnp.stack([placed(part, attn_cols, member, model_width) for part in proj_grads]),
            out_bias_grad[None],
            out_bias_grad[None],
            placed(up_grad, mlp_cols, member, group * mlp_cols).reshape(-1, model_width),
            mix_weight_grad,
        ],
        0,
    )
    param_pieces_grad = jnp.moveaxis(
        param_grad.reshape(params.shape[0], members, rows), 1, 0
    )
    param_part = sum_group(scatter_rows(param_pieces_grad, jnp.float32))
    mixing_grad = sum_all(mixing_grad)

    mlp_grad = jnp.stack([up_weight_grad, down_weight_grad])
    attn_grad = jnp.stack(attn_grads)
    mlp_mom = MOMENTUM * mlp_moment + mlp_grad
    (mlp_cur,) = orthogonal([mlp_mom])
    mlp_new = mlp_master * (1.0 - LR_MUON * DECAY) - LR_MUON * 0.2 * math.sqrt(FF) * mlp_cur
    mlp_copy = jnp.concatenate(
        by_member(gather_group(mlp_new.astype(jnp.bfloat16)), member), 2
    )
    attn_mom = MOMENTUM * attn_moment + attn_grad
    (attn_cur,) = orthogonal([attn_mom])
    attn_new = (
        attn_master * (1.0 - LR_MUON * DECAY) - LR_MUON * 0.2 * math.sqrt(model_width) * attn_cur
    )
    attn_copy = jnp.concatenate(
        by_member(gather_group(attn_new.astype(jnp.bfloat16)), member), 2
    )
    params_m_new, params_v_new, params_new = adamw(params, param_part, params_m, params_v)
    mix_out_m_new, mix_out_v_new, mix_out_new = adamw(mix_out, mixing_grad, mix_out_m, mix_out_v)
    return (
        layer_out,
        history_grad,
        attn_grad,
        attn_mom,
        attn_new,
        attn_copy,
        mlp_grad,
        mlp_mom,
        mlp_new,
        mlp_copy,
        param_part,
        param_part[11:13],
        params_m_new,
        params_v_new,
        params_new,
        mixing_grad,
        mix_out_m_new,
        mix_out_v_new,
        mix_out_new,
    )


def solution(mesh):
    in_specs = (
        P(None, ("dp", "fsdp"), None),
        P(("dp", "fsdp"), None),
        P(("dp", "fsdp"), None),
        P(("dp", "fsdp"), None),
        P(),
        P(None, "fsdp", None),
        P(None, "fsdp", "dp"),
        P(None, "fsdp", "dp"),
        P(None, "fsdp", None),
        P(None, "fsdp", "dp"),
        P(None, "fsdp", "dp"),
        P(None, "fsdp"),
        P(None, "fsdp"),
        P(None, "fsdp"),
        P(),
        P(),
        P(),
    )
    out_specs = (
        P(("dp", "fsdp"), None),
        P(None, ("dp", "fsdp"), None),
        P(None, "fsdp", "dp"),
        P(None, "fsdp", "dp"),
        P(None, "fsdp", "dp"),
        P(None, "fsdp", None),
        P(None, "fsdp", "dp"),
        P(None, "fsdp", "dp"),
        P(None, "fsdp", "dp"),
        P(None, "fsdp", None),
        P(None, "fsdp"),
        P(None, "fsdp"),
        P(None, "fsdp"),
        P(None, "fsdp"),
        P(None, "fsdp"),
        P(),
        P(),
        P(),
        P(),
    )
    return jax.shard_map(body, mesh=mesh, in_specs=in_specs, out_specs=out_specs, check_vma=False)
```

time: 4790 us -> 1310 us (0.27)
  waiting for transfers between devices: 3800 us -> 618 us
  matrix products: 627 us -> 237 us
  starting transfers between devices: 0.89 us -> 136 us
  blocking collectives: 122 us -> 0 us
  other arithmetic: 94.8 us -> 161 us
    all_gather x4 -> x0, waiting for transfers between devices: 1700 us -> none  [the longest x1 1150 us: body(): lax.all_gather(mlp_weight, 'fsdp', axis=1, tiled=True)]
    reduce_scatter x11 -> x0, waiting for transfers between devices: 1140 us -> none  [the longest x4 393 us: body(): lax.psum_scatter(col_term(lefts[member], rights[member]), 'dp', scatter_d...]
    unnamed x24 -> x0, waiting for transfers between devices: 893 us -> none
    ppermute x0 -> x112, waiting for transfers between devices: none -> 618 us  [the longest x33 262 us: shift_z(): lax.ppermute(values, 'fsdp', [(at, (at + 2 * hops) % count) for at in ran...]
    dot_general x51 -> x50, matrix products: 442 us -> 148 us  [the longest x38 48.4 us: high_dot(): jnp.einsum(equation, left_side, right_side, precision=HIGHEST, preferred_...]
    ppermute x0 -> x112, starting transfers between devices: none -> 136 us  [the longest x34 52.2 us: swap_core(): return lax.ppermute(values, 'dp', [(at, at ^ 1) for at in range(4)])]
    psum x5 -> x0, waiting for transfers between devices: 68.7 us -> none  [body(): attn_gram, mlp_gram = lax.psum((gram_of(attn_cur), gram_of(mlp_cur)), 'dp')]
    all_gather x1 -> x0, blocking collectives: 68.2 us -> none  [body(): lax.all_gather(params.astype(jnp.bfloat16), 'fsdp', axis=1, tiled=True)]
  transfers between devices with their start and end apart: 22 -> 112, of which waited for: 20 -> 36; matrix products, arithmetic and copies ran while one was open for 15% -> 40% of each run, Pallas kernels for 0% -> 0%
where the time goes in v1:
time: 1310 us; the launch traced here: 1300 us
  waiting for transfers between devices  618 us (47%)
  matrix products  237 us (18%)
  other arithmetic  161 us (12%)
  local copies, waits for them, and re-layouts  141 us (11%)
  starting transfers between devices  136 us (10%)
    ppermute x33, waiting for transfers between devices, shift_z(): lax.ppermute(values, 'fsdp', [(at, (at + 2 * hops) % count) for at in ran...  262 us
    ppermute x23, waiting for transfers between devices, swap_x(): return lax.ppermute(values, 'fsdp', [(at, at ^ 1) for at in range(count)])  243 us
    ppermute x19, waiting for transfers between devices, swap_y(): return lax.ppermute(values, 'dp', [(at, at ^ 2) for at in range(4)])  109 us
    ppermute x34, starting transfers between devices, swap_core(): return lax.ppermute(values, 'dp', [(at, at ^ 1) for at in range(4)])  52.2 us
    ppermute x33, starting transfers between devices, shift_z(): lax.ppermute(values, 'fsdp', [(at, (at + 2 * hops) % count) for at in ran...  51.4 us
    dot_general x38, matrix products, high_dot(): jnp.einsum(equation, left_side, right_side, precision=HIGHEST, preferred_...  48.4 us
    dot_general x7, matrix products, product_nt(): lax.dot_general(left_side, right_side, (((1,), (1,)), ((), ())), preferre...  46 us
    dot_general x7, matrix products, product_tn(): lax.dot_general(left_side, right_side, (((0,), (0,)), ((), ())), preferre...  42.4 us
  transfers between devices with their start and end apart: 112, of which 36 were waited for; matrix products, arithmetic and copies ran while one was open for 40% of the time, Pallas kernels for 0%

profile of v1, /device:TPU:1, one launch (start us, length us, event | category | flops | bytes accessed | tf_op | source)
XLA Modules:
  0.0 1298.9 jit_solution(6657916764162097264)
XLA Ops:
  54.4 23.6 %collective-permute-done.2 = bf16[53,256]{1,0:T(8,128)(2,1)S(1)} collective-permute-done((bf16[53,256]{1,0:T(8,128)(2,1)S(1)}, bf16[53,256]{1,0:T(8,128)(2,1)S(1)}, u32[]{:S(2)}, u32[]{:S(2)}) %collective-permute-start.2) | collective-permute-done | bytes 27168 | tf_op jit(solution)/shard_map/ppermute | solution.py:116
  81.6 21.7 %collective-permute-done.6 = bf16[53,256]{1,0:T(8,128)(2,1)S(1)} collective-permute-done((bf16[53,256]{1,0:T(8,128)(2,1)S(1)}, bf16[53,256]{1,0:T(8,128)(2,1)S(1)}, u32[]{:S(2)}, u32[]{:S(2)}) %collective-permute-start.6) | collective-permute-done | bytes 27168 | tf_op jit(solution)/shard_map/ppermute | solution.py:116
  146.4 78.7 %collective-permute-done.13 = bf16[256,2048]{1,0:T(8,128)(2,1)S(1)} collective-permute-done((bf16[256,2048]{1,0:T(8,128)(2,1)}, bf16[256,2048]{1,0:T(8,128)(2,1)S(1)}, u32[]{:S(2)}, u32[]{:S(2)}) %collective-permute-start.13) | collective-permute-done | bytes 1048608 | tf_op jit(solution)/shard_map/ppermute | solution.py:121
  232.3 38.7 %collective-permute-done.14 = bf16[256,2048]{1,0:T(8,128)(2,1)S(1)} collective-permute-done((bf16[256,2048]{1,0:T(8,128)(2,1)S(1)}, bf16[256,2048]{1,0:T(8,128)(2,1)S(1)}, u32[]{:S(2)}, u32[]{:S(2)}) %collective-permute-start.14) | collective-permute-done | bytes 1048608 | tf_op jit(solution)/shard_map/ppermute | solution.py:116
  272.1 21.4 %collective-permute-done.19 = bf16[256,2048]{1,0:T(8,128)(2,1)S(1)} collective-permute-done((bf16[256,2048]{1,0:T(8,128)(2,1)S(1)}, bf16[256,2048]{1,0:T(8,128)(2,1)S(1)}, u32[]{:S(2)}, u32[]{:S(2)}) %collective-permute-start.19) | collective-permute-done | bytes 1048608 | tf_op jit(solution)/shard_map/ppermute | solution.py:116
  298.2 43.0 %collective-permute-done.20 = bf16[256,2048]{1,0:T(8,128)(2,1)S(1)} collective-permute-done((bf16[256,2048]{1,0:T(8,128)(2,1)}, bf16[256,2048]{1,0:T(8,128)(2,1)S(1)}, u32[]{:S(2)}, u32[]{:S(2)}) %collective-permute-start.20) | collective-permute-done | bytes 1048608 | tf_op jit(solution)/shard_map/ppermute | solution.py:121
  349.4 18.6 %collective-permute-done.21 = bf16[256,2048]{1,0:T(8,128)(2,1)S(1)} collective-permute-done((bf16[256,2048]{1,0:T(8,128)(2,1)S(1)}, bf16[256,2048]{1,0:T(8,128)(2,1)S(1)}, u32[]{:S(2)}, u32[]{:S(2)}) %collective-permute-start.21) | collective-permute-done | bytes 1048608 | tf_op jit(solution)/shard_map/ppermute | solution.py:116
  370.8 19.7 %collective-permute-done.33 = bf16[4,256,512]{2,1,0:T(8,128)(2,1)S(1)} collective-permute-done((bf16[4,256,512]{2,1,0:T(8,128)(2,1)S(1)}, bf16[4,256,512]{2,1,0:T(8,128)(2,1)S(1)}, u32[]{:S(2)}, u32[]{:S(2)}) %collective-permute-start.33) | collective-permute-done | bytes 1048608 | tf_op jit(solution)/shard_map/ppermute | solution.py:116
  404.9 12.2 collective-permute-done.16
  425.5 14.2 %collective-permute-done.23 = bf16[256,2048]{1,0:T(8,128)(2,1)S(1)} collective-permute-done((bf16[256,2048]{1,0:T(8,128)(2,1)S(1)}, bf16[256,2048]{1,0:T(8,128)(2,1)S(1)}, u32[]{:S(2)}, u32[]{:S(2)}) %collective-permute-start.23) | collective-permute-done | bytes 1048608 | tf_op jit(solution)/shard_map/ppermute | solution.py:116
  470.0 35.0 %multiply_convert_fusion = (bf16[1024,2048]{1,0:T(8,128)(2,1)S(1)}, f32[1024,2048]{1,0:T(8,128)}, f32[1024,2048]{1,0:T(8,128)}) fusion(f32[2048]{0:T(1024)S(1)} %bitcast.975, bf16[2048,2048]{1,0:T(8,128)(2,1)} %bitcast.38, bf16[256,2048]{1,0:T(8,128)(2,1)} %collective-permute-done.9, bf16[256,2048]{1,0:T(8,128)(2,1)} %collective-permute-done.8, ...), kind=kOutput, calls=%fused_computation.7 | convolution fusion | flops 8745123840 | bytes 33562624 | tf_op jit(solution)/shard_map/dot_general | solution.py:343
  505.1 14.8 %fusion.272 = f32[1024,2048]{1,0:T(8,128)} fusion(bf16[1024,2048]{1,0:T(8,128)(2,1)S(1)} %get-tuple-element.121, bf16[2048,2048]{1,0:T(8,128)(2,1)} %bitcast.49), kind=kOutput, calls=%fused_computation.663 | convolution fusion | flops 8589934592 | bytes 20971520 | tf_op jit(solution)/shard_map/dot_general | solution.py:75
  519.9 21.2 %convert_reduce_fusion = (f32[2048]{0:T(1024)S(1)}, bf16[1024,2048]{1,0:T(8,128)(2,1)}) fusion(f32[1024,2048]{1,0:T(8,128)} %get-tuple-element.122, bf16[2048,2048]{1,0:T(8,128)(2,1)} %bitcast.49, bf16[256,2048]{1,0:T(8,128)(2,1)} %copy-done.79, bf16[256,2048]{1,0:T(8,128)(2,1)S(1)} %copy-done.74, bf16[256,2048]{1,0:T(8,128)(2,1)S(1)} %copy-done.77, ...), kind=kOutput, calls=%fused_computation.5 | convolution fusion | flops 8642361344 | bytes 33570816 | tf_op jit(solution)/shard_map/dot_general | solution.py:346
  541.0 12.4 convolution_convert_fusion.1
  571.8 17.4 %collective-permute-done.54 = bf16[1024,512]{1,0:T(8,128)(2,1)S(1)} collective-permute-done((bf16[1024,512]{1,0:T(8,128)(2,1)S(1)}, bf16[1024,512]{1,0:T(8,128)(2,1)S(1)}, u32[]{:S(2)}, u32[]{:S(2)}) %collective-permute-start.54) | collective-permute-done | bytes 1048608 | tf_op jit(solution)/shard_map/ppermute | solution.py:111
  632.4 14.6 %fusion.266 = (bf16[1024,2048]{1,0:T(8,128)(2,1)}, f32[1024,2048]{1,0:T(8,128)}) fusion(bf16[1024,2048]{1,0:T(8,128)(2,1)S(1)} %copy-done.197, bf16[2048,2048]{1,0:T(8,128)(2,1)} %bitcast.38), kind=kOutput, calls=%fused_computation.657 | convolution fusion | flops 8592031744 | bytes 25165824 | tf_op jit(solution)/shard_map/dot_general | solution.py:75
  678.4 61.8 %collective-permute-done.92 = bf16[4,256,2048]{2,1,0:T(8,128)(2,1)} collective-permute-done((bf16[4,256,2048]{2,1,0:T(8,128)(2,1)}, bf16[4,256,2048]{2,1,0:T(8,128)(2,1)}, u32[]{:S(2)}, u32[]{:S(2)}) %collective-permute-start.92) | collective-permute-done | bytes 4194336 | tf_op jit(solution)/shard_map/ppermute | solution.py:116
  751.4 38.0 %collective-permute-done.90 = bf16[256,2048]{1,0:T(8,128)(2,1)} collective-permute-done((bf16[256,2048]{1,0:T(8,128)(2,1)}, bf16[256,2048]{1,0:T(8,128)(2,1)}, u32[]{:S(2)}, u32[]{:S(2)}) %collective-permute-start.90) | collective-permute-done | bytes 1048608 | tf_op jit(solution)/shard_map/ppermute | solution.py:121
  796.5 16.6 %collective-permute-done.95 = bf16[256,2048]{1,0:T(8,128)(2,1)S(1)} collective-permute-done((bf16[256,2048]{1,0:T(8,128)(2,1)S(1)}, bf16[256,2048]{1,0:T(8,128)(2,1)S(1)}, u32[]{:S(2)}, u32[]{:S(2)}) %collective-permute-start.95) | collective-permute-done | bytes 1048608 | tf_op jit(solution)/shard_map/ppermute | solution.py:121
  813.1 43.6 %collective-permute-done.94 = bf16[256,2048]{1,0:T(8,128)(2,1)S(1)} collective-permute-done((bf16[256,2048]{1,0:T(8,128)(2,1)S(1)}, bf16[256,2048]{1,0:T(8,128)(2,1)S(1)}, u32[]{:S(2)}, u32[]{:S(2)}) %collective-permute-start.94) | collective-permute-done | bytes 1048608 | tf_op jit(solution)/shard_map/ppermute | solution.py:121
  1005.1 12.5 collective-permute-done.69
  1052.4 22.4 %collective-permute-done.60 = bf16[256,2048]{1,0:T(8,128)(2,1)S(1)} collective-permute-done((bf16[256,2048]{1,0:T(8,128)(2,1)}, bf16[256,2048]{1,0:T(8,128)(2,1)S(1)}, u32[]{:S(2)}, u32[]{:S(2)}) %collective-permute-start.60) | collective-permute-done | bytes 1048608 | tf_op jit(solution)/shard_map/ppermute | solution.py:111
  1146.3 18.4 %collective-permute-done.48 = bf16[256,2048]{1,0:T(8,128)(2,1)} collective-permute-done((bf16[256,2048]{1,0:T(8,128)(2,1)}, bf16[256,2048]{1,0:T(8,128)(2,1)}, u32[]{:S(2)}, u32[]{:S(2)}) %collective-permute-start.48) | collective-permute-done | bytes 1048608 | tf_op jit(solution)/shard_map/ppermute | solution.py:111
  1224.7 13.0 collective-permute-done.84
  (955 shorter events, 660.7 us)
Async XLA Ops:
  51.6 92.7 %collective-permute-start.28 = (bf16[4,256,512]{2,1,0:T(8,128)(2,1)}, bf16[4,256,512]{2,1,0:T(8,128)(2,1)}, u32[]{:S(2)}, u32[]{:S(2)}) collective-permute-start(bf16[4,256,512]{2,1,0:T(8,128)(2,1)} %get-tuple-element.120), channel_id=1, source_target_pairs={{0,2},{1,3},{2,4},{3,5},{4,6},{5,7},{6,0},{7,1},{8,10},{9,11},{10,... | collective-permute-start | bytes 3145736 | tf_op jit(solution)/shard_map/ppermute | solution.py:121
  52.7 89.1 %collective-permute-start.27 = (bf16[4,256,512]{2,1,0:T(8,128)(2,1)}, bf16[4,256,512]{2,1,0:T(8,128)(2,1)}, u32[]{:S(2)}, u32[]{:S(2)}) collective-permute-start(bf16[4,256,512]{2,1,0:T(8,128)(2,1)} %get-tuple-element.120), channel_id=1, source_target_pairs={{0,1},{1,0},{2,3},{3,2},{4,5},{5,4},{6,7},{7,6},{8,9},{9,8},{10,11... | collective-permute-start | bytes 3145736 | tf_op jit(solution)/shard_map/ppermute | solution.py:116
  54.2 80.0 %collective-permute-start.11 = (bf16[256,2048]{1,0:T(8,128)(2,1)}, bf16[256,2048]{1,0:T(8,128)(2,1)}, u32[]{:S(2)}, u32[]{:S(2)}) collective-permute-start(bf16[256,2048]{1,0:T(8,128)(2,1)} %dynamic-slice_bitcast_fusion.13), channel_id=1, source_target_pairs={{0,2},{1,3},{2,4},{3,5},{4,6},{5,7},{6,0},{7,1},{8,10},{9,11},{10,... | collective-permute-start | bytes 3145736 | tf_op jit(solution)/shard_map/ppermute | solution.py:121
  131.8 93.2 %collective-permute-start.13 = (bf16[256,2048]{1,0:T(8,128)(2,1)}, bf16[256,2048]{1,0:T(8,128)(2,1)S(1)}, u32[]{:S(2)}, u32[]{:S(2)}) collective-permute-start(bf16[256,2048]{1,0:T(8,128)(2,1)} %dynamic-slice_bitcast_fusion.13), channel_id=1, source_target_pairs={{0,4},{1,5},{2,6},{3,7},{4,0},{5,1},{6,2},{7,3},{8,12},{9,13},{10,... | collective-permute-start | bytes 3145736 | tf_op jit(solution)/shard_map/ppermute | solution.py:121
  134.2 91.3 %collective-permute-start.18 = (bf16[256,2048]{1,0:T(8,128)(2,1)}, bf16[256,2048]{1,0:T(8,128)(2,1)S(1)}, u32[]{:S(2)}, u32[]{:S(2)}) collective-permute-start(bf16[256,2048]{1,0:T(8,128)(2,1)} %dynamic-slice_bitcast_fusion.12), channel_id=1, source_target_pairs={{0,2},{1,3},{2,4},{3,5},{4,6},{5,7},{6,0},{7,1},{8,10},{9,11},{10,... | collective-permute-start | bytes 3145736 | tf_op jit(solution)/shard_map/ppermute | solution.py:121
  139.4 156.2 %collective-permute-start.30 = (bf16[4,256,512]{2,1,0:T(8,128)(2,1)}, bf16[4,256,512]{2,1,0:T(8,128)(2,1)S(1)}, u32[]{:S(2)}, u32[]{:S(2)}) collective-permute-start(bf16[4,256,512]{2,1,0:T(8,128)(2,1)} %get-tuple-element.120), channel_id=1, source_target_pairs={{0,4},{1,5},{2,6},{3,7},{4,0},{5,1},{6,2},{7,3},{8,12},{9,13},{10,... | collective-permute-start | bytes 3145736 | tf_op jit(solution)/shard_map/ppermute | solution.py:121
  141.8 88.1 %collective-permute-start.12 = (bf16[256,2048]{1,0:T(8,128)(2,1)}, bf16[256,2048]{1,0:T(8,128)(2,1)S(1)}, u32[]{:S(2)}, u32[]{:S(2)}) collective-permute-start(bf16[256,2048]{1,0:T(8,128)(2,1)} %collective-permute-done.11), channel_id=1, source_target_pairs={{0,1},{1,0},{2,3},{3,2},{4,5},{5,4},{6,7},{7,6},{8,9},{9,8},{10,11... | collective-permute-start | bytes 3145736 | tf_op jit(solution)/shard_map/ppermute | solution.py:116
  144.3 200.5 %collective-permute-start.32 = (bf16[4,256,512]{2,1,0:T(8,128)(2,1)}, bf16[4,256,512]{2,1,0:T(8,128)(2,1)S(1)}, u32[]{:S(2)}, u32[]{:S(2)}) collective-permute-start(bf16[4,256,512]{2,1,0:T(8,128)(2,1)} %get-tuple-element.120), channel_id=1, source_target_pairs={{0,6},{1,7},{2,0},{3,1},{4,2},{5,3},{6,4},{7,5},{8,14},{9,15},{10,... | collective-permute-start | bytes 3145736 | tf_op jit(solution)/shard_map/ppermute | solution.py:121
  369.3 78.0 %collective-permute-start.37 = (bf16[256,2048]{1,0:T(8,128)(2,1)S(1)}, bf16[256,2048]{1,0:T(8,128)(2,1)S(1)}, u32[]{:S(2)}, u32[]{:S(2)}) collective-permute-start(bf16[256,2048]{1,0:T(8,128)(2,1)S(1)} %add_convert_fusion.14), channel_id=1, source_target_pairs={{0,8},{8,0},{16,24},{24,16},{1,9},{9,1},{17,25},{25,17},{2,10},{10... | collective-permute-start | bytes 3145736 | tf_op jit(solution)/shard_map/ppermute | solution.py:107
  447.4 114.4 %collective-permute-start.53 = (bf16[1024,512]{1,0:T(8,128)(2,1)}, bf16[1024,512]{1,0:T(8,128)(2,1)}, u32[]{:S(2)}, u32[]{:S(2)}) collective-permute-start(bf16[1024,512]{1,0:T(8,128)(2,1)} %bitcast.137), channel_id=1, source_target_pairs={{0,8},{8,0},{16,24},{24,16},{1,9},{9,1},{17,25},{25,17},{2,10},{10... | collective-permute-start | bytes 3145736 | tf_op jit(solution)/shard_map/ppermute | solution.py:107
  458.7 113.0 %collective-permute-start.52 = (bf16[1024,512]{1,0:T(8,128)(2,1)}, bf16[1024,512]{1,0:T(8,128)(2,1)}, u32[]{:S(2)}, u32[]{:S(2)}) collective-permute-start(bf16[1024,512]{1,0:T(8,128)(2,1)} %bitcast.132), channel_id=1, source_target_pairs={{0,8},{8,0},{16,24},{24,16},{1,9},{9,1},{17,25},{25,17},{2,10},{10... | collective-permute-start | bytes 3145736 | tf_op jit(solution)/shard_map/ppermute | solution.py:107
  558.3 106.2 %collective-permute-start.88 = (bf16[4,256,2048]{2,1,0:T(8,128)(2,1)}, bf16[4,256,2048]{2,1,0:T(8,128)(2,1)}, u32[]{:S(2)}, u32[]{:S(2)}) collective-permute-start(bf16[4,256,2048]{2,1,0:T(8,128)(2,1)} %dynamic-slice_bitcast_fusion.1), channel_id=1, source_target_pairs={{0,1},{1,0},{2,3},{3,2},{4,5},{5,4},{6,7},{7,6},{8,9},{9,8},{10,11... | collective-permute-start | bytes 12582920 | tf_op jit(solution)/shard_map/ppermute | solution.py:116
  627.3 112.9 %collective-permute-start.92 = (bf16[4,256,2048]{2,1,0:T(8,128)(2,1)}, bf16[4,256,2048]{2,1,0:T(8,128)(2,1)}, u32[]{:S(2)}, u32[]{:S(2)}) collective-permute-start(bf16[4,256,2048]{2,1,0:T(8,128)(2,1)} %dynamic-slice_bitcast_fusion), channel_id=1, source_target_pairs={{0,1},{1,0},{2,3},{3,2},{4,5},{5,4},{6,7},{7,6},{8,9},{9,8},{10,11... | collective-permute-start | bytes 12582920 | tf_op jit(solution)/shard_map/ppermute | solution.py:116
  664.2 131.7 %collective-permute-start.25 = (bf16[256,2048]{1,0:T(8,128)(2,1)}, bf16[256,2048]{1,0:T(8,128)(2,1)}, u32[]{:S(2)}, u32[]{:S(2)}) collective-permute-start(bf16[256,2048]{1,0:T(8,128)(2,1)} %get-tuple-element.173), channel_id=1, source_target_pairs={{0,16},{8,24},{16,0},{24,8},{1,17},{9,25},{17,1},{25,9},{2,18},{10... | collective-permute-start | bytes 3145736 | tf_op jit(solution)/shard_map/ppermute | solution.py:111
  675.2 74.6 %collective-permute-start.91 = (bf16[256,2048]{1,0:T(8,128)(2,1)}, bf16[256,2048]{1,0:T(8,128)(2,1)}, u32[]{:S(2)}, u32[]{:S(2)}) collective-permute-start(bf16[256,2048]{1,0:T(8,128)(2,1)} %get-tuple-element.146), channel_id=1, source_target_pairs={{0,6},{1,7},{2,0},{3,1},{4,2},{5,3},{6,4},{7,5},{8,14},{9,15},{10,... | collective-permute-start | bytes 3145736 | tf_op jit(solution)/shard_map/ppermute | solution.py:121
  678.4 111.0 %collective-permute-start.90 = (bf16[256,2048]{1,0:T(8,128)(2,1)}, bf16[256,2048]{1,0:T(8,128)(2,1)}, u32[]{:S(2)}, u32[]{:S(2)}) collective-permute-start(bf16[256,2048]{1,0:T(8,128)(2,1)} %get-tuple-element.147), channel_id=1, source_target_pairs={{0,4},{1,5},{2,6},{3,7},{4,0},{5,1},{6,2},{7,3},{8,12},{9,13},{10,... | collective-permute-start | bytes 3145736 | tf_op jit(solution)/shard_map/ppermute | solution.py:121
  749.8 106.9 %collective-permute-start.94 = (bf16[256,2048]{1,0:T(8,128)(2,1)S(1)}, bf16[256,2048]{1,0:T(8,128)(2,1)S(1)}, u32[]{:S(2)}, u32[]{:S(2)}) collective-permute-start(bf16[256,2048]{1,0:T(8,128)(2,1)S(1)} %get-tuple-element.150), channel_id=1, source_target_pairs={{0,4},{1,5},{2,6},{3,7},{4,0},{5,1},{6,2},{7,3},{8,12},{9,13},{10,... | collective-permute-start | bytes 3145736 | tf_op jit(solution)/shard_map/ppermute | solution.py:121
  789.4 79.0 %collective-permute-start.65 = (bf16[256,2048]{1,0:T(8,128)(2,1)}, bf16[256,2048]{1,0:T(8,128)(2,1)}, u32[]{:S(2)}, u32[]{:S(2)}) collective-permute-start(bf16[256,2048]{1,0:T(8,128)(2,1)} %get-tuple-element.162), channel_id=1, source_target_pairs={{0,8},{8,0},{16,24},{24,16},{1,9},{9,1},{17,25},{25,17},{2,10},{10... | collective-permute-start | bytes 3145736 | tf_op jit(solution)/shard_map/ppermute | solution.py:107
  795.9 78.3 %collective-permute-start.24 = (bf16[256,2048]{1,0:T(8,128)(2,1)}, bf16[256,2048]{1,0:T(8,128)(2,1)}, u32[]{:S(2)}, u32[]{:S(2)}) collective-permute-start(bf16[256,2048]{1,0:T(8,128)(2,1)} %get-tuple-element.173), channel_id=1, source_target_pairs={{0,8},{8,0},{16,24},{24,16},{1,9},{9,1},{17,25},{25,17},{2,10},{10... | collective-permute-start | bytes 3145736 | tf_op jit(solution)/shard_map/ppermute | solution.py:107
  796.0 78.2 %collective-permute-start.26 = (bf16[256,2048]{1,0:T(8,128)(2,1)}, bf16[256,2048]{1,0:T(8,128)(2,1)}, u32[]{:S(2)}, u32[]{:S(2)}) collective-permute-start(bf16[256,2048]{1,0:T(8,128)(2,1)} %collective-permute-done.25), channel_id=1, source_target_pairs={{0,8},{8,0},{16,24},{24,16},{1,9},{9,1},{17,25},{25,17},{2,10},{10... | collective-permute-start | bytes 3145736 | tf_op jit(solution)/shard_map/ppermute | solution.py:107
  1017.5 120.8 %collective-permute-start.64 = (bf16[256,2048]{1,0:T(8,128)(2,1)}, bf16[256,2048]{1,0:T(8,128)(2,1)}, u32[]{:S(2)}, u32[]{:S(2)}) collective-permute-start(bf16[256,2048]{1,0:T(8,128)(2,1)} %get-tuple-element.161), channel_id=1, source_target_pairs={{0,8},{8,0},{16,24},{24,16},{1,9},{9,1},{17,25},{25,17},{2,10},{10... | collective-permute-start | bytes 3145736 | tf_op jit(solution)/shard_map/ppermute | solution.py:107
  1039.5 100.8 %collective-permute-start.98 = (bf16[2,256,2048]{2,1,0:T(8,128)(2,1)}, bf16[2,256,2048]{2,1,0:T(8,128)(2,1)}, u32[]{:S(2)}, u32[]{:S(2)}) collective-permute-start(bf16[2,256,2048]{2,1,0:T(8,128)(2,1)} %get-tuple-element.296), channel_id=1, source_target_pairs={{0,16},{8,24},{16,0},{24,8},{1,17},{9,25},{17,1},{25,9},{2,18},{10... | collective-permute-start | bytes 6291464 | tf_op jit(solution)/shard_map/ppermute | solution.py:111
  1138.3 133.2 %collective-permute-start.100 = (bf16[2,256,2048]{2,1,0:T(8,128)(2,1)}, bf16[2,256,2048]{2,1,0:T(8,128)(2,1)}, u32[]{:S(2)}, u32[]{:S(2)}) collective-permute-start(bf16[2,256,2048]{2,1,0:T(8,128)(2,1)} %get-tuple-element.296), channel_id=1, source_target_pairs={{0,8},{8,0},{16,24},{24,16},{1,9},{9,1},{17,25},{25,17},{2,10},{10... | collective-permute-start | bytes 6291464 | tf_op jit(solution)/shard_map/ppermute | solution.py:107
  1140.3 131.3 %collective-permute-start.99 = (bf16[2,256,2048]{2,1,0:T(8,128)(2,1)}, bf16[2,256,2048]{2,1,0:T(8,128)(2,1)}, u32[]{:S(2)}, u32[]{:S(2)}) collective-permute-start(bf16[2,256,2048]{2,1,0:T(8,128)(2,1)} %collective-permute-done.98), channel_id=1, source_target_pairs={{0,8},{8,0},{16,24},{24,16},{1,9},{9,1},{17,25},{25,17},{2,10},{10... | collective-permute-start | bytes 6291464 | tf_op jit(solution)/shard_map/ppermute | solution.py:107
  (302 other events, 6005.0 us)

commit v2 on v1

--- a/solution.py
+++ b/solution.py
@@ -103,111 +103,187 @@
     return (allowed, weight.astype(jnp.float32) / 256.0)
 
 
-def swap_core(values):
-    return lax.ppermute(values, "dp", [(at, at ^ 1) for at in range(4)])
-
-
-def swap_y(values):
-    return lax.ppermute(values, "dp", [(at, at ^ 2) for at in range(4)])
-
-
-def swap_x(values):
-    count = lax.axis_size("fsdp")
-    return lax.ppermute(values, "fsdp", [(at, at ^ 1) for at in range(count)])
-
-
-def shift_z(values, hops):
-    count = lax.axis_size("fsdp")
-    return lax.ppermute(values, "fsdp", [(at, (at + 2 * hops) % count) for at in range(count)])
-
-
-def gather_rows(shard):
-    depth = lax.axis_size("fsdp") // 2
-    z_at = lax.axis_index("fsdp") // 2
-    x_at = lax.axis_index("fsdp") % 2
-    ring = [shard] + [shift_z(shard, hops) for hops in range(1, depth)]
-    whole = jnp.zeros((depth, 2) + shard.shape, shard.dtype)
-    rest = (0,) * shard.ndim
-    for hops in range(depth):
-        owner = (z_at + depth - hops) % depth
-        whole = lax.dynamic_update_slice(whole, ring[hops][None, None], (owner, x_at) + rest)
-        other = swap_x(ring[hops])
-        whole = lax.dynamic_update_slice(whole, other[None, None], (owner, 1 - x_at) + rest)
-    return whole.reshape((2 * depth,) + shard.shape)
-
-
-def scatter_rows(whole, link_type):
-    count = lax.axis_size("fsdp")
-    depth = count // 2
-    z_at = lax.axis_index("fsdp") // 2
-    x_at = lax.axis_index("fsdp") % 2
-    paired = whole.reshape((depth, 2) + whole.shape[1:])
-
-    def half(which):
-        return lax.dynamic_index_in_dim(paired, which, 1, keepdims=False)
-
-    arrived = swap_x(half(1 - x_at).astype(link_type))
-    summed = half(x_at).astype(jnp.float32) + arrived.astype(jnp.float32)
-    total = lax.dynamic_index_in_dim(summed, z_at, 0, keepdims=False)
-    low_sum = summed.astype(link_type)
-    for hops in range(1, depth):
-        outgoing = lax.dynamic_index_in_dim(low_sum, (z_at + hops) % depth, 0, keepdims=False)
-        total = total + shift_z(outgoing, hops).astype(jnp.float32)
-    return total
-
-
-def gather_group(values):
-    across = swap_y(values)
-    return [values, swap_core(values), across, swap_core(across)]
-
-
-def scatter_group(parts):
-    first = parts[0] + swap_core(parts[1].astype(jnp.bfloat16)).astype(jnp.float32)
-    second = parts[2] + swap_core(parts[3].astype(jnp.bfloat16)).astype(jnp.float32)
-    return first + swap_y(second.astype(jnp.bfloat16)).astype(jnp.float32)
-
-
-def flip(values, step):
-    blocks = values.reshape((4, values.shape[0] // 4) + values.shape[1:])
-    return jnp.stack([blocks[at ^ step] for at in range(4)]).reshape(values.shape)
-
-
-def gather_columns(values):
-    across = flip(swap_y(values), 2)
-    return [values, flip(swap_core(values), 1), across, flip(swap_core(across), 1)]
-
-
-def scatter_columns(parts):
-    first = parts[0] + swap_core(flip(parts[1].astype(jnp.bfloat16), 1)).astype(jnp.float32)
-    second = parts[2] + swap_core(flip(parts[3].astype(jnp.bfloat16), 1)).astype(jnp.float32)
-    return first + swap_y(flip(second.astype(jnp.bfloat16), 2)).astype(jnp.float32)
-
-
-def sum_group(values):
-    values = values + swap_core(values)
-    return values + swap_y(values)
-
-
-def sum_all(values):
-    values = sum_group(values)
-    count = lax.axis_size("fsdp")
-    step = 1
-    while step < count:
-        values = values + lax.ppermute(
-            values, "fsdp", [(at, at ^ step) for at in range(count)]
-        )
-        step *= 2
-    return values
-
-
-def by_member(parts, member):
-    odd_core = member % 2 == 1
-    high_y = member >= 2
-    near = [jnp.where(odd_core, parts[1], parts[0]), jnp.where(odd_core, parts[0], parts[1])]
-    far = [jnp.where(odd_core, parts[3], parts[2]), jnp.where(odd_core, parts[2], parts[3])]
-    low_pair = [jnp.where(high_y, b, a) for a, b in zip(near, far)]
-    high_pair = [jnp.where(high_y, a, b) for a, b in zip(near, far)]
-    return low_pair + high_pair
+class Lane:
+    def __init__(self):
+        self.last = None
+
+    def send(self, values, axis, pairs):
+        if self.last is not None:
+            values, _ = lax.optimization_barrier((values, self.last))
+        self.last = lax.ppermute(values, axis, pairs)
+        return self.last
+
+
+class Links:
+    def __init__(self):
+        self.members = lax.axis_size("fsdp")
+        self.depth = self.members // 2
+        place = lax.axis_index("fsdp")
+        self.z_at = place // 2
+        self.x_at = place % 2
+        self.member = lax.axis_index("dp")
+        self.lanes = {name: Lane() for name in ("x", "up", "down", "y", "core")}
+
+    def swap_core(self, values):
+        return self.lanes["core"].send(values, "dp", [(at, at ^ 1) for at in range(4)])
+
+    def swap_y(self, values):
+        return self.lanes["y"].send(values, "dp", [(at, at ^ 2) for at in range(4)])
+
+    def swap_x(self, values, low=0, high=None):
+        high = self.depth if high is None else high
+        pairs = [
+            (at, at ^ 1)
+            for at in range(self.members)
+            if low <= at // 2 < high
+        ]
+        return self.lanes["x"].send(values, "fsdp", pairs)
+
+    def slots(self):
+        return [
+            ((self.z_at + self.depth - hops) % self.depth) * 2
+            + (self.x_at if side == 0 else 1 - self.x_at)
+            for side in range(2)
+            for hops in range(self.depth)
+        ]
+
+    def slot_of(self, owner):
+        hops = (self.z_at + self.depth - owner // 2) % self.depth
+        side = (owner % 2) ^ self.x_at
+        return side * self.depth + hops
+
+    def to_slots(self, values):
+        width = values.shape[-1] // self.members
+        return jnp.concatenate(
+            [
+                lax.dynamic_slice_in_dim(values, owner * width, width, values.ndim - 1)
+                for owner in self.slots()
+            ],
+            -1,
+        )
+
+    def from_slots(self, values, first=0, count=None):
+        width = values.shape[-1] // self.members
+        count = self.members if count is None else count
+        return jnp.concatenate(
+            [
+                lax.dynamic_slice_in_dim(
+                    values, self.slot_of(first + at) * width, width, values.ndim - 1
+                )
+                for at in range(count)
+            ],
+            -1,
+        )
+
+    def gather_rows(self, shard):
+        depth = self.depth
+        z_at = self.z_at
+        near = [shard]
+        far = [self.swap_x(shard)]
+        rise, fall, rise_far, fall_far = {}, {}, {}, {}
+        up_run = down_run = shard
+        for hops in range(1, depth):
+            up_run = self.lanes["up"].send(
+                up_run,
+                "fsdp",
+                [(at, at + 2) for at in range(2 * hops - 2, self.members - 2)],
+            )
+            down_run = self.lanes["down"].send(
+                down_run,
+                "fsdp",
+                [(at + 2, at) for at in range(0, self.members - 2 * hops)],
+            )
+            rise[hops], fall[hops] = up_run, down_run
+            if 2 * hops < depth:
+                rise_far[hops] = self.swap_x(up_run, hops, depth)
+                fall_far[hops] = self.swap_x(down_run, 0, depth - hops)
+            else:
+                either = jnp.where(z_at >= hops, up_run, down_run)
+                pairs = [
+                    (at, at ^ 1)
+                    for at in range(self.members)
+                    if at // 2 >= hops or at // 2 < depth - hops
+                ]
+                rise_far[hops] = fall_far[hops] = self.lanes["x"].send(either, "fsdp", pairs)
+        for hops in range(1, depth):
+            near.append(jnp.where(z_at >= hops, rise[hops], fall[depth - hops]))
+            far.append(jnp.where(z_at >= hops, rise_far[hops], fall_far[depth - hops]))
+        return jnp.concatenate(near + far, 0)
+
+    def scatter_rows(self, left_side, right_side):
+        half = left_side.shape[1] // 2
+        rows = half // self.depth
+        outgoing = product_tn(left_side[:, half:], right_side).astype(jnp.bfloat16)
+        arrived = self.swap_x(outgoing).astype(jnp.float32)
+        summed = (product_tn(left_side[:, :half], right_side) + arrived).astype(jnp.bfloat16)
+        total = summed[:rows].astype(jnp.float32)
+        for hops in range(1, self.depth):
+            slot = self.depth - hops
+            lane = self.lanes["down" if 2 * hops > self.depth else "up"]
+            total = total + lane.send(
+                summed[slot * rows : (slot + 1) * rows],
+                "fsdp",
+                [(at, (at + 2 * hops) % self.members) for at in range(self.members)],
+            ).astype(jnp.float32)
+        return total
+
+    def gather_tokens(self, values):
+        pair = jnp.concatenate([values, self.swap_y(values)], 0)
+        return jnp.concatenate([pair, self.swap_core(pair)], 0)
+
+    def scatter_tokens(self, values):
+        half = values.shape[0] // 2
+        quarter = half // 2
+        arrived = self.swap_core(values[half:].astype(jnp.bfloat16))
+        summed = values[:half] + arrived.astype(jnp.float32)
+        return summed[:quarter] + self.swap_y(summed[quarter:].astype(jnp.bfloat16)).astype(
+            jnp.float32
+        )
+
+    def partner(self, at):
+        return self.member ^ ((at % 2) * 2 + at // 2)
+
+    def gather_columns(self, values):
+        across = self.swap_y(turn_y(values))
+        pair = jnp.concatenate([values, across], 1)
+        return jnp.concatenate([pair, self.swap_core(turn_core(pair))], 1)
+
+    def scatter_columns(self, parts):
+        sent = turn_core(jnp.concatenate(parts[2:], 1).astype(jnp.bfloat16))
+        arrived = self.swap_core(sent)
+        width = parts[0].shape[1]
+        first = parts[0] + arrived[:, :width].astype(jnp.float32)
+        second = parts[1] + arrived[:, width:].astype(jnp.float32)
+        return first + self.swap_y(turn_y(second.astype(jnp.bfloat16))).astype(jnp.float32)
+
+    def sum_group(self, values):
+        values = values + self.swap_core(values)
+        return values + self.swap_y(values)
+
+    def gather_copies(self, values):
+        across = self.swap_y(values)
+        other, other_across = self.swap_core(jnp.stack([values, across]))
+        odd_core = self.member % 2 == 1
+        high_y = self.member >= 2
+        near = [jnp.where(odd_core, other, values), jnp.where(odd_core, values, other)]
+        far = [
+            jnp.where(odd_core, other_across, across),
+            jnp.where(odd_core, across, other_across),
+        ]
+        low_pair = [jnp.where(high_y, b, a) for a, b in zip(near, far)]
+        high_pair = [jnp.where(high_y, a, b) for a, b in zip(near, far)]
+        return jnp.concatenate(low_pair + high_pair, -1)
+
+
+def turn_y(values):
+    count = values.shape[0] // 4
+    blocks = [values[at * count : (at + 1) * count] for at in (1, 0, 3, 2)]
+    return jnp.concatenate(blocks, 0)
+
+
+def turn_core(values):
+    half = values.shape[0] // 2
+    return jnp.concatenate([values[half:], values[:half]], 0)
 
 
 def high_dot(equation, left_side, right_side):
@@ -216,9 +292,8 @@
     )
 
 
-def orthogonal(moments):
-    gram = jnp.concatenate([high_dot("mik,mjk->mij", part, part) for part in moments], 0)
-    gram = sum_group(gram)
+def orthogonal(links, moments):
+    gram = links.sum_group(high_dot("mik,mjk->mij", moments, moments))
     norm = jnp.sqrt(jnp.trace(gram, axis1=1, axis2=2)) + 1e-07
     gram = gram / (norm * norm)[:, None, None]
     eye = jnp.eye(gram.shape[-1], dtype=jnp.float32)[None]
@@ -230,13 +305,7 @@
         if turn < 4:
             gram = high_dot("mij,mjk->mik", high_dot("mij,mjk->mik", factor, gram), factor)
     chain = chain / norm[:, None, None]
-    results = []
-    start = 0
-    for part in moments:
-        count = part.shape[0]
-        results.append(high_dot("mij,mjk->mik", chain[start : start + count], part))
-        start += count
-    return results
+    return high_dot("mij,mjk->mik", chain, moments)
 
 
 def adamw(current, grad_in, moment_one, moment_two):
@@ -272,41 +341,49 @@
     mix_out_v,
 ):
     hist_count, tok_count, model_width = history.shape
-    members = lax.axis_size("fsdp")
+    links = Links()
+    members = links.members
+    member = links.member
     rows = attn_weight.shape[1]
     group = lax.axis_size("dp")
-    member = lax.axis_index("dp")
     attn_cols = attn_weight.shape[2] // group
     mlp_cols = mlp_weight.shape[2] // group
+    col_blocks = attn_cols // rows
     heads = HEADS // group
     group_tok = group * tok_count
+    param_rows = params.shape[0]
     head_scale = 1.0 / math.sqrt(HEAD)
 
-    param_pieces = gather_rows(params.astype(jnp.bfloat16))
-    param_vals_low = jnp.moveaxis(param_pieces, 0, 1).reshape(params.shape[0], model_width)
+    param_pieces = lax.all_to_all(
+        jnp.broadcast_to(params.astype(jnp.bfloat16)[None], (members, param_rows, rows)),
+        "fsdp",
+        0,
+        0,
+        tiled=True,
+    )
+    param_vals_low = jnp.moveaxis(param_pieces, 0, 1).reshape(param_rows, model_width)
     param_vals = param_vals_low.astype(jnp.float32)
     mix_weight = param_vals_low[17:]
-    full_up = gather_rows(columns_of(mlp_weight[0], member, mlp_cols, 1)).reshape(
-        model_width, mlp_cols
-    )
-    full_down = gather_rows(columns_of(mlp_weight[1], member, mlp_cols, 1)).reshape(
-        model_width, mlp_cols
-    )
-    full_attn = gather_rows(columns_of(attn_weight, member, attn_cols, 2))
-    full_attn = jnp.moveaxis(full_attn, 0, 1).reshape(4, model_width, attn_cols)
+
+    full_up = links.gather_rows(columns_of(mlp_weight[0], member, mlp_cols, 1))
+    full_down = links.gather_rows(columns_of(mlp_weight[1], member, mlp_cols, 1))
+    attn_shard = columns_of(attn_weight, member, attn_cols, 2)
+    attn_shard = jnp.concatenate([attn_shard[at] for at in range(4)], 1)
+    full_attn = links.gather_rows(attn_shard)
+    full_attn = [full_attn[:, at * attn_cols : (at + 1) * attn_cols] for at in range(4)]
 
     mixing = lax.optimization_barrier(mix_out.astype(jnp.bfloat16)).astype(jnp.float32)
     _, tok_weight = pack_info(doc_lengths[0], doc_domain[0], domain_weight, tok_count)
-    group_lengths = gather_group(doc_lengths)
+    out_cot = out_grad.astype(jnp.float32) * tok_weight[:, None]
+    cot_low = out_cot.astype(jnp.bfloat16)
+    group_lengths = links.gather_tokens(doc_lengths)
     allowed = jnp.stack(
         [
-            pack_info(lengths[0], doc_domain[0], domain_weight, tok_count)[0]
-            for lengths in group_lengths
+            pack_info(group_lengths[at], doc_domain[0], domain_weight, tok_count)[0]
+            for at in range(group)
         ]
     )
-    out_cot = out_grad.astype(jnp.float32) * tok_weight[:, None]
-    cot_low = out_cot.astype(jnp.bfloat16)
-    group_cot = jnp.concatenate(gather_group(cot_low), 0)
+    group_cot = links.gather_tokens(links.to_slots(cot_low))
 
     last_hist = history[hist_count - 1].astype(jnp.float32)
     inv_rms = lax.rsqrt(jnp.mean(last_hist * last_hist, -1, keepdims=True) + 1e-06)
@@ -326,49 +403,43 @@
                 jnp.float32
             )
         streams.append(running)
-    norm_keep = []
-    group_normed = []
-    for index in (3, 0, 1, 2):
+    norm_keep = [None] * 4
+    group_normed = [None] * 4
+    for index in (3, 2, 0, 1):
         result, normed, inv_std = layer_norm(
             streams[index], param_vals[index], param_vals[4 + index]
         )
-        group_normed.append(
-            jnp.concatenate(gather_group(result.astype(jnp.bfloat16)), 0)
-        )
-        norm_keep.append((normed, inv_std))
-    group_normed = group_normed[1:] + group_normed[:1]
-    norm_keep = norm_keep[1:] + norm_keep[:1]
+        group_normed[index] = links.gather_tokens(links.to_slots(result.astype(jnp.bfloat16)))
+        norm_keep[index] = (normed, inv_std)
 
     up_bias = lax.dynamic_index_in_dim(param_vals, 13 + member, 0)
     up_pre = jnp.dot(group_normed[3], full_up, preferred_element_type=jnp.float32) + up_bias
     act_val, gelu_up = jax.vjp(exact_gelu, up_pre)
     act_low = act_val.astype(jnp.bfloat16)
+    down_weight_grad = links.scatter_rows(group_cot, act_low)
     act_grad = jnp.dot(group_cot, full_down, preferred_element_type=jnp.float32)
     up_grad = gelu_up(act_grad)[0].astype(jnp.bfloat16)
-    down_weight_grad = scatter_rows(
-        product_tn(group_cot, act_low).astype(jnp.bfloat16).reshape(members, rows, mlp_cols),
-        jnp.bfloat16,
-    )
-    up_weight_grad = scatter_rows(
-        product_tn(group_normed[3], up_grad)
-        .astype(jnp.bfloat16)
-        .reshape(members, rows, mlp_cols),
-        jnp.bfloat16,
-    )
+    up_weight_grad = links.scatter_rows(group_normed[3], up_grad)
     mlp_in_grad = product_nt(up_grad, full_up)
+    in_grads = [None, None, None, links.from_slots(links.scatter_tokens(mlp_in_grad))]
     mlp_part = product_nt(act_low, full_down)
 
-    def scatter_tokens(part):
-        return scatter_group(
-            [part[at * tok_count : (at + 1) * tok_count] for at in range(group)]
-        )
-
-    in_grads = [None, None, None, scatter_tokens(mlp_in_grad)]
+    cot_cols = links.from_slots(group_cot, member * col_blocks, col_blocks)
+    context_grad_part = product_nt(cot_cols, full_attn[3])
 
     cosine, sine_tab = rope_tables(tok_count)
 
     def split_heads(values):
         return values.reshape(group, tok_count, heads, HEAD)
+
+    context_grad = split_heads(
+        links.scatter_columns(
+            [
+                links.from_slots(context_grad_part, links.partner(at) * col_blocks, col_blocks)
+                for at in range(group)
+            ]
+        ).astype(jnp.bfloat16)
+    )
 
     def bias_piece(row):
         return lax.dynamic_slice(param_vals, (row, member * attn_cols), (1, attn_cols))
@@ -407,24 +478,16 @@
     context_low = (
         take(probs_low, value_low).reshape(group_tok, attn_cols).astype(jnp.bfloat16)
     )
-    group_context = jnp.concatenate(by_member(gather_columns(context_low), member), 1)
-    attn_out = jnp.dot(group_context, full_attn[3], preferred_element_type=jnp.float32)
-    out_part = lax.dynamic_update_slice(
-        mlp_part,
-        columns_of(mlp_part, member, attn_cols, 1) + attn_out,
-        (0, member * attn_cols),
-    )
-    layer_out = (
-        streams[3] + scatter_tokens(out_part) + (param_vals[11] + param_vals[12])
-    ).astype(jnp.bfloat16)
-
-    cot_cols = columns_of(group_cot, member, attn_cols, 1)
-    context_grad_part = product_nt(cot_cols, full_attn[3])
-    context_grad = split_heads(
-        scatter_columns(
-            [columns_of(context_grad_part, member ^ at, attn_cols, 1) for at in range(group)]
-        ).astype(jnp.bfloat16)
-    )
+    context_all = links.gather_columns(context_low)
+    pieces = []
+    for owner in links.slots():
+        place = (owner // col_blocks) ^ member
+        place = (place % 2) * 2 + place // 2
+        start = place * attn_cols + (owner % col_blocks) * rows
+        pieces.append(lax.dynamic_slice_in_dim(context_all, start, rows, 1))
+    group_context = jnp.concatenate(pieces, 1)
+    out_weight_grad = links.scatter_rows(group_context, cot_cols)
+
     prob_grad = pair(context_grad, value_low)
     score_grad = (
         probs * (prob_grad - jnp.sum(probs * prob_grad, -1, keepdims=True))
@@ -439,19 +502,32 @@
         rotate(key_grad, cosine, -sine_tab).reshape(group_tok, attn_cols).astype(jnp.bfloat16)
     )
     proj_grads = (query_back, key_back, value_grad)
-    for index in range(3):
-        in_grads[index] = scatter_tokens(product_nt(proj_grads[index], full_attn[index]))
-    lefts = (group_normed[0], group_normed[1], group_normed[2], group_context)
-    rights = (query_back, key_back, value_grad, cot_cols)
-    attn_grads = [
-        scatter_rows(
-            product_tn(left_side, right_side)
-            .astype(jnp.bfloat16)
-            .reshape(members, rows, attn_cols),
-            jnp.bfloat16,
-        )
-        for left_side, right_side in zip(lefts, rights)
-    ]
+    attn_grads = [None, None, None, out_weight_grad]
+    for index in (2, 0, 1):
+        attn_grads[index] = links.scatter_rows(group_normed[index], proj_grads[index])
+    for index in (2, 0, 1):
+        in_grads[index] = links.from_slots(
+            links.scatter_tokens(product_nt(proj_grads[index], full_attn[index]))
+        )
+
+    mlp_grad = jnp.stack([up_weight_grad, down_weight_grad])
+    mlp_mom = MOMENTUM * mlp_moment + mlp_grad
+    mlp_cur = orthogonal(links, mlp_mom)
+    mlp_new = mlp_master * (1.0 - LR_MUON * DECAY) - LR_MUON * 0.2 * math.sqrt(FF) * mlp_cur
+    mlp_copy = links.gather_copies(mlp_new.astype(jnp.bfloat16))
+
+    attn_out = jnp.dot(group_context, full_attn[3], preferred_element_type=jnp.float32)
+    out_part = mlp_part
+    for at in range(col_blocks):
+        place = links.slot_of(member * col_blocks + at) * rows
+        piece = lax.dynamic_slice_in_dim(out_part, place, rows, 1)
+        piece = piece + attn_out[:, at * rows : (at + 1) * rows]
+        out_part = lax.dynamic_update_slice_in_dim(out_part, piece, place, 1)
+    layer_out = (
+        streams[3]
+        + links.from_slots(links.scatter_tokens(out_part))
+        + (param_vals[11] + param_vals[12])
+    ).astype(jnp.bfloat16)
 
     stream_grads = []
     gain_list = []
@@ -503,47 +579,44 @@
     history_grad = jnp.stack(hist_parts)
     out_bias_grad = jnp.sum(cot_low.astype(jnp.float32), 0)
 
-    def placed(values, width, at, total):
+    def placed(values, width, total):
         return lax.dynamic_update_slice(
             jnp.zeros((total,), jnp.float32),
             jnp.sum(values.astype(jnp.float32), 0),
-            (at * width,),
+            (member * width,),
         )
 
     param_grad = jnp.concatenate(
         [
             jnp.stack(gain_list),
             jnp.stack(shift_list),
-            jnp.stack([placed(part, attn_cols, member, model_width) for part in proj_grads]),
+            jnp.stack([placed(part, attn_cols, model_width) for part in proj_grads]),
             out_bias_grad[None],
             out_bias_grad[None],
-            placed(up_grad, mlp_cols, member, group * mlp_cols).reshape(-1, model_width),
+            placed(up_grad, mlp_cols, group * mlp_cols).reshape(-1, model_width),
             mix_weight_grad,
         ],
         0,
     )
-    param_pieces_grad = jnp.moveaxis(
-        param_grad.reshape(params.shape[0], members, rows), 1, 0
-    )
-    param_part = sum_group(scatter_rows(param_pieces_grad, jnp.float32))
-    mixing_grad = sum_all(mixing_grad)
-
-    mlp_grad = jnp.stack([up_weight_grad, down_weight_grad])
+    param_pieces_grad = jnp.moveaxis(param_grad.reshape(param_rows, members, rows), 1, 0)
+    mix_size = mixing_grad.size
+    mix_rows = -(-mix_size // rows)
+    mix_flat = jnp.pad(mixing_grad.reshape(-1), (0, mix_rows * rows - mix_size))
+    mix_flat = jnp.broadcast_to(mix_flat.reshape(1, mix_rows, rows), (members, mix_rows, rows))
+    small = lax.all_to_all(
+        jnp.concatenate([param_pieces_grad, mix_flat], 1), "fsdp", 0, 0, tiled=True
+    )
+    small = links.sum_group(jnp.sum(small, 0))
+    param_part = small[:param_rows]
+    mixing_grad = small[param_rows:].reshape(-1)[:mix_size].reshape(mixing_grad.shape)
+
     attn_grad = jnp.stack(attn_grads)
-    mlp_mom = MOMENTUM * mlp_moment + mlp_grad
-    (mlp_cur,) = orthogonal([mlp_mom])
-    mlp_new = mlp_master * (1.0 - LR_MUON * DECAY) - LR_MUON * 0.2 * math.sqrt(FF) * mlp_cur
-    mlp_copy = jnp.concatenate(
-        by_member(gather_group(mlp_new.astype(jnp.bfloat16)), member), 2
-    )
     attn_mom = MOMENTUM * attn_moment + attn_grad
-    (attn_cur,) = orthogonal([attn_mom])
+    attn_cur = orthogonal(links, attn_mom)
     attn_new = (
         attn_master * (1.0 - LR_MUON * DECAY) - LR_MUON * 0.2 * math.sqrt(model_width) * attn_cur
     )
-    attn_copy = jnp.concatenate(
-        by_member(gather_group(attn_new.astype(jnp.bfloat16)), member), 2
-    )
+    attn_copy = links.gather_copies(attn_new.astype(jnp.bfloat16))
     params_m_new, params_v_new, params_new = adamw(params, param_part, params_m, params_v)
     mix_out_m_new, mix_out_v_new, mix_out_new = adamw(mix_out, mixing_grad, mix_out_m, mix_out_v)
     return (

time: 1310 us -> 1210 us (0.924)
  waiting for transfers between devices: 618 us -> 445 us
  other arithmetic: 161 us -> 186 us
  starting transfers between devices: 136 us -> 161 us
    ppermute x112 -> x93, waiting for transfers between devices: 618 us -> 436 us  [send(): self.last = lax.ppermute(values, axis, pairs)]
    unnamed x444 -> x648, local copies, waits for them, and re-layouts: 22 us -> 59.5 us
    dynamic_update_slice x32 -> x0, local copies, waits for them, and re-layouts: 35.7 us -> none  [the longest x16 18.1 us: gather_rows(): lax.dynamic_update_slice(whole, ring[hops][None, None], (owner, x_at) + r...]
    convert_element_type x12 -> x2, other arithmetic: 36.2 us -> 2.73 us  [the longest x1 2.73 us: body(): context_grad = split_heads(links.scatter_columns([links.from_slots(contex...]
    concatenate x3 -> x23, other arithmetic: 6.68 us -> 36.4 us  [the longest x5 10.3 us: gather_tokens(): return jnp.concatenate([pair, self.swap_core(pair)], 0)]
    ppermute x112 -> x93, starting transfers between devices: 136 us -> 152 us  [send(): self.last = lax.ppermute(values, axis, pairs)]
    slice x12 -> x25, local copies, waits for them, and re-layouts: 14.7 us -> 28.8 us  [the longest x5 10.3 us: scatter_tokens(): arrived = self.swap_core(values[half:].astype(jnp.bfloat16))]
    dot_general x7 -> x13, matrix products: 42.4 us -> 52.8 us  [product_tn(): lax.dot_general(left_side, right_side, (((0,), (0,)), ((), ())), preferre...]
  transfers between devices with their start and end apart: 112 -> 95, of which waited for: 36 -> 38; matrix products, arithmetic and copies ran while one was open for 40% -> 36% of each run, Pallas kernels for 0% -> 0%
where the time goes in v2:
time: 1210 us; the launch traced here: 1190 us
  waiting for transfers between devices  445 us (37%)
  matrix products  244 us (20%)
  other arithmetic  186 us (15%)
  starting transfers between devices  161 us (13%)
  local copies, waits for them, and re-layouts  152 us (13%)
    ppermute x93, waiting for transfers between devices, send(): self.last = lax.ppermute(values, axis, pairs)  436 us
    ppermute x93, starting transfers between devices, send(): self.last = lax.ppermute(values, axis, pairs)  152 us
    unnamed x648, local copies, waits for them, and re-layouts  59.5 us
    dot_general x13, matrix products, product_tn(): lax.dot_general(left_side, right_side, (((0,), (0,)), ((), ())), preferre...  52.8 us
    dot_general x7, matrix products, product_nt(): lax.dot_general(left_side, right_side, (((1,), (1,)), ((), ())), preferre...  48.8 us
    dot_general x38, matrix products, high_dot(): jnp.einsum(equation, left_side, right_side, precision=HIGHEST, preferred_...  48.1 us
    dot_general x1, matrix products, body(): jnp.dot(group_normed[3], full_up, preferred_element_type=jnp.float32)  36.5 us
  transfers between devices with their start and end apart: 95, of which 38 were waited for; matrix products, arithmetic and copies ran while one was open for 36% of the time, Pallas kernels for 0%

profile of v2, /device:TPU:1, one launch (start us, length us, event | category | flops | bytes accessed | tf_op | source)
XLA Modules:
  0.0 1193.9 jit_solution(11098138049932649914)
XLA Ops:
  76.5 18.8 %collective-permute-done.8 = bf16[256,2048]{1,0:T(8,128)(2,1)S(1)} collective-permute-done((bf16[256,2048]{1,0:T(8,128)(2,1)}, bf16[256,2048]{1,0:T(8,128)(2,1)S(1)}, u32[]{:S(2)}, u32[]{:S(2)}) %collective-permute-start.8) | collective-permute-done | bytes 1048608 | tf_op jit(solution)/shard_map/ppermute | solution.py:113
  105.2 13.3 %collective-permute-done.9 = bf16[256,2048]{1,0:T(8,128)(2,1)S(1)} collective-permute-done((bf16[256,2048]{1,0:T(8,128)(2,1)S(1)}, bf16[256,2048]{1,0:T(8,128)(2,1)S(1)}, u32[]{:S(2)}, u32[]{:S(2)}) %collective-permute-start.9) | collective-permute-done | bytes 1048608 | tf_op jit(solution)/shard_map/ppermute | solution.py:113
  140.1 12.2 %collective-permute-done.15 = bf16[256,2048]{1,0:T(8,128)(2,1)S(1)} collective-permute-done((bf16[256,2048]{1,0:T(8,128)(2,1)S(1)}, bf16[256,2048]{1,0:T(8,128)(2,1)S(1)}, u32[]{:S(2)}, u32[]{:S(2)}) %collective-permute-start.15) | collective-permute-done | bytes 1048608 | tf_op jit(solution)/shard_map/ppermute | solution.py:113
  170.5 13.2 %collective-permute-done.19 = bf16[256,2048]{1,0:T(8,128)(2,1)S(1)} collective-permute-done((bf16[256,2048]{1,0:T(8,128)(2,1)S(1)}, bf16[256,2048]{1,0:T(8,128)(2,1)S(1)}, u32[]{:S(2)}, u32[]{:S(2)}) %collective-permute-start.19) | collective-permute-done | bytes 1048608 | tf_op jit(solution)/shard_map/ppermute | solution.py:113
  193.3 36.5 %multiply_convert_fusion = (bf16[1024,2048]{1,0:T(8,128)(2,1)}, f32[1024,2048]{1,0:T(8,128)}, f32[1024,2048]{1,0:T(8,128)}) fusion(f32[2048]{0:T(1024)S(1)} %bitcast.727, bf16[2048,2048]{1,0:T(8,128)(2,1)} %select_dynamic-update-slice_fusion.8, bf16[512,2048]{1,0:T(8,128)(2,1)S(1)} %collective-permute-done.5, ...), kind=kOutput, calls=%fused_computation.7 | convolution fusion | flops 8740929536 | bytes 33562624 | tf_op jit(solution)/shard_map/dot_general | solution.py:416
  238.9 8.3 convolution_convert_fusion
  277.4 11.5 collective-permute-done.32
  301.8 11.3 collective-permute-done.33
  328.5 20.8 %convert_reduce_fusion = (f32[2048]{0:T(1024)S(1)}, bf16[1024,2048]{1,0:T(8,128)(2,1)}) fusion(f32[1024,2048]{1,0:T(8,128)} %get-tuple-element.301, bf16[2048,2048]{1,0:T(8,128)(2,1)} %select_dynamic-update-slice_fusion.4, bf16[512,2048]{1,0:T(8,128)(2,1)S(1)} %copy-done.77, bf16[256,2048]{1,0:T(8,128)(2,1)} %collective-permute-done.1, ...), kind=kOutput, calls=%fused_computation.3 | convolution fusion | flops 8638167040 | bytes 33570816 | tf_op jit(solution)/shard_map/dot_general | solution.py:420
  350.0 12.6 %fusion.299 = f32[1024,2048]{1,0:T(8,128)S(1)} fusion(bf16[1024,2048]{1,0:T(8,128)(2,1)} %get-tuple-element.464, bf16[2048,2048]{1,0:T(8,128)(2,1)} %select_dynamic-update-slice_fusion.8), kind=kOutput, calls=%fused_computation.733 | convolution fusion | flops 8589934592 | bytes 20971520 | tf_op jit(solution)/shard_map/dot_general | solution.py:75
  371.5 15.0 %fusion.298 = f32[1024,2048]{1,0:T(8,128)} fusion(bf16[1024,2048]{1,0:T(8,128)(2,1)} %get-tuple-element.300, bf16[2048,2048]{1,0:T(8,128)(2,1)} %select_dynamic-update-slice_fusion.4), kind=kOutput, calls=%fused_computation.732 | convolution fusion | flops 8589934592 | bytes 20971520 | tf_op jit(solution)/shard_map/dot_general | solution.py:75
  425.8 13.1 %collective-permute-done.40 = bf16[256,2048]{1,0:T(8,128)(2,1)S(1)} collective-permute-done((bf16[256,2048]{1,0:T(8,128)(2,1)S(1)}, bf16[256,2048]{1,0:T(8,128)(2,1)S(1)}, u32[]{:S(2)}, u32[]{:S(2)}) %collective-permute-start.40) | collective-permute-done | bytes 1048608 | tf_op jit(solution)/shard_map/ppermute | solution.py:113
  569.2 33.7 %collective-permute-done.51 = bf16[1024,2048]{1,0:T(8,128)(2,1)} collective-permute-done((bf16[1024,2048]{1,0:T(8,128)(2,1)}, bf16[1024,2048]{1,0:T(8,128)(2,1)}, u32[]{:S(2)}, u32[]{:S(2)}) %collective-permute-start.51) | collective-permute-done | bytes 4194336 | tf_op jit(solution)/shard_map/ppermute | solution.py:113
  662.3 44.7 %collective-permute-done.54 = bf16[256,2048]{1,0:T(8,128)(2,1)S(1)} collective-permute-done((bf16[256,2048]{1,0:T(8,128)(2,1)S(1)}, bf16[256,2048]{1,0:T(8,128)(2,1)S(1)}, u32[]{:S(2)}, u32[]{:S(2)}) %collective-permute-start.54) | collective-permute-done | bytes 1048608 | tf_op jit(solution)/shard_map/ppermute | solution.py:113
  713.9 7.9 add_convert_fusion.1
  726.0 11.8 collective-permute-done.63
  744.2 25.3 %collective-permute-done.55 = bf16[256,2048]{1,0:T(8,128)(2,1)S(1)} collective-permute-done((bf16[256,2048]{1,0:T(8,128)(2,1)S(1)}, bf16[256,2048]{1,0:T(8,128)(2,1)S(1)}, u32[]{:S(2)}, u32[]{:S(2)}) %collective-permute-start.55) | collective-permute-done | bytes 1048608 | tf_op jit(solution)/shard_map/ppermute | solution.py:113
  783.5 33.7 %collective-permute-done.56 = bf16[256,2048]{1,0:T(8,128)(2,1)} collective-permute-done((bf16[256,2048]{1,0:T(8,128)(2,1)}, bf16[256,2048]{1,0:T(8,128)(2,1)}, u32[]{:S(2)}, u32[]{:S(2)}) %collective-permute-start.56) | collective-permute-done | bytes 1048608 | tf_op jit(solution)/shard_map/ppermute | solution.py:113
  895.9 36.3 %collective-permute-done.67 = bf16[2,256,2048]{2,1,0:T(8,128)(2,1)S(1)} collective-permute-done((bf16[2,256,2048]{2,1,0:T(8,128)(2,1)S(1)}, bf16[2,256,2048]{2,1,0:T(8,128)(2,1)S(1)}, u32[]{:S(2)}, u32[]{:S(2)}) %collective-permute-start.67) | collective-permute-done | bytes 2097184 | tf_op jit(solution)/shard_map/ppermute | solution.py:113
  948.9 8.9 collective-permute-done.79
  972.5 12.2 %collective-permute-done.85 = bf16[256,512]{1,0:T(8,128)(2,1)S(1)} collective-permute-done((bf16[256,512]{1,0:T(8,128)(2,1)S(1)}, bf16[256,512]{1,0:T(8,128)(2,1)S(1)}, u32[]{:S(2)}, u32[]{:S(2)}) %collective-permute-start.85) | collective-permute-done | bytes 262176 | tf_op jit(solution)/shard_map/ppermute | solution.py:113
  1019.5 9.7 collective-permute-done.70
  1104.4 22.2 %collective-permute-done.90 = f32[4,256,256]{2,1,0:T(8,128)S(1)} collective-permute-done((f32[4,256,256]{2,1,0:T(8,128)S(1)}, f32[4,256,256]{2,1,0:T(8,128)S(1)}, u32[]{:S(2)}, u32[]{:S(2)}) %collective-permute-start.90) | collective-permute-done | bytes 1048608 | tf_op jit(solution)/shard_map/ppermute | solution.py:113
  1153.6 21.2 %collective-permute-done.91 = bf16[4,256,512]{2,1,0:T(8,128)(2,1)S(1)} collective-permute-done((bf16[4,256,512]{2,1,0:T(8,128)(2,1)S(1)}, bf16[4,256,512]{2,1,0:T(8,128)(2,1)S(1)}, u32[]{:S(2)}, u32[]{:S(2)}) %collective-permute-start.91) | collective-permute-done | bytes 1048608 | tf_op jit(solution)/shard_map/ppermute | solution.py:113
  (1142 shorter events, 733.7 us)
Async XLA Ops:
  9.5 60.7 %collective-permute-start.6 = (bf16[256,2048]{1,0:T(8,128)(2,1)}, bf16[256,2048]{1,0:T(8,128)(2,1)}, u32[]{:S(2)}, u32[]{:S(2)}) collective-permute-start(bf16[256,2048]{1,0:T(8,128)(2,1)} %get-tuple-element.307), channel_id=1, source_target_pairs={{0,2},{1,3},{2,4},{3,5},{4,6},{5,7},{8,10},{9,11},{10,12},{11,13},... | collective-permute-start | bytes 3145736 | tf_op jit(solution)/shard_map/ppermute | solution.py:113
  14.6 56.3 %collective-permute-start.7 = (bf16[256,2048]{1,0:T(8,128)(2,1)}, bf16[256,2048]{1,0:T(8,128)(2,1)}, u32[]{:S(2)}, u32[]{:S(2)}) collective-permute-start(bf16[256,2048]{1,0:T(8,128)(2,1)} %get-tuple-element.307), channel_id=1, source_target_pairs={{2,0},{3,1},{4,2},{5,3},{6,4},{7,5},{10,8},{11,9},{12,10},{13,11},... | collective-permute-start | bytes 3145736 | tf_op jit(solution)/shard_map/ppermute | solution.py:113
  15.9 57.8 %collective-permute-start.12 = (bf16[256,2048]{1,0:T(8,128)(2,1)}, bf16[256,2048]{1,0:T(8,128)(2,1)}, u32[]{:S(2)}, u32[]{:S(2)}) collective-permute-start(bf16[256,2048]{1,0:T(8,128)(2,1)} %get-tuple-element.307), channel_id=1, source_target_pairs={{0,1},{1,0},{2,3},{3,2},{4,5},{5,4},{6,7},{7,6},{8,9},{9,8},{10,11... | collective-permute-start | bytes 3145736 | tf_op jit(solution)/shard_map/ppermute | solution.py:113
  98.2 64.8 %collective-permute-start.4 = (bf16[512,2048]{1,0:T(8,128)(2,1)S(1)}, bf16[512,2048]{1,0:T(8,128)(2,1)S(1)}, u32[]{:S(2)}, u32[]{:S(2)}) collective-permute-start(bf16[512,2048]{1,0:T(8,128)(2,1)S(1)} %pad_maximum_fusion.10), channel_id=1, source_target_pairs={{0,8},{8,0},{16,24},{24,16},{1,9},{9,1},{17,25},{25,17},{2,10},{10... | collective-permute-start | bytes 6291464 | tf_op jit(solution)/shard_map/ppermute | solution.py:113
  168.5 79.2 %collective-permute-start.43 = (bf16[256,2048]{1,0:T(8,128)(2,1)S(1)}, bf16[256,2048]{1,0:T(8,128)(2,1)S(1)}, u32[]{:S(2)}, u32[]{:S(2)}) collective-permute-start(bf16[256,2048]{1,0:T(8,128)(2,1)S(1)} %constant_dynamic-update-slice_fusion.44), channel_id=1, source_target_pairs={{0,16},{8,24},{16,0},{24,8},{1,17},{9,25},{17,1},{25,9},{2,18},{10... | collective-permute-start | bytes 3145736 | tf_op jit(solution)/shard_map/ppermute | solution.py:113
  169.8 60.8 %collective-permute-start.22 = (bf16[256,2048]{1,0:T(8,128)(2,1)S(1)}, bf16[256,2048]{1,0:T(8,128)(2,1)S(1)}, u32[]{:S(2)}, u32[]{:S(2)}) collective-permute-start(bf16[256,2048]{1,0:T(8,128)(2,1)S(1)} %collective-permute-done.21), channel_id=1, source_target_pairs={{4,6},{5,7},{12,14},{13,15},{20,22},{21,23},{28,30},{29,31}} | collective-permute-start | bytes 3145736 | tf_op jit(solution)/shard_map/ppermute | solution.py:113
  183.7 53.9 %collective-permute-start.20 = (bf16[256,2048]{1,0:T(8,128)(2,1)S(1)}, bf16[256,2048]{1,0:T(8,128)(2,1)S(1)}, u32[]{:S(2)}, u32[]{:S(2)}) collective-permute-start(bf16[256,2048]{1,0:T(8,128)(2,1)S(1)} %collective-permute-done.19), channel_id=1, source_target_pairs={{2,0},{3,1},{10,8},{11,9},{18,16},{19,17},{26,24},{27,25}} | collective-permute-start | bytes 3145736 | tf_op jit(solution)/shard_map/ppermute | solution.py:113
  189.8 101.8 %collective-permute-start.29 = (bf16[512,2048]{1,0:T(8,128)(2,1)S(1)}, bf16[512,2048]{1,0:T(8,128)(2,1)S(1)}, u32[]{:S(2)}, u32[]{:S(2)}) collective-permute-start(bf16[512,2048]{1,0:T(8,128)(2,1)S(1)} %pad_maximum_fusion.11), channel_id=1, source_target_pairs={{0,8},{8,0},{16,24},{24,16},{1,9},{9,1},{17,25},{25,17},{2,10},{10... | collective-permute-start | bytes 6291464 | tf_op jit(solution)/shard_map/ppermute | solution.py:113
  510.8 92.2 %collective-permute-start.51 = (bf16[1024,2048]{1,0:T(8,128)(2,1)}, bf16[1024,2048]{1,0:T(8,128)(2,1)}, u32[]{:S(2)}, u32[]{:S(2)}) collective-permute-start(bf16[1024,2048]{1,0:T(8,128)(2,1)} %convolution_convert_fusion), channel_id=1, source_target_pairs={{0,1},{1,0},{2,3},{3,2},{4,5},{5,4},{6,7},{7,6},{8,9},{9,8},{10,11... | collective-permute-start | bytes 12582920 | tf_op jit(solution)/shard_map/ppermute | solution.py:113
  568.2 70.1 %collective-permute-start.50 = (bf16[1024,1024]{1,0:T(8,128)(2,1)}, bf16[1024,1024]{1,0:T(8,128)(2,1)}, u32[]{:S(2)}, u32[]{:S(2)}) collective-permute-start(bf16[1024,1024]{1,0:T(8,128)(2,1)} %pad_maximum_fusion.16), channel_id=1, source_target_pairs={{0,8},{8,0},{16,24},{24,16},{1,9},{9,1},{17,25},{25,17},{2,10},{10... | collective-permute-start | bytes 6291464 | tf_op jit(solution)/shard_map/ppermute | solution.py:113
  622.4 91.5 %collective-permute-start.52 = (bf16[1024,2048]{1,0:T(8,128)(2,1)}, bf16[1024,2048]{1,0:T(8,128)(2,1)}, u32[]{:S(2)}, u32[]{:S(2)}) collective-permute-start(bf16[1024,2048]{1,0:T(8,128)(2,1)} %convolution_convert_fusion.1), channel_id=1, source_target_pairs={{0,1},{1,0},{2,3},{3,2},{4,5},{5,4},{6,7},{7,6},{8,9},{9,8},{10,11... | collective-permute-start | bytes 12582920 | tf_op jit(solution)/shard_map/ppermute | solution.py:113
  638.3 68.8 %collective-permute-start.54 = (bf16[256,2048]{1,0:T(8,128)(2,1)S(1)}, bf16[256,2048]{1,0:T(8,128)(2,1)S(1)}, u32[]{:S(2)}, u32[]{:S(2)}) collective-permute-start(bf16[256,2048]{1,0:T(8,128)(2,1)S(1)} %copy-done.108), channel_id=1, source_target_pairs={{0,4},{1,5},{2,6},{3,7},{4,0},{5,1},{6,2},{7,3},{8,12},{9,13},{10,... | collective-permute-start | bytes 3145736 | tf_op jit(solution)/shard_map/ppermute | solution.py:113
  638.3 71.0 %collective-permute-start.59 = (bf16[512,2048]{1,0:T(8,128)(2,1)S(1)}, bf16[512,2048]{1,0:T(8,128)(2,1)S(1)}, u32[]{:S(2)}, u32[]{:S(2)}) collective-permute-start(bf16[512,2048]{1,0:T(8,128)(2,1)S(1)} %slice.1105), channel_id=1, source_target_pairs={{0,8},{8,0},{16,24},{24,16},{1,9},{9,1},{17,25},{25,17},{2,10},{10... | collective-permute-start | bytes 6291464 | tf_op jit(solution)/shard_map/ppermute | solution.py:113
  709.2 61.9 %collective-permute-start.60 = (bf16[512,2048]{1,0:T(8,128)(2,1)S(1)}, bf16[512,2048]{1,0:T(8,128)(2,1)S(1)}, u32[]{:S(2)}, u32[]{:S(2)}) collective-permute-start(bf16[512,2048]{1,0:T(8,128)(2,1)S(1)} %slice.1106), channel_id=1, source_target_pairs={{0,8},{8,0},{16,24},{24,16},{1,9},{9,1},{17,25},{25,17},{2,10},{10... | collective-permute-start | bytes 6291464 | tf_op jit(solution)/shard_map/ppermute | solution.py:113
  723.0 52.6 %collective-permute-start.58 = (bf16[256,2048]{1,0:T(8,128)(2,1)S(1)}, bf16[256,2048]{1,0:T(8,128)(2,1)S(1)}, u32[]{:S(2)}, u32[]{:S(2)}) collective-permute-start(bf16[256,2048]{1,0:T(8,128)(2,1)S(1)} %get-tuple-element.160), channel_id=1, source_target_pairs={{0,6},{1,7},{2,0},{3,1},{4,2},{5,3},{6,4},{7,5},{8,14},{9,15},{10,... | collective-permute-start | bytes 3145736 | tf_op jit(solution)/shard_map/ppermute | solution.py:113
  769.4 47.7 %collective-permute-start.56 = (bf16[256,2048]{1,0:T(8,128)(2,1)}, bf16[256,2048]{1,0:T(8,128)(2,1)}, u32[]{:S(2)}, u32[]{:S(2)}) collective-permute-start(bf16[256,2048]{1,0:T(8,128)(2,1)} %get-tuple-element.158), channel_id=1, source_target_pairs={{0,4},{1,5},{2,6},{3,7},{4,0},{5,1},{6,2},{7,3},{8,12},{9,13},{10,... | collective-permute-start | bytes 3145736 | tf_op jit(solution)/shard_map/ppermute | solution.py:113
  769.6 52.7 %collective-permute-start.72 = (bf16[1024,512]{1,0:T(8,128)(2,1)}, bf16[1024,512]{1,0:T(8,128)(2,1)}, u32[]{:S(2)}, u32[]{:S(2)}) collective-permute-start(bf16[1024,512]{1,0:T(8,128)(2,1)} %fusion.168), channel_id=1, source_target_pairs={{0,1},{1,0},{2,3},{3,2},{4,5},{5,4},{6,7},{7,6},{8,9},{9,8},{10,11... | collective-permute-start | bytes 3145736 | tf_op jit(solution)/shard_map/ppermute | solution.py:113
  771.1 58.3 %collective-permute-start.61 = (bf16[512,2048]{1,0:T(8,128)(2,1)}, bf16[512,2048]{1,0:T(8,128)(2,1)}, u32[]{:S(2)}, u32[]{:S(2)}) collective-permute-start(bf16[512,2048]{1,0:T(8,128)(2,1)} %slice.1107), channel_id=1, source_target_pairs={{0,8},{8,0},{16,24},{24,16},{1,9},{9,1},{17,25},{25,17},{2,10},{10... | collective-permute-start | bytes 6291464 | tf_op jit(solution)/shard_map/ppermute | solution.py:113
  776.6 69.8 %collective-permute-start.80 = (bf16[256,512]{1,0:T(8,128)(2,1)}, bf16[256,512]{1,0:T(8,128)(2,1)S(1)}, u32[]{:S(2)}, u32[]{:S(2)}) collective-permute-start(bf16[256,512]{1,0:T(8,128)(2,1)} %get-tuple-element.182), channel_id=1, source_target_pairs={{0,6},{1,7},{2,0},{3,1},{4,2},{5,3},{6,4},{7,5},{8,14},{9,15},{10,... | collective-permute-start | bytes 786440 | tf_op jit(solution)/shard_map/ppermute | solution.py:113
  782.8 50.6 %collective-permute-start.64 = (bf16[256,2048]{1,0:T(8,128)(2,1)}, bf16[256,2048]{1,0:T(8,128)(2,1)S(1)}, u32[]{:S(2)}, u32[]{:S(2)}) collective-permute-start(bf16[256,2048]{1,0:T(8,128)(2,1)} %slice.1112), channel_id=1, source_target_pairs={{0,16},{8,24},{16,0},{24,8},{1,17},{9,25},{17,1},{25,9},{2,18},{10... | collective-permute-start | bytes 3145736 | tf_op jit(solution)/shard_map/ppermute | solution.py:113
  866.1 79.3 %collective-permute-start.83 = (bf16[1024,512]{1,0:T(8,128)(2,1)}, bf16[1024,512]{1,0:T(8,128)(2,1)}, u32[]{:S(2)}, u32[]{:S(2)}) collective-permute-start(bf16[1024,512]{1,0:T(8,128)(2,1)} %fusion.171), channel_id=1, source_target_pairs={{0,1},{1,0},{2,3},{3,2},{4,5},{5,4},{6,7},{7,6},{8,9},{9,8},{10,11... | collective-permute-start | bytes 3145736 | tf_op jit(solution)/shard_map/ppermute | solution.py:113
  889.0 70.1 %collective-permute-start.82 = (bf16[256,512]{1,0:T(8,128)(2,1)}, bf16[256,512]{1,0:T(8,128)(2,1)}, u32[]{:S(2)}, u32[]{:S(2)}) collective-permute-start(bf16[256,512]{1,0:T(8,128)(2,1)} %get-tuple-element.184), channel_id=1, source_target_pairs={{0,6},{1,7},{2,0},{3,1},{4,2},{5,3},{6,4},{7,5},{8,14},{9,15},{10,... | collective-permute-start | bytes 786440 | tf_op jit(solution)/shard_map/ppermute | solution.py:113
  892.1 49.7 %collective-permute-start.78 = (bf16[256,512]{1,0:T(8,128)(2,1)S(1)}, bf16[256,512]{1,0:T(8,128)(2,1)S(1)}, u32[]{:S(2)}, u32[]{:S(2)}) collective-permute-start(bf16[256,512]{1,0:T(8,128)(2,1)S(1)} %get-tuple-element.180), channel_id=1, source_target_pairs={{0,2},{1,3},{2,4},{3,5},{4,6},{5,7},{6,0},{7,1},{8,10},{9,11},{10,... | collective-permute-start | bytes 786440 | tf_op jit(solution)/shard_map/ppermute | solution.py:113
  934.9 55.4 %collective-permute-start.68 = (bf16[2,2,256,2048]{3,2,1,0:T(8,128)(2,1)}, bf16[2,2,256,2048]{3,2,1,0:T(8,128)(2,1)}, u32[]{:S(2)}, u32[]{:S(2)}) collective-permute-start(bf16[2,2,256,2048]{3,2,1,0:T(8,128)(2,1)} %pad_maximum_fusion.7), channel_id=1, source_target_pairs={{0,8},{8,0},{16,24},{24,16},{1,9},{9,1},{17,25},{25,17},{2,10},{10... | collective-permute-start | bytes 12582920 | tf_op jit(solution)/shard_map/ppermute | solution.py:113
  (349 other events, 4671.8 us)

commit v3 on v0

v3 whole, which is shorter than its diff:
```python
import functools
import math

import jax
import jax.numpy as jnp
from jax import lax
from jax.experimental import pallas as pl
from jax.experimental.pallas import tpu as pltpu
from jax.sharding import PartitionSpec as P

HEADS = 16
HEAD = 128
FF = 8192
ROT = 32
MIXW = 36
DOCS = 3
NDOM = 22
STEP = 6


NS_A = 3.4445
NS_B = -4.775
NS_C = 2.0315
ROPE_BASE = 10000.0
LR_MUON = 0.1
LR_ADAM = 0.03
DECAY = 0.01
MOMENTUM = 0.95
BETA_ONE = 0.9
BETA_TWO = 0.95
HIGHEST = lax.Precision.HIGHEST


def rope_rows(tok_count):
    half_rot = ROT // 2
    inverse_freq = ROPE_BASE ** (-(2.0 * jnp.arange(half_rot, dtype=jnp.float32)) / ROT)
    angles = jnp.arange(tok_count, dtype=jnp.float32)[:, None] * inverse_freq[None, :]
    cosine, sine_tab = jnp.cos(angles), jnp.sin(angles)
    zero = jnp.zeros_like(sine_tab)
    rest = jnp.zeros((tok_count, HEAD - ROT), jnp.float32)
    return jnp.stack(
        [
            jnp.concatenate([cosine, cosine, rest + 1.0], 1),
            jnp.concatenate([-sine_tab, zero, rest], 1),
            jnp.concatenate([zero, sine_tab, rest], 1),
        ]
    )


def product_nt(left_side, right_side):
    return lax.dot_general(
        left_side, right_side, (((1,), (1,)), ((), ())), preferred_element_type=jnp.float32
    )


def product_tn(left_side, right_side):
    return lax.dot_general(
        left_side, right_side, (((0,), (0,)), ((), ())), preferred_element_type=jnp.float32
    )


def token_weights(lengths, domains, weight_table, tok_count):
    doc_ends = jnp.cumsum(lengths)
    positions = jnp.arange(tok_count, dtype=jnp.int32)
    doc_of = jnp.sum((positions[:, None] >= doc_ends[None, :]).astype(jnp.int32), 1)
    domain = jnp.sum(
        jnp.where(
            doc_of[:, None] == jnp.arange(DOCS, dtype=jnp.int32)[None, :], domains[None, :], 0
        ),
        1,
    )
    weight = jnp.sum(
        jnp.where(
            domain[:, None] == jnp.arange(NDOM, dtype=jnp.int32)[None, :], weight_table[None, :], 0
        ),
        1,
    )
    return weight.astype(jnp.float32) / 256.0


SMALL_COST = pl.CostEstimate(flops=1, bytes_accessed=1, transcendentals=0)
VMEM_BYTES = 56 * 1024 * 1024


def kernel_params():
    return pltpu.CompilerParams(vmem_limit_bytes=VMEM_BYTES)


def whole_block(shape):
    return pl.BlockSpec(shape, lambda *_: (0,) * len(shape))


def shaped(shape, dtype):
    return jax.ShapeDtypeStruct(shape, dtype)


def gelu_pair(values):
    share = 0.5 * (1.0 + lax.erf(values * math.sqrt(0.5)))
    bell = jnp.exp(-0.5 * values * values) * (1.0 / math.sqrt(2.0 * math.pi))
    return (values * share, share + values * bell)


def dot_nn(left_side, right_side):
    return jnp.dot(left_side, right_side, preferred_element_type=jnp.float32)


def exact_dot(left_side, right_side, dims=((1,), (0,))):
    return lax.dot_general(
        left_side,
        right_side,
        (dims, ((), ())),
        precision=HIGHEST,
        preferred_element_type=jnp.float32,
    )


def copy_kernel(order_ref, *refs, counts):
    sources, targets = refs[: -len(counts)], refs[-len(counts) :]
    at = 0
    for target, count in zip(targets, counts):
        height = target.shape[0] // count
        for place in range(count):
            target[place * height : (place + 1) * height, :] = sources[at][...]
            at += 1


def take_blocks(groups, order, width):
    count = order.shape[0]
    if width % 128:
        return [
            jnp.concatenate(
                [
                    jnp.concatenate(
                        [
                            lax.dynamic_slice_in_dim(values, order[at] * width, width, 1)
                            for at in range(count)
                        ],
                        1,
                    )
                    for values in arrays
                ],
                0,
            )
            for arrays in groups
        ]
    flat = [values for arrays in groups for values in arrays]
    heights = [len(arrays) * arrays[0].shape[0] for arrays in groups]
    return pl.pallas_call(
        functools.partial(copy_kernel, counts=[len(arrays) for arrays in groups]),
        grid_spec=pltpu.PrefetchScalarGridSpec(
            num_scalar_prefetch=1,
            grid=(count,),
            in_specs=[
                pl.BlockSpec((values.shape[0], width), lambda at, order_ref: (0, order_ref[at]))
                for values in flat
            ],
            out_specs=[
                pl.BlockSpec((height, width), lambda at, order_ref: (0, at)) for height in heights
            ],
        ),
        out_shape=[
            shaped((height, count * width), arrays[0].dtype)
            for height, arrays in zip(heights, groups)
        ],
        compiler_params=kernel_params(),
        cost_estimate=SMALL_COST,
        name="take_blocks",
    )(order, *flat)


def rows_kernel(order_ref, left_ref, even_ref, odd_ref, near_ref, far_ref):
    width = even_ref.shape[0]
    half = near_ref.shape[0]
    for at, right_ref in enumerate((even_ref, odd_ref)):
        span = slice(at * width, (at + 1) * width)
        result = product_nt(left_ref[...], right_ref[...])
        near_ref[:, span] = result[:half].astype(near_ref.dtype)
        far_ref[:, span] = result[half:].astype(far_ref.dtype)


def product_rows(left_side, right_side, order, width, far_type):
    tokens, depth = left_side.shape
    half = tokens // 2
    count = order.shape[0]
    if width % 128:
        ((result,),) = [take_blocks([[product_nt(left_side, right_side)]], order, width)]
        return (result[:half], result[half:].astype(far_type))
    out_block = pl.BlockSpec((half, 2 * width), lambda at, order_ref: (0, at))
    return pl.pallas_call(
        rows_kernel,
        grid_spec=pltpu.PrefetchScalarGridSpec(
            num_scalar_prefetch=1,
            grid=(count // 2,),
            in_specs=[
                pl.BlockSpec((tokens, depth), lambda at, order_ref: (0, 0)),
                pl.BlockSpec((width, depth), lambda at, order_ref: (order_ref[2 * at], 0)),
                pl.BlockSpec((width, depth), lambda at, order_ref: (order_ref[2 * at + 1], 0)),
            ],
            out_specs=[out_block, out_block],
        ),
        out_shape=[
            shaped((half, count * width), jnp.float32),
            shaped((half, count * width), far_type),
        ],
        compiler_params=kernel_params(),
        cost_estimate=SMALL_COST,
        name="product_rows",
    )(order, left_side, right_side, right_side)


def grad_kernel(left_refs, right_refs, extra_refs, out_ref):
    start = 0
    for left_ref, right_ref in zip(left_refs, right_refs):
        span = slice(start, start + right_ref.shape[1])
        start = span.stop
        result = product_tn(left_ref[...], right_ref[...])
        if extra_refs:
            result = result + extra_refs[0][:, span].astype(jnp.float32)
        out_ref[:, span] = result.astype(out_ref.dtype)


def half_product(lefts, rights, part, extra=None):
    tokens, width = lefts[0].shape
    columns = rights[0].shape[1]
    tile = 512
    col_tile = columns if len(rights) > 1 else 512
    steps = width // 2 // tile
    out_block = pl.BlockSpec((tile, len(rights) * col_tile), lambda at, to: (at, to))
    extras = [] if extra is None else [extra]
    return pl.pallas_call(
        grad_kernel,
        grid=(steps, columns // col_tile),
        in_specs=[
            [pl.BlockSpec((tokens, tile), lambda at, to: (0, part * steps + at))] * len(lefts),
            [pl.BlockSpec((tokens, col_tile), lambda at, to: (0, to))] * len(rights),
            [out_block] * len(extras),
        ],
        out_specs=out_block,
        out_shape=shaped((width // 2, len(rights) * columns), jnp.bfloat16),
        compiler_params=kernel_params(),
        cost_estimate=SMALL_COST,
        name="half_product",
    )(lefts, rights, extras)


MIX_STEP = 64
MIX_ROWS = 16


def mix_forward_kernel(hist_ref, weight_ref, mixing_ref, norm_ref, *outs):
    normed_refs = outs[:4]
    kept_ref, coef_ref, inner_ref, scale_ref, stream_ref = outs[4:]
    hist_count = hist_ref.shape[0]
    last = hist_ref[hist_count - 1].astype(jnp.float32)
    inv_rms = lax.rsqrt(jnp.mean(last * last, -1, keepdims=True) + 1e-06)
    inner = product_nt((last * inv_rms).astype(jnp.bfloat16), weight_ref[...])
    inner_ref[...] = inner
    hidden, _ = gelu_pair(inner)
    coef_ref[...] = exact_dot(hidden, mixing_ref[:MIXW]) + mixing_ref[MIXW:]

    def rows_step(step, carry):
        rows = pl.ds(pl.multiple_of(step * MIX_ROWS, MIX_ROWS), MIX_ROWS)
        coef = coef_ref[rows, :]
        for index in range(4):
            running = None
            for source in range(hist_count):
                at = index * hist_count + source
                term = coef[:, at : at + 1] * hist_ref[source, rows, :].astype(jnp.float32)
                running = term if running is None else running + term
            if index == 3:
                stream_ref[rows, :] = running
            centred = running - jnp.mean(running, -1, keepdims=True)
            inv_std = lax.rsqrt(jnp.mean(centred * centred, -1, keepdims=True) + 1e-05)
            normed = centred * inv_std
            kept_ref[index, rows, :] = normed
            scale_ref[rows, index : index + 1] = inv_std
            result = normed * norm_ref[index : index + 1] + norm_ref[4 + index : 5 + index]
            normed_refs[index][rows, :] = result.astype(jnp.bfloat16)
        return carry

    lax.fori_loop(0, MIX_STEP // MIX_ROWS, rows_step, 0)


def mix_forward(history, mix_weight, mixing, norm_rows):
    hist_count, tok_count, width = history.shape
    token_block = pl.BlockSpec((MIX_STEP, width), lambda at: (at, 0))
    narrow = pl.BlockSpec((MIX_STEP, MIXW), lambda at: (at, 0))
    return pl.pallas_call(
        mix_forward_kernel,
        grid=(tok_count // MIX_STEP,),
        in_specs=[
            pl.BlockSpec((hist_count, MIX_STEP, width), lambda at: (0, at, 0)),
            whole_block(mix_weight.shape),
            whole_block(mixing.shape),
            whole_block(norm_rows.shape),
        ],
        out_specs=[token_block] * 4
        + [
            pl.BlockSpec((4, MIX_STEP, width), lambda at: (0, at, 0)),
            narrow,
            narrow,
            pl.BlockSpec((MIX_STEP, 4), lambda at: (at, 0)),
            token_block,
        ],
        out_shape=[shaped((tok_count, width), jnp.bfloat16)] * 4
        + [
            shaped((4, tok_count, width), jnp.float32),
            shaped((tok_count, MIXW), jnp.float32),
            shaped((tok_count, MIXW), jnp.float32),
            shaped((tok_count, 4), jnp.float32),
            shaped((tok_count, width), jnp.float32),
        ],
        compiler_params=kernel_params(),
        cost_estimate=SMALL_COST,
        name="mix_forward",
    )(history, mix_weight, mixing, norm_rows)


def mix_backward_kernel(
    hist_ref,
    cot_ref,
    tok_ref,
    back_refs,
    kept_ref,
    coef_ref,
    inner_ref,
    scale_ref,
    weight_ref,
    mixing_ref,
    norm_ref,
    out_ref,
    sums_ref,
    weight_grad_ref,
    mixing_grad_ref,
    stream_ref,
    last_ref,
    coef_grad_ref,
):
    hist_count = hist_ref.shape[0]

    @pl.when(pl.program_id(0) == 0)
    def _():
        sums_ref[...] = jnp.zeros_like(sums_ref)
        weight_grad_ref[...] = jnp.zeros_like(weight_grad_ref)
        mixing_grad_ref[...] = jnp.zeros_like(mixing_grad_ref)

    def rows_step(step, carry):
        rows = pl.ds(pl.multiple_of(step * MIX_ROWS, MIX_ROWS), MIX_ROWS)
        coef = coef_ref[rows, :]
        out_cot = cot_ref[rows, :].astype(jnp.float32) * tok_ref[rows, :]
        cot_low = out_cot.astype(jnp.bfloat16).astype(jnp.float32)
        sums_ref[8:9] += jnp.sum(cot_low, 0, keepdims=True)
        for index in range(4):
            back = back_refs[index][rows, :]
            normed = kept_ref[index, rows, :]
            sums_ref[index : index + 1] += jnp.sum(back * normed, 0, keepdims=True)
            sums_ref[4 + index : 5 + index] += jnp.sum(back, 0, keepdims=True)
            scaled = back * norm_ref[index : index + 1]
            grad = scaled - jnp.mean(scaled, -1, keepdims=True)
            grad = grad - normed * jnp.mean(scaled * normed, -1, keepdims=True)
            grad = grad * scale_ref[rows, index : index + 1]
            if index == 3:
                grad = grad + out_cot
            stream_ref[index] = grad
        for source in range(hist_count):
            values = hist_ref[source, rows, :].astype(jnp.float32)
            running = None
            for index in range(4):
                at = index * hist_count + source
                grad = stream_ref[index]
                coef_grad_ref[rows, at : at + 1] = jnp.sum(values * grad, -1, keepdims=True)
                term = coef[:, at : at + 1] * grad
                running = term if running is None else running + term
            if source == hist_count - 1:
                last_ref[rows, :] = running
            else:
                out_ref[source, rows, :] = running.astype(jnp.bfloat16)
        return carry

    lax.fori_loop(0, MIX_STEP // MIX_ROWS, rows_step, 0)
    coef_grad = coef_grad_ref[...]
    hidden, slope = gelu_pair(inner_ref[...])
    mixing_grad_ref[:MIXW] += exact_dot(hidden, coef_grad, ((0,), (0,)))
    mixing_grad_ref[MIXW:] += jnp.sum(coef_grad, 0, keepdims=True)
    hidden_grad = exact_dot(coef_grad, mixing_ref[:MIXW], ((1,), (1,)))
    inner_grad = (hidden_grad * slope).astype(jnp.bfloat16)
    last = hist_ref[hist_count - 1].astype(jnp.float32)
    inv_rms = lax.rsqrt(jnp.mean(last * last, -1, keepdims=True) + 1e-06)
    unit = last * inv_rms
    weight_grad_ref[...] += product_tn(inner_grad, unit.astype(jnp.bfloat16))
    unit_grad = dot_nn(inner_grad, weight_ref[...])
    last_grad = inv_rms * (unit_grad - unit * jnp.mean(unit_grad * unit, -1, keepdims=True))
    out_ref[hist_count - 1] = (last_ref[...] + last_grad).astype(jnp.bfloat16)


def mix_backward(
    history, cot, tok_weight, backs, kept, coef, inner, scale, mix_weight, mixing, norm_rows
):
    hist_count, tok_count, width = history.shape
    token_block = pl.BlockSpec((MIX_STEP, width), lambda at: (at, 0))
    narrow = pl.BlockSpec((MIX_STEP, MIXW), lambda at: (at, 0))
    hist_block = pl.BlockSpec((hist_count, MIX_STEP, width), lambda at: (0, at, 0))
    return pl.pallas_call(
        mix_backward_kernel,
        grid=(tok_count // MIX_STEP,),
        in_specs=[
            hist_block,
            token_block,
            pl.BlockSpec((MIX_STEP, 1), lambda at: (at, 0)),
            [token_block] * 4,
            pl.BlockSpec((4, MIX_STEP, width), lambda at: (0, at, 0)),
            narrow,
            narrow,
            pl.BlockSpec((MIX_STEP, 4), lambda at: (at, 0)),
            whole_block(mix_weight.shape),
            whole_block(mixing.shape),
            whole_block(norm_rows.shape),
        ],
        out_specs=[
            hist_block,
            whole_block((16, width)),
            whole_block(mix_weight.shape),
            whole_block(mixing.shape),
        ],
        out_shape=[
            shaped(history.shape, jnp.bfloat16),
            shaped((16, width), jnp.float32),
            shaped(mix_weight.shape, jnp.float32),
            shaped(mixing.shape, jnp.float32),
        ],
        scratch_shapes=[
            pltpu.VMEM((4, MIX_ROWS, width), jnp.float32),
            pltpu.VMEM((MIX_STEP, width), jnp.float32),
            pltpu.VMEM((MIX_STEP, MIXW), jnp.float32),
        ],
        compiler_params=kernel_params(),
        cost_estimate=SMALL_COST,
        name="mix_backward",
    )(history, cot, tok_weight, backs, kept, coef, inner, scale, mix_weight, mixing, norm_rows)


def mlp_up_kernel(normed_ref, up_ref, bias_ref, act_ref, slope_ref):
    tokens = normed_ref.shape[0]
    part = tokens // 4
    for at in range(4):
        rows = pl.ds(at * part, part)
        act_val, slope = gelu_pair(dot_nn(normed_ref[rows, :], up_ref[...]) + bias_ref[...])
        act_ref[rows, :] = act_val.astype(jnp.bfloat16)
        slope_ref[rows, :] = slope


def mlp_up(normed, up_weight, bias):
    tokens, width = normed.shape
    hidden = up_weight.shape[1]
    tile = 256
    act_block = pl.BlockSpec((tokens, tile), lambda at: (0, at))
    return pl.pallas_call(
        mlp_up_kernel,
        grid=(hidden // tile,),
        in_specs=[
            whole_block(normed.shape),
            pl.BlockSpec((width, tile), lambda at: (0, at)),
            pl.BlockSpec((1, tile), lambda at: (0, at)),
        ],
        out_specs=[act_block, act_block],
        out_shape=[shaped((tokens, hidden), jnp.bfloat16), shaped((tokens, hidden), jnp.float32)],
        compiler_params=kernel_params(),
        cost_estimate=SMALL_COST,
        name="mlp_up",
    )(normed, up_weight, bias)


def mlp_back_kernel(cot_ref, down_ref, slope_ref, grad_ref, sum_ref):
    tokens = cot_ref.shape[0]
    part = tokens // 4
    total = None
    for at in range(4):
        rows = pl.ds(at * part, part)
        act_grad = dot_nn(cot_ref[rows, :], down_ref[...])
        up_grad = (act_grad * slope_ref[rows, :]).astype(jnp.bfloat16)
        grad_ref[rows, :] = up_grad
        term = jnp.sum(up_grad.astype(jnp.float32), 0, keepdims=True)
        total = term if total is None else total + term
    sum_ref[...] = total


def mlp_back(cot, down_weight, slope):
    tokens, width = cot.shape
    hidden = down_weight.shape[1]
    tile = 256
    act_block = pl.BlockSpec((tokens, tile), lambda at: (0, at))
    row_block = pl.BlockSpec((1, tile), lambda at: (0, at))
    return pl.pallas_call(
        mlp_back_kernel,
        grid=(hidden // tile,),
        in_specs=[
            whole_block(cot.shape),
            pl.BlockSpec((width, tile), lambda at: (0, at)),
            act_block,
        ],
        out_specs=[act_block, row_block],
        out_shape=[shaped((tokens, hidden), jnp.bfloat16), shaped((1, hidden), jnp.float32)],
        compiler_params=kernel_params(),
        cost_estimate=SMALL_COST,
        name="mlp_back",
    )(cot, down_weight, slope)


def attention_kernel(
    ends_ref, normed_refs, weight_refs, bias_ref, rope_ref, cot_ref, ctx_ref, grad_refs, sum_ref
):
    tokens, width = ctx_ref.shape
    at = pl.program_id(0)
    head_scale = 1.0 / math.sqrt(HEAD)
    half_rot = ROT // 2
    cosine, rise, fall = rope_ref[0], rope_ref[1], rope_ref[2]

    def turned(values):
        return pltpu.roll(values, HEAD - half_rot, 1) * rise + pltpu.roll(values, half_rot, 1) * fall

    def doc_of(positions):
        found = jnp.zeros(positions.shape, jnp.int32)
        for doc in range(DOCS):
            found = found + (positions >= ends_ref[at, doc]).astype(jnp.int32)
        return found

    column = lax.broadcasted_iota(jnp.int32, (tokens, tokens), 1)
    row = lax.broadcasted_iota(jnp.int32, (tokens, tokens), 0)
    allowed = (doc_of(row) == doc_of(column)) & (row >= column)
    query_all = dot_nn(normed_refs[0][...], weight_refs[0][...]) + bias_ref[0:1]
    key_all = dot_nn(normed_refs[1][...], weight_refs[1][...]) + bias_ref[1:2]
    value_all = (dot_nn(normed_refs[2][...], weight_refs[2][...]) + bias_ref[2:3]).astype(
        jnp.bfloat16
    )

    @pl.when(at == 0)
    def _():
        sum_ref[...] = jnp.zeros_like(sum_ref)

    for head in range(width // HEAD):
        span = slice(head * HEAD, (head + 1) * HEAD)
        query = query_all[:, span]
        key = key_all[:, span]
        value = value_all[:, span]
        query = (query * cosine + turned(query)).astype(jnp.bfloat16)
        key = (key * cosine + turned(key)).astype(jnp.bfloat16)
        cot = cot_ref[:, span]
        scores = jnp.where(allowed, product_nt(query, key) * head_scale, -1000000000.0)
        weights = jnp.exp(scores - jnp.max(scores, -1, keepdims=True))
        weights = weights / jnp.sum(weights, -1, keepdims=True)
        weights_low = weights.astype(jnp.bfloat16)
        ctx_ref[:, span] = dot_nn(weights_low, value).astype(jnp.bfloat16)
        prob_grad = product_nt(cot, value)
        score_grad = (
            weights * (prob_grad - jnp.sum(weights * prob_grad, -1, keepdims=True))
        ).astype(jnp.bfloat16)
        query_grad = dot_nn(score_grad, key) * head_scale
        key_grad = product_tn(score_grad, query) * head_scale
        value_grad = product_tn(weights_low, cot)
        grads = (
            query_grad * cosine - turned(query_grad),
            key_grad * cosine - turned(key_grad),
            value_grad,
        )
        for index in range(3):
            grad_low = grads[index].astype(jnp.bfloat16)
            grad_refs[index][:, span] = grad_low
            sum_ref[index : index + 1, span] += jnp.sum(
                grad_low.astype(jnp.float32), 0, keepdims=True
            )


def attention_inner(ends, normed, weights, bias, rope, cot):
    group, _ = ends.shape
    tokens = normed[0].shape[0] // group
    model_width, width = weights[0].shape
    normed_block = pl.BlockSpec((tokens, model_width), lambda at: (at, 0))
    head_block = pl.BlockSpec((tokens, width), lambda at: (at, 0))
    out = shaped((group * tokens, width), jnp.bfloat16)
    return pl.pallas_call(
        attention_kernel,
        grid=(group,),
        in_specs=[
            pl.BlockSpec(memory_space=pltpu.SMEM),
            [normed_block] * 3,
            [whole_block(weights[0].shape)] * 3,
            whole_block(bias.shape),
            whole_block(rope.shape),
            head_block,
        ],
        out_specs=[head_block, [head_block] * 3, whole_block((8, width))],
        out_shape=[out, [out] * 3, shaped((8, width), jnp.float32)],
        compiler_params=kernel_params(),
        cost_estimate=SMALL_COST,
        name="attention_inner",
    )(ends, normed, weights, bias, rope, cot)


def finish_kernel(part_refs, moment_ref, grad_ref, mom_ref, gram_ref):
    @pl.when(pl.program_id(0) == 0)
    def _():
        gram_ref[...] = jnp.zeros_like(gram_ref)

    for at, refs in enumerate(part_refs):
        total = refs[0][...].astype(jnp.float32)
        for ref in refs[1:]:
            total = total + ref[...].astype(jnp.float32)
        grad_ref[at] = total
        mom_new = MOMENTUM * moment_ref[at] + total
        mom_ref[at] = mom_new
        gram_ref[at] += exact_dot(mom_new, mom_new, ((1,), (1,)))


def finish_gradient(parts, moment):
    count, rows, width = moment.shape
    tile = 512
    part_block = pl.BlockSpec((rows, tile), lambda at: (0, at))
    stack_block = pl.BlockSpec((count, rows, tile), lambda at: (0, 0, at))
    return pl.pallas_call(
        finish_kernel,
        grid=(width // tile,),
        in_specs=[[[part_block] * len(own) for own in parts], stack_block],
        out_specs=[stack_block, stack_block, whole_block((count, rows, rows))],
        out_shape=[shaped(moment.shape, jnp.float32)] * 2
        + [shaped((count, rows, rows), jnp.float32)],
        compiler_params=kernel_params(),
        cost_estimate=SMALL_COST,
        name="finish_gradient",
    )(parts, moment)


def newton_kernel(gram_ref, mom_ref, master_ref, new_ref, copy_ref, *, rate):
    count, rows, _ = gram_ref.shape
    at_row = lax.broadcasted_iota(jnp.int32, (rows, rows), 0)
    eye = (at_row == lax.broadcasted_iota(jnp.int32, (rows, rows), 1)).astype(jnp.float32)
    chains = [None] * count
    grams = []
    norms = []
    for at in range(count):
        gram = gram_ref[at]
        trace = jnp.sum(jnp.sum(gram * eye, 1, keepdims=True), 0, keepdims=True)
        norm = jnp.sqrt(trace) + 1e-07
        norms.append(norm)
        grams.append(gram / (norm * norm))
    for turn in range(5):
        squares = [exact_dot(gram, gram) for gram in grams]
        factors = [
            NS_A * eye + NS_B * gram + NS_C * square for gram, square in zip(grams, squares)
        ]
        if turn == 0:
            chains = factors
        else:
            chains = [exact_dot(factor, chain) for factor, chain in zip(factors, chains)]
        if turn < 4:
            halves = [exact_dot(factor, gram) for factor, gram in zip(factors, grams)]
            grams = [exact_dot(half, factor) for half, factor in zip(halves, factors)]
    for at in range(count):
        turned = exact_dot(chains[at] / norms[at], mom_ref[at])
        fresh = master_ref[at] * (1.0 - LR_MUON * DECAY) - rate * turned
        new_ref[at] = fresh
        copy_ref[at] = fresh.astype(jnp.bfloat16)


def newton_update(gram, mom, master, rate):
    count, rows, width = mom.shape
    step = 2
    stack_block = pl.BlockSpec((step, rows, width), lambda at: (at, 0, 0))
    return pl.pallas_call(
        functools.partial(newton_kernel, rate=rate),
        grid=(count // step,),
        in_specs=[
            pl.BlockSpec((step, rows, rows), lambda at: (at, 0, 0)),
            stack_block,
            stack_block,
        ],
        out_specs=[stack_block, stack_block],
        out_shape=[shaped(mom.shape, jnp.float32), shaped(mom.shape, jnp.bfloat16)],
        compiler_params=kernel_params(),
        cost_estimate=SMALL_COST,
        name="newton_update",
    )(gram, mom, master)


class Links:
    def __init__(self):
        self.members = lax.axis_size("fsdp")
        self.depth = self.members // 2
        place = lax.axis_index("fsdp")
        self.z_at = place // 2
        self.x_at = place % 2
        self.member = lax.axis_index("dp")

    def swap_core(self, values):
        return lax.ppermute(values, "dp", [(at, at ^ 1) for at in range(4)])

    def swap_y(self, values):
        return lax.ppermute(values, "dp", [(at, at ^ 2) for at in range(4)])

    def swap_x(self, values):
        return lax.ppermute(values, "fsdp", [(at, at ^ 1) for at in range(self.members)])

    def swap_z(self, values, turn):
        pairs = [(at, at ^ (2 * turn)) for at in range(self.members)]
        return lax.ppermute(values, "fsdp", pairs)

    def slots(self):
        return [
            (self.z_at ^ turn) * 2 + (self.x_at ^ side)
            for side in range(2)
            for turn in range(self.depth)
        ]

    def slot_of(self, owner):
        return ((owner % 2) ^ self.x_at) * self.depth + ((owner // 2) ^ self.z_at)

    def slots_of(self, first, count):
        return jnp.stack([self.slot_of(first + at) for at in range(count)]).astype(jnp.int32)

    def hop(self, line):
        rise, fall = line
        hops = len(rise)
        up_pairs = [(at, at + 2) for at in range(2 * hops - 2, self.members - 2)]
        down_pairs = [(at + 2, at) for at in range(0, self.members - 2 * hops)]
        return (
            rise + [lax.ppermute(rise[-1], "fsdp", up_pairs)],
            fall + [lax.ppermute(fall[-1], "fsdp", down_pairs)],
        )

    def near(self, line, turn):
        rise, fall = line
        found = {}
        for place in range(self.depth):
            found.setdefault((place ^ turn) - place, []).append(place)
        result = None
        for distance, places in found.items():
            values = fall[distance] if distance >= 0 else rise[-distance]
            if result is None:
                result = values
                continue
            here = self.z_at == places[0]
            for place in places[1:]:
                here = here | (self.z_at == place)
            result = jnp.where(here, values, result)
        return result

    def partner(self, at):
        return self.member ^ ((at % 2) * 2 + at // 2)

    def sum_group(self, values):
        values = values + self.swap_core(values)
        return values + self.swap_y(values)

    def sum_stack(self, values):
        values = values + self.swap_core(values)
        half = values.shape[0] // 2
        odd_core = self.member % 2
        own = lax.dynamic_slice_in_dim(values, odd_core * half, half, 0)
        own = own + self.swap_y(own)
        other = self.swap_core(own)
        first = jnp.where(odd_core == 1, other, own)
        return jnp.concatenate([first, jnp.where(odd_core == 1, own, other)], 0)

    def gather_copies(self, values, across):
        other = self.swap_core(values)
        other_across = self.swap_core(across)
        odd_core = self.member % 2 == 1
        high_y = self.member >= 2
        near = [jnp.where(odd_core, other, values), jnp.where(odd_core, values, other)]
        far = [
            jnp.where(odd_core, other_across, across),
            jnp.where(odd_core, across, other_across),
        ]
        low_pair = [jnp.where(high_y, b, a) for a, b in zip(near, far)]
        high_pair = [jnp.where(high_y, a, b) for a, b in zip(near, far)]
        return jnp.concatenate(low_pair + high_pair, -1)


def turn_y(values):
    count = values.shape[0] // 4
    blocks = [values[at * count : (at + 1) * count] for at in (1, 0, 3, 2)]
    return jnp.concatenate(blocks, 0)


def turn_core(values):
    half = values.shape[0] // 2
    return jnp.concatenate([values[half:], values[:half]], 0)


def cut(values, counts):
    parts = []
    start = 0
    for count in counts:
        parts.append(values[start : start + count])
        start += count
    return parts


def low(values):
    return values.astype(jnp.bfloat16)


def wide(values):
    return values.astype(jnp.float32)


def adamw(current, grad_in, moment_one, moment_two):
    one_new = BETA_ONE * moment_one + (1.0 - BETA_ONE) * grad_in
    two_new = BETA_TWO * moment_two + (1.0 - BETA_TWO) * grad_in * grad_in
    one_hat = one_new / (1.0 - BETA_ONE**STEP)
    two_hat = two_new / (1.0 - BETA_TWO**STEP)
    updated = current * (1.0 - LR_ADAM * DECAY) - LR_ADAM * one_hat / (jnp.sqrt(two_hat) + 1e-08)
    return (one_new, two_new, updated)


def columns_of(values, member, width, axis):
    return lax.dynamic_slice_in_dim(values, member * width, width, axis)


def fence(*values):
    return lax.optimization_barrier(values)


def body(
    history,
    out_grad,
    doc_lengths,
    doc_domain,
    domain_weight,
    attn_weight,
    attn_master,
    attn_moment,
    mlp_weight,
    mlp_master,
    mlp_moment,
    params,
    params_m,
    params_v,
    mix_out,
    mix_out_m,
    mix_out_v,
):
    hist_count, tok_count, model_width = history.shape
    links = Links()
    members, depth, member = links.members, links.depth, links.member
    rows = attn_weight.shape[1]
    group = lax.axis_size("dp")
    attn_cols = attn_weight.shape[2] // group
    mlp_cols = mlp_weight.shape[2] // group
    col_blocks = attn_cols // rows
    group_tok = group * tok_count
    near_tok = group_tok // 2
    half_width = model_width // 2
    param_rows = params.shape[0]

    slots = jnp.stack(links.slots()).astype(jnp.int32)
    plain = links.slots_of(0, members)

    def scatter_z(summed, turns):
        return [links.swap_z(summed[turn * rows : (turn + 1) * rows], turn) for turn in turns]

    def spread(left_side, right_side):
        return product_rows(left_side, right_side, plain, rows, jnp.bfloat16)

    up_own = columns_of(mlp_weight[0], member, mlp_cols, 1)
    param_pieces = lax.all_to_all(
        jnp.broadcast_to(low(params)[None], (members, param_rows, rows)), "fsdp", 0, 0, tiled=True
    )
    up_line = links.hop(([up_own], [up_own]))
    far_up = links.swap_x(up_own)
    param_low = jnp.moveaxis(param_pieces, 0, 1).reshape(param_rows, model_width)
    tok_weight = token_weights(doc_lengths[0], doc_domain[0], domain_weight, tok_count)
    (cot_own,) = take_blocks([[low(wide(out_grad) * tok_weight[:, None])]], slots, rows)
    near_lengths = jnp.concatenate([doc_lengths, links.swap_y(doc_lengths)], 0)
    group_lengths = jnp.concatenate([near_lengths, links.swap_core(near_lengths)], 0)
    attn_own = columns_of(attn_weight, member, attn_cols, 2)
    attn_own = jnp.concatenate([attn_own[at] for at in range(4)], 1)
    mixing = wide(lax.optimization_barrier(low(mix_out)))
    up_line, far_up, attn_own, param_low, group_lengths, cot_own, mixing = fence(
        up_line, far_up, attn_own, param_low, group_lengths, cot_own, mixing
    )

    for _ in range(2, depth - 1):
        up_line = links.hop(up_line)
    far_attn = links.swap_x(attn_own)
    cot_near = jnp.concatenate([cot_own, links.swap_y(cot_own)], 0)
    *normed_own, kept, coef, inner, scale, stream_three = mix_forward(
        history, param_low[17:], mixing, wide(param_low[:8])
    )
    normed_own = take_blocks(
        [[normed_own[3], normed_own[2]], [normed_own[0], normed_own[1]]], slots, rows
    )
    down_own = columns_of(mlp_weight[1], member, mlp_cols, 1)
    (
        up_line, far_attn, attn_own, param_low, cot_near, normed_own, kept, coef, inner, scale,
        stream_three, down_own,
    ) = fence(
        up_line, far_attn, attn_own, param_low, cot_near, normed_own, kept, coef, inner, scale,
        stream_three, down_own,
    )
    param_vals = wide(param_low)

    up_line = links.hop(up_line)
    down_line = links.hop(([down_own], [down_own]))
    far_second = links.swap_x(jnp.concatenate([down_own, links.near(up_line, 1)], 0))
    first_y = links.swap_y(normed_own[0])
    cot_core = links.swap_core(cot_near)
    up_line, down_line, far_second, first_y, cot_core, cot_near, normed_own = fence(
        up_line, down_line, far_second, first_y, cot_core, cot_near, normed_own
    )
    far_down, far_up_one = cut(far_second, (rows, rows))

    for _ in range(2, depth):
        down_line = links.hop(down_line)
    up_near = [links.near(up_line, turn) for turn in range(depth)]
    far_third = links.swap_x(jnp.concatenate(up_near[2:], 0))
    first_core = links.swap_core(normed_own[0])
    first_far = links.swap_core(first_y)
    last_y = links.swap_y(normed_own[1])
    group_cot = jnp.concatenate([cot_near, cot_core], 0)
    attn_pair = jnp.concatenate([attn_own, far_attn], 0)
    down_line, far_third, first_core, first_far, last_y, attn_pair, up_near, group_cot = fence(
        down_line, far_third, first_core, first_far, last_y, attn_pair, up_near, group_cot
    )

    attn_line = links.hop(([attn_pair], [attn_pair]))
    down_near = [links.near(down_line, turn) for turn in range(depth)]
    far_fourth = links.swap_x(jnp.concatenate(down_near[1 : depth - 1], 0))
    first_parts = (normed_own[0], first_y, first_core, first_far)
    group_normed = [None] * 4
    group_normed[3] = jnp.concatenate([values[:tok_count] for values in first_parts], 0)
    full_up = jnp.concatenate(up_near + [far_up, far_up_one, far_third], 0)
    up_bias = lax.dynamic_index_in_dim(param_vals, 13 + member, 0)
    act_low, slope = mlp_up(group_normed[3], full_up, up_bias)
    down_sent = half_product([group_cot], [act_low], 1)
    attn_line, far_fourth, act_low, slope, down_sent, down_near, full_up = fence(
        attn_line, far_fourth, act_low, slope, down_sent, down_near, full_up
    )

    for _ in range(2, depth - 1):
        attn_line = links.hop(attn_line)
    far_last = links.swap_x(down_near[depth - 1])
    down_first = links.swap_x(down_sent[:rows])
    last_core = links.swap_core(normed_own[1])
    last_far = links.swap_core(last_y)
    group_normed[2] = jnp.concatenate([values[tok_count:] for values in first_parts], 0)
    attn_line, far_last, down_first, down_sent, last_core, last_far, group_normed = fence(
        attn_line, far_last, down_first, down_sent, last_core, last_far, group_normed
    )

    attn_line = links.hop(attn_line)
    down_rest = links.swap_x(down_sent[rows:])
    full_down = jnp.concatenate(down_near + [far_down, far_fourth, far_last], 0)
    up_grad, up_sum = mlp_back(group_cot, full_down, slope)
    up_sent = half_product([group_normed[3]], [up_grad], 1)
    last_parts = (normed_own[1], last_y, last_core, last_far)
    group_normed[0] = jnp.concatenate([values[:tok_count] for values in last_parts], 0)
    group_normed[1] = jnp.concatenate([values[tok_count:] for values in last_parts], 0)
    (cot_cols,) = take_blocks([[group_cot]], links.slots_of(member * col_blocks, col_blocks), rows)
    attn_near = [links.near(attn_line, turn) for turn in range(depth)]
    half_depth = depth // 2
    up_sent = cut(up_sent, (half_depth * rows, half_depth * rows))
    attn_near, down_rest, up_grad, up_sum, up_sent, full_down, cot_cols, group_normed = fence(
        attn_near, down_rest, up_grad, up_sum, up_sent, full_down, cot_cols, group_normed
    )

    up_first = links.swap_x(up_sent[0])
    full_attn = [
        jnp.concatenate(
            [
                values[side * rows : (side + 1) * rows, at * attn_cols : (at + 1) * attn_cols]
                for side in range(2)
                for values in attn_near
            ],
            0,
        )
        for at in range(4)
    ]
    order = [links.slots_of(links.partner(at) * col_blocks, col_blocks) for at in range(group)]
    context_sum = jnp.concatenate(
        product_rows(cot_cols, full_attn[3], jnp.concatenate(order), rows, jnp.float32), 0
    )
    context_sum = [context_sum[:, at * attn_cols : (at + 1) * attn_cols] for at in range(group)]
    sent = low(jnp.concatenate(context_sum[2:], 1))
    arrived = links.swap_core(turn_core(sent))
    context_y = links.swap_y(turn_y(low(context_sum[1] + wide(arrived[:, attn_cols:]))))
    context_grad = low(context_sum[0] + wide(arrived[:, :attn_cols]) + wide(context_y))
    down_summed = half_product(
        [group_cot], [act_low], 0, jnp.concatenate([down_first, down_rest], 0)
    )
    down_parts = scatter_z(down_summed, range(1, depth - 1))
    up_first, down_summed, down_parts, full_attn, context_grad, up_sent = fence(
        up_first, down_summed, down_parts, full_attn, context_grad, up_sent
    )

    up_rest = links.swap_x(up_sent[1])
    down_parts = [down_summed[:rows]] + down_parts + scatter_z(down_summed, [depth - 1])
    attn_bias = lax.dynamic_slice(param_vals, (8, member * attn_cols), (3, attn_cols))
    context_low, proj_grads, proj_sums = attention_inner(
        jnp.cumsum(group_lengths, 1),
        group_normed[:3],
        full_attn[:3],
        attn_bias,
        rope_rows(tok_count),
        context_grad,
    )
    two_sent = half_product(
        [group_normed[2], group_normed[0]], [proj_grads[2], proj_grads[0]], 1
    )
    three_near, three_sent = spread(up_grad, full_up)
    context_turned = turn_y(context_low)
    (
        up_rest, down_parts, context_low, context_turned, proj_grads, proj_sums, two_sent,
        three_near, three_sent,
    ) = fence(
        up_rest, down_parts, context_low, context_turned, proj_grads, proj_sums, two_sent,
        three_near, three_sent,
    )

    two_x = links.swap_x(two_sent)
    up_summed = half_product(
        [group_normed[3]], [up_grad], 0, jnp.concatenate([up_first, up_rest], 0)
    )
    up_parts = scatter_z(up_summed, range(1, depth - 1))
    context_near = jnp.concatenate([context_low, links.swap_y(context_turned)], 1)
    context_far = links.swap_core(turn_core(context_near))
    order = []
    for owner in links.slots():
        place = (owner // col_blocks) ^ member
        place = (place % 2) * 2 + place // 2
        order.append(place * col_blocks + owner % col_blocks)
    (group_context,) = take_blocks(
        [[jnp.concatenate([context_near, context_far], 1)]],
        jnp.stack(order).astype(jnp.int32),
        rows,
    )
    one_sent = half_product([group_normed[1], group_context], [proj_grads[1], cot_cols], 1)
    three_arrived = links.swap_core(three_sent)
    token_parts = [spread(proj_grads[at], full_attn[at]) for at in range(3)]
    two_x, up_summed, up_parts, group_context, one_sent, token_parts, three_arrived = fence(
        two_x, up_summed, up_parts, group_context, one_sent, token_parts, three_arrived
    )

    def across_y(near, arrived):
        summed = near + wide(arrived)
        return summed[:tok_count] + wide(links.swap_y(low(summed[tok_count:])))

    one_x = links.swap_x(one_sent)
    up_parts = [up_summed[:rows]] + up_parts + scatter_z(up_summed, [depth - 1])
    two_summed = half_product(
        [group_normed[2], group_normed[0]], [proj_grads[2], proj_grads[0]], 0, two_x
    )
    two_parts = scatter_z(two_summed, [1])
    back_three = across_y(three_near, three_arrived)
    token_arrived = [links.swap_core(far) for _, far in token_parts]
    back_two = across_y(token_parts[2][0], token_arrived[2])
    one_x, up_parts, two_summed, two_parts, back_three, back_two, token_arrived = fence(
        one_x, up_parts, two_summed, two_parts, back_three, back_two, token_arrived
    )

    two_parts = [two_summed[:rows]] + two_parts + scatter_z(two_summed, range(2, depth))
    mlp_grad, mlp_mom, mlp_gram = finish_gradient([up_parts, down_parts], mlp_moment)
    one_summed = half_product(
        [group_normed[1], group_context], [proj_grads[1], cot_cols], 0, one_x
    )
    one_parts = scatter_z(one_summed, [1])
    mlp_gram = links.sum_stack(mlp_gram)
    back_zero = across_y(token_parts[0][0], token_arrived[0])
    back_one = across_y(token_parts[1][0], token_arrived[1])
    two_parts, one_summed, one_parts, back_zero, back_one, mlp_mom, mlp_gram = fence(
        two_parts, one_summed, one_parts, back_zero, back_one, mlp_mom, mlp_gram
    )

    one_parts = [one_summed[:rows]] + one_parts + scatter_z(one_summed, range(2, depth))
    mlp_new, mlp_low = newton_update(
        mlp_gram, mlp_mom, mlp_master, LR_MUON * 0.2 * math.sqrt(FF)
    )
    mlp_across = links.swap_y(mlp_low)
    history_grad, sums, mix_weight_grad, mixing_grad = mix_backward(
        history,
        out_grad,
        tok_weight[:, None],
        [back_zero, back_one, back_two, back_three],
        kept,
        coef,
        inner,
        scale,
        param_low[17:],
        mixing,
        param_vals[:8],
    )
    one_parts, mlp_low, mlp_across, sums, mix_weight_grad, mixing_grad = fence(
        one_parts, mlp_low, mlp_across, sums, mix_weight_grad, mixing_grad
    )

    attn_parts = [
        [values[:, :attn_cols] for values in two_parts],
        [values[:, attn_cols:] for values in two_parts],
        [values[:, :attn_cols] for values in one_parts],
        [values[:, attn_cols:] for values in one_parts],
    ]
    attn_parts = [attn_parts[1], attn_parts[2], attn_parts[0], attn_parts[3]]
    attn_grad, attn_mom, attn_gram = finish_gradient(attn_parts, attn_moment)
    attn_gram = links.sum_stack(attn_gram)
    mlp_near, mlp_sent = product_rows(act_low, full_down, plain, rows, jnp.float32)
    attn_out = jnp.dot(group_context, full_attn[3], preferred_element_type=jnp.float32)

    def with_attn(part, addend):
        own = columns_of(part, member, attn_cols, 1) + addend
        return lax.dynamic_update_slice_in_dim(part, own, member * attn_cols, 1)

    out_sent = low(with_attn(mlp_sent, attn_out[near_tok:]))
    out_near = with_attn(mlp_near, attn_out[:near_tok])

    def placed(values, total):
        return lax.dynamic_update_slice_in_dim(
            jnp.zeros((values.shape[0], total), jnp.float32), values, member * values.shape[1], 1
        )

    param_grad = jnp.concatenate(
        [
            sums[:8],
            placed(proj_sums[:3], model_width),
            sums[8:9],
            sums[8:9],
            placed(up_sum, group * mlp_cols).reshape(-1, model_width),
            mix_weight_grad,
        ],
        0,
    )
    param_pieces_grad = jnp.moveaxis(param_grad.reshape(param_rows, members, rows), 1, 0)
    mix_size = mixing_grad.size
    mix_rows = -(-mix_size // rows)
    mix_flat = jnp.pad(mixing_grad.reshape(-1), (0, mix_rows * rows - mix_size))
    mix_flat = jnp.broadcast_to(mix_flat.reshape(1, mix_rows, rows), (members, mix_rows, rows))
    small_sent = jnp.concatenate([param_pieces_grad, mix_flat], 1)
    attn_gram, small_sent, attn_mom, out_sent, out_near = fence(
        attn_gram, small_sent, attn_mom, out_sent, out_near
    )

    attn_new, attn_low = newton_update(
        attn_gram, attn_mom, attn_master, LR_MUON * 0.2 * math.sqrt(model_width)
    )
    attn_copy = links.gather_copies(attn_low, links.swap_y(attn_low))
    out_own = across_y(out_near, links.swap_core(out_sent))
    layer_out = low(stream_three + out_own + (param_vals[11] + param_vals[12]))
    mlp_copy = links.gather_copies(mlp_low, mlp_across)
    small = lax.all_to_all(small_sent, "fsdp", 0, 0, tiled=True)
    small = links.sum_group(jnp.sum(small, 0))
    param_part = small[:param_rows]
    mixing_grad = small[param_rows:].reshape(-1)[:mix_size].reshape(mixing_grad.shape)
    params_m_new, params_v_new, params_new = adamw(params, param_part, params_m, params_v)
    mix_out_m_new, mix_out_v_new, mix_out_new = adamw(mix_out, mixing_grad, mix_out_m, mix_out_v)
    return (
        layer_out,
        history_grad,
        attn_grad,
        attn_mom,
        attn_new,
        attn_copy,
        mlp_grad,
        mlp_mom,
        mlp_new,
        mlp_copy,
        param_part,
        param_part[11:13],
        params_m_new,
        params_v_new,
        params_new,
        mixing_grad,
        mix_out_m_new,
        mix_out_v_new,
        mix_out_new,
    )


def solution(mesh):
    in_specs = (
        P(None, ("dp", "fsdp"), None),
        P(("dp", "fsdp"), None),
        P(("dp", "fsdp"), None),
        P(("dp", "fsdp"), None),
        P(),
        P(None, "fsdp", None),
        P(None, "fsdp", "dp"),
        P(None, "fsdp", "dp"),
        P(None, "fsdp", None),
        P(None, "fsdp", "dp"),
        P(None, "fsdp", "dp"),
        P(None, "fsdp"),
        P(None, "fsdp"),
        P(None, "fsdp"),
        P(),
        P(),
        P(),
    )
    out_specs = (
        P(("dp", "fsdp"), None),
        P(None, ("dp", "fsdp"), None),
        P(None, "fsdp", "dp"),
        P(None, "fsdp", "dp"),
        P(None, "fsdp", "dp"),
        P(None, "fsdp", None),
        P(None, "fsdp", "dp"),
        P(None, "fsdp", "dp"),
        P(None, "fsdp", "dp"),
        P(None, "fsdp", None),
        P(None, "fsdp"),
        P(None, "fsdp"),
        P(None, "fsdp"),
        P(None, "fsdp"),
        P(None, "fsdp"),
        P(),
        P(),
        P(),
        P(),
    )
    return jax.shard_map(body, mesh=mesh, in_specs=in_specs, out_specs=out_specs, check_vma=False)
```

time: 4790 us -> 1040 us (0.22)
  waiting for transfers between devices: 3800 us -> 366 us
  matrix products: 627 us -> 4.75 us
  Pallas kernels: 0 us -> 320 us
  blocking collectives: 122 us -> 0 us
  starting transfers between devices: 0.89 us -> 116 us
    all_gather x4 -> x0, waiting for transfers between devices: 1700 us -> none  [the longest x1 1150 us: body(): lax.all_gather(mlp_weight, 'fsdp', axis=1, tiled=True)]
    reduce_scatter x11 -> x0, waiting for transfers between devices: 1140 us -> none  [the longest x4 393 us: body(): lax.psum_scatter(col_term(lefts[member], rights[member]), 'dp', scatter_d...]
    unnamed x24 -> x0, waiting for transfers between devices: 893 us -> none
    dot_general x69 -> x1, matrix products: 627 us -> 4.75 us  [body(): jnp.dot(group_context, full_attn[3], preferred_element_type=jnp.float32)]
    ppermute x0 -> x80, waiting for transfers between devices: none -> 362 us  [the longest x16 138 us: swap_y(): return lax.ppermute(values, 'dp', [(at, at ^ 2) for at in range(4)])]
    pallas_call x0 -> x27, Pallas kernels: none -> 320 us  [the longest x8 70.7 us: half_product(): pl.pallas_call(grad_kernel, grid=(steps, columns // col_tile), in_specs=[...]
    ppermute x0 -> x80, starting transfers between devices: none -> 109 us  [the longest x22 30.6 us: swap_core(): return lax.ppermute(values, 'dp', [(at, at ^ 1) for at in range(4)])]
    psum x5 -> x0, waiting for transfers between devices: 68.7 us -> none  [body(): attn_gram, mlp_gram = lax.psum((gram_of(attn_cur), gram_of(mlp_cur)), 'dp')]
  transfers between devices with their start and end apart: 22 -> 82, of which waited for: 20 -> 29; matrix products, arithmetic and copies ran while one was open for 15% -> 17% of each run, Pallas kernels for 0% -> 27%
where the time goes in v3:
time: 1040 us; the launch traced here: 1030 us
  waiting for transfers between devices  366 us (35%)
  Pallas kernels  320 us (31%)
  starting transfers between devices  116 us (11%)
  local copies, waits for them, and re-layouts  110 us (11%)
  other arithmetic  106 us (10%)
    ppermute x16, waiting for transfers between devices, swap_y(): return lax.ppermute(values, 'dp', [(at, at ^ 2) for at in range(4)])  138 us
    ppermute x12, waiting for transfers between devices, swap_z(): return lax.ppermute(values, 'fsdp', pairs)  93.1 us
    ppermute x9, waiting for transfers between devices, hop(): lax.ppermute(fall[-1], 'fsdp', down_pairs)  79 us
    pallas_call x8, Pallas kernels, half_product(): pl.pallas_call(grad_kernel, grid=(steps, columns // col_tile), in_specs=[...  70.7 us
    pallas_call x6, Pallas kernels, product_rows(): pl.pallas_call(rows_kernel, grid_spec=pltpu.PrefetchScalarGridSpec(num_sc...  56.4 us
    ppermute x12, waiting for transfers between devices, swap_x(): lax.ppermute(values, 'fsdp', [(at, at ^ 1) for at in range(self.members)])  48.5 us
    unnamed x206, local copies, waits for them, and re-layouts  42.8 us
    pallas_call x2, Pallas kernels, newton_update(): pl.pallas_call(functools.partial(newton_kernel, rate=rate), grid=(count /...  41.7 us
  transfers between devices with their start and end apart: 82, of which 29 were waited for; matrix products, arithmetic and copies ran while one was open for 17% of the time, Pallas kernels for 27%

profile of v3, /device:TPU:1, one launch (start us, length us, event | category | flops | bytes accessed | tf_op | source)
XLA Modules:
  0.0 1026.5 jit_solution(1669149430598691718)
XLA Ops:
  47.9 18.4 %mix_forward.1 = (bf16[256,2048]{1,0:T(8,128)(2,1)}, bf16[256,2048]{1,0:T(8,128)(2,1)}, bf16[256,2048]{1,0:T(8,128)(2,1)}, bf16[256,2048]{1,0:T(8,128)(2,1)}, f3...) custom-call(bf16[9,256,2048]{2,1,0:T(8,128)(2,1)} %hist_ref.3, ...), custom_call_target="tpu_custom_call" | custom-call | flops 1 | bytes 1 | tf_op jit(solution)/shard_map/mix_forward/pallas_call | solution.py:288
  87.1 14.8 %collective-permute-done.10 = bf16[256,2048]{1,0:T(8,128)(2,1)S(1)} collective-permute-done((bf16[256,2048]{1,0:T(8,128)(2,1)}, bf16[256,2048]{1,0:T(8,128)(2,1)S(1)}, u32[]{:S(2)}, u32[]{:S(2)}) %collective-permute-start.10) | collective-permute-done | bytes 1048608 | tf_op jit(solution)/shard_map/ppermute | solution.py:726
  105.7 18.5 %collective-permute-done.12 = bf16[256,2048]{1,0:T(8,128)(2,1)} collective-permute-done((bf16[256,2048]{1,0:T(8,128)(2,1)S(1)}, bf16[256,2048]{1,0:T(8,128)(2,1)}, u32[]{:S(2)}, u32[]{:S(2)}) %collective-permute-start.12) | collective-permute-done | bytes 1048608 | tf_op jit(solution)/shard_map/ppermute | solution.py:726
  143.0 22.9 %collective-permute-done.18 = bf16[256,2048]{1,0:T(8,128)(2,1)S(1)} collective-permute-done((bf16[256,2048]{1,0:T(8,128)(2,1)}, bf16[256,2048]{1,0:T(8,128)(2,1)S(1)}, u32[]{:S(2)}, u32[]{:S(2)}) %collective-permute-start.18) | collective-permute-done | bytes 1048608 | tf_op jit(solution)/shard_map/ppermute | solution.py:726
  228.6 17.4 %mlp_up.1 = (bf16[1024,2048]{1,0:T(8,128)(2,1)}, f32[1024,2048]{1,0:T(8,128)}) custom-call(bf16[1024,2048]{1,0:T(8,128)(2,1)} %pad_maximum_fusion.2.normed_ref.left_refs_0_, bf16[2048,2048]{1,0:T(8,128)(2,1)} %constant_dynamic-update-slice_fusion.up_ref.even_ref.odd_ref, f32[1,2048]{1,0:T(1,128)} %get-tuple-element.577.bias_ref), custom_call_target="tpu_custom_call" | custom-call | flops 1 | bytes 1 | tf_op jit(solution)/shard_map/mlp_up/pallas_call | solution.py:457
  278.5 13.5 %collective-permute-done.30 = bf16[256,2048]{1,0:T(8,128)(2,1)S(1)} collective-permute-done((bf16[256,2048]{1,0:T(8,128)(2,1)S(1)}, bf16[256,2048]{1,0:T(8,128)(2,1)S(1)}, u32[]{:S(2)}, u32[]{:S(2)}) %collective-permute-start.30) | collective-permute-done | bytes 1048608 | tf_op jit(solution)/shard_map/ppermute | solution.py:700
  292.1 22.5 %collective-permute-done.29 = bf16[256,2048]{1,0:T(8,128)(2,1)S(1)} collective-permute-done((bf16[256,2048]{1,0:T(8,128)(2,1)S(1)}, bf16[256,2048]{1,0:T(8,128)(2,1)S(1)}, u32[]{:S(2)}, u32[]{:S(2)}) %collective-permute-start.29) | collective-permute-done | bytes 1048608 | tf_op jit(solution)/shard_map/ppermute | solution.py:700
  326.5 16.0 %mlp_back.1 = (bf16[1024,2048]{1,0:T(8,128)(2,1)}, f32[1,2048]{1,0:T(1,128)}) custom-call(bf16[1024,2048]{1,0:T(8,128)(2,1)} %pad_maximum_fusion.1.left_refs_0_.cot_ref.refs_0_, bf16[2048,2048]{1,0:T(8,128)(2,1)} %constant_dynamic-update-slice_fusion.6.down_ref.even_ref.odd_ref, f32[1024,2048]{1,0:T(8,128)} %get-tuple-element.318.slope_ref), custom_call_target="tpu_custom_call" | custom-call | flops 1 | bytes 1 | tf_op jit(solution)/shard_map/mlp_back/pallas_call | solution.py:493
  437.9 15.7 %collective-permute-done.40 = bf16[1024,512]{1,0:T(8,128)(2,1)S(1)} collective-permute-done((bf16[1024,512]{1,0:T(8,128)(2,1)S(1)}, bf16[1024,512]{1,0:T(8,128)(2,1)S(1)}, u32[]{:S(2)}, u32[]{:S(2)}) %collective-permute-start.40) | collective-permute-done | bytes 1048608 | tf_op jit(solution)/shard_map/ppermute | solution.py:697
  456.6 27.2 %collective-permute-done.38.part_refs_1__2_ = bf16[256,2048]{1,0:T(8,128)(2,1)S(1)} collective-permute-done((bf16[256,2048]{1,0:T(8,128)(2,1)S(1)}, bf16[256,2048]{1,0:T(8,128)(2,1)S(1)}, u32[]{:S(2)}, u32[]{:S(2)}) %collective-permute-start.38) | collective-permute-done | bytes 1048608 | tf_op jit(solution)/shard_map/ppermute | solution.py:704
  493.0 14.2 %product_rows.7 = (f32[512,2048]{1,0:T(8,128)}, bf16[512,2048]{1,0:T(8,128)(2,1)}) custom-call(s32[8]{0:T(128)} %stack.152.order_ref, bf16[1024,2048]{1,0:T(8,128)(2,1)} %get-tuple-element.354.right_refs_0_.left_ref, bf16[2048,2048]{1,0:T(8,128)(2,1)} %constant_dynamic-update-slice_fusion.up_ref.even_ref.odd_ref, ...), custom_call_target="tpu_custom_call" | custom-call | flops 1 | bytes 1 | tf_op jit(solution)/shard_map/product_rows/pallas_call | solution.py:189
  507.2 27.2 %attention_inner.1 = (bf16[1024,512]{1,0:T(8,128)(2,1)}, bf16[1024,512]{1,0:T(8,128)(2,1)}, bf16[1024,512]{1,0:T(8,128)(2,1)}, bf16[1024,512]{1,0:T(8,128)(2,1)}, f32[8,512]{1,0:T(8,128)}) custom-call(s32[4,3]{1,0:T(4,128)} %reduce_window_sum.18.ends_ref, bf16[1024,2048]{1,0:T(8,128)(2,1)} %pad_maximum_fusion.4.normed_refs_0_.left_refs_1_, ...), custom_call_target="tpu_custom_call" | custom-call | flops 1 | bytes 1 | tf_op jit(solution)/shard_map/attention_inner/pallas_call | solution.py:580
  540.7 22.6 %collective-permute-done.46 = bf16[1024,512]{1,0:T(8,128)(2,1)S(1)} collective-permute-done((bf16[1024,512]{1,0:T(8,128)(2,1)S(1)}, bf16[1024,512]{1,0:T(8,128)(2,1)S(1)}, u32[]{:S(2)}, u32[]{:S(2)}) %collective-permute-start.46) | collective-permute-done | bytes 1048608 | tf_op jit(solution)/shard_map/ppermute | solution.py:697
  656.2 17.8 %collective-permute-done.52 = bf16[256,2048]{1,0:T(8,128)(2,1)S(1)} collective-permute-done((bf16[256,2048]{1,0:T(8,128)(2,1)S(1)}, bf16[256,2048]{1,0:T(8,128)(2,1)S(1)}, u32[]{:S(2)}, u32[]{:S(2)}) %collective-permute-start.52) | collective-permute-done | bytes 1048608 | tf_op jit(solution)/shard_map/ppermute | solution.py:697
  678.0 18.5 %collective-permute-done.54 = bf16[256,2048]{1,0:T(8,128)(2,1)S(1)} collective-permute-done((bf16[256,2048]{1,0:T(8,128)(2,1)S(1)}, bf16[256,2048]{1,0:T(8,128)(2,1)S(1)}, u32[]{:S(2)}, u32[]{:S(2)}) %collective-permute-start.54) | collective-permute-done | bytes 1048608 | tf_op jit(solution)/shard_map/ppermute | solution.py:697
  698.8 13.3 %collective-permute-done.51 = bf16[256,1024]{1,0:T(8,128)(2,1)S(1)} collective-permute-done((bf16[256,1024]{1,0:T(8,128)(2,1)S(1)}, bf16[256,1024]{1,0:T(8,128)(2,1)S(1)}, u32[]{:S(2)}, u32[]{:S(2)}) %collective-permute-start.51) | collective-permute-done | bytes 524320 | tf_op jit(solution)/shard_map/ppermute | solution.py:704
  735.7 23.2 %collective-permute-done.63 = f32[1,256,256]{2,1,0:T(8,128)S(1)} collective-permute-done((f32[1,256,256]{2,1,0:T(8,128)S(1)}, f32[1,256,256]{2,1,0:T(8,128)S(1)}, u32[]{:S(2)}, u32[]{:S(2)}) %collective-permute-start.63) | collective-permute-done | bytes 262176 | tf_op jit(solution)/shard_map/ppermute | solution.py:697
  804.4 22.5 %collective-permute-done.57 = bf16[256,1024]{1,0:T(8,128)(2,1)S(1)} collective-permute-done((bf16[256,1024]{1,0:T(8,128)(2,1)}, bf16[256,1024]{1,0:T(8,128)(2,1)S(1)}, u32[]{:S(2)}, u32[]{:S(2)}) %collective-permute-start.57) | collective-permute-done | bytes 524320 | tf_op jit(solution)/shard_map/ppermute | solution.py:704
  827.6 19.1 %newton_update.2 = (f32[2,256,2048]{2,1,0:T(8,128)}, bf16[2,256,2048]{2,1,0:T(8,128)(2,1)}) custom-call(f32[2,256,256]{2,1,0:T(8,128)} %pad_maximum_fusion.21.gram_ref, f32[2,256,2048]{2,1,0:T(8,128)} %get-tuple-element.223.mom_ref, f32[2,256,2048]{2,1,0:T(8,128)} %master_ref.2), custom_call_target="tpu_custom_call" | custom-call | flops 1 | bytes 1 | tf_op jit(solution)/shard_map/newton_update/pallas_call | solution.py:668
  852.3 32.6 %mix_backward.1 = (bf16[9,256,2048]{2,1,0:T(8,128)(2,1)}, f32[16,2048]{1,0:T(8,128)}, f32[36,2048]{1,0:T(8,128)}, f32[37,36]{1,0:T(8,128)}) custom-call(bf16[9,256,2048]{2,1,0:T(8,128)(2,1)} %hist_ref.3, bf16[256,2048]{1,0:T(8,128)(2,1)} %cot_ref.1, f32[256,1]{1,0:T(8,128)} %copy.51.tok_ref, f32[256,2048]{1,0:T(8,128)} %slice_add_fusion.2.back_refs_0_, ...), custom_call_target="tpu_custom_call" | custom-call | flops 1 | bytes 1 | tf_op jit(solution)/shard_map/mix_backward/pallas_call | solution.py:403
  911.1 14.3 %product_rows.11 = (f32[512,2048]{1,0:T(8,128)}, f32[512,2048]{1,0:T(8,128)}) custom-call(s32[8]{0:T(128)} %stack.152.order_ref, bf16[1024,2048]{1,0:T(8,128)(2,1)} %get-tuple-element.326.right_refs_0_.left_ref, bf16[2048,2048]{1,0:T(8,128)(2,1)} %constant_dynamic-update-slice_fusion.6.down_ref.even_ref.odd_ref, ...), custom_call_target="tpu_custom_call" | custom-call | flops 1 | bytes 1 | tf_op jit(solution)/shard_map/product_rows/pallas_call | solution.py:189
  944.9 22.6 %newton_update.3 = (f32[4,256,512]{2,1,0:T(8,128)}, bf16[4,256,512]{2,1,0:T(8,128)(2,1)}) custom-call(f32[4,256,256]{2,1,0:T(8,128)} %pad_maximum_fusion.20.gram_ref, f32[4,256,512]{2,1,0:T(8,128)} %get-tuple-element.219.mom_ref, f32[4,256,512]{2,1,0:T(8,128)} %master_ref.3), custom_call_target="tpu_custom_call" | custom-call | flops 1 | bytes 1 | tf_op jit(solution)/shard_map/newton_update/pallas_call | solution.py:668
  977.4 16.0 %collective-permute-done.79 = f32[59,256]{1,0:T(8,128)S(1)} collective-permute-done((f32[59,256]{1,0:T(8,128)S(1)}, f32[59,256]{1,0:T(8,128)S(1)}, u32[]{:S(2)}, u32[]{:S(2)}) %collective-permute-start.79) | collective-permute-done | bytes 60448 | tf_op jit(solution)/shard_map/ppermute | solution.py:697
  1005.3 19.4 %collective-permute-done.72 = bf16[256,2048]{1,0:T(8,128)(2,1)S(1)} collective-permute-done((bf16[256,2048]{1,0:T(8,128)(2,1)S(1)}, bf16[256,2048]{1,0:T(8,128)(2,1)S(1)}, u32[]{:S(2)}, u32[]{:S(2)}) %collective-permute-start.72) | collective-permute-done | bytes 1048608 | tf_op jit(solution)/shard_map/ppermute | solution.py:697
  (533 shorter events, 553.9 us)
Async XLA Ops:
  132.7 47.2 %collective-permute-start.23 = (bf16[512,2048]{1,0:T(8,128)(2,1)}, bf16[512,2048]{1,0:T(8,128)(2,1)}, u32[]{:S(2)}, u32[]{:S(2)}) collective-permute-start(bf16[512,2048]{1,0:T(8,128)(2,1)} %get-tuple-element.274), channel_id=1, source_target_pairs={{0,16},{8,24},{16,0},{24,8},{1,17},{9,25},{17,1},{25,9},{2,18},{10... | collective-permute-start | bytes 6291464 | tf_op jit(solution)/shard_map/ppermute | solution.py:697
  135.7 46.5 %collective-permute-start.20 = (bf16[512,2048]{1,0:T(8,128)(2,1)S(1)}, bf16[512,2048]{1,0:T(8,128)(2,1)S(1)}, u32[]{:S(2)}, u32[]{:S(2)}) collective-permute-start(bf16[512,2048]{1,0:T(8,128)(2,1)S(1)} %pad_maximum_fusion.12), channel_id=1, source_target_pairs={{0,1},{1,0},{2,3},{3,2},{4,5},{5,4},{6,7},{7,6},{8,9},{9,8},{10,11... | collective-permute-start | bytes 6291464 | tf_op jit(solution)/shard_map/ppermute | solution.py:700
  175.4 95.2 %collective-permute-start.31 = (bf16[512,2048]{1,0:T(8,128)(2,1)}, bf16[512,2048]{1,0:T(8,128)(2,1)}, u32[]{:S(2)}, u32[]{:S(2)}) collective-permute-start(bf16[512,2048]{1,0:T(8,128)(2,1)} %get-tuple-element.274), channel_id=1, source_target_pairs={{0,8},{8,0},{16,24},{24,16},{1,9},{9,1},{17,25},{25,17},{2,10},{10... | collective-permute-start | bytes 6291464 | tf_op jit(solution)/shard_map/ppermute | solution.py:694
  192.8 66.9 %collective-permute-start.25 = (bf16[512,2048]{1,0:T(8,128)(2,1)S(1)}, bf16[512,2048]{1,0:T(8,128)(2,1)}, u32[]{:S(2)}, u32[]{:S(2)}) collective-permute-start(bf16[512,2048]{1,0:T(8,128)(2,1)S(1)} %pad_maximum_fusion.13), channel_id=1, source_target_pairs={{2,0},{3,1},{4,2},{5,3},{6,4},{7,5},{10,8},{11,9},{12,10},{13,11},... | collective-permute-start | bytes 6291464 | tf_op jit(solution)/shard_map/ppermute | solution.py:726
  194.1 65.6 %collective-permute-start.24 = (bf16[512,2048]{1,0:T(8,128)(2,1)S(1)}, bf16[512,2048]{1,0:T(8,128)(2,1)}, u32[]{:S(2)}, u32[]{:S(2)}) collective-permute-start(bf16[512,2048]{1,0:T(8,128)(2,1)S(1)} %pad_maximum_fusion.13), channel_id=1, source_target_pairs={{0,2},{1,3},{2,4},{3,5},{4,6},{5,7},{8,10},{9,11},{10,12},{11,13},... | collective-permute-start | bytes 6291464 | tf_op jit(solution)/shard_map/ppermute | solution.py:725
  205.4 54.3 %collective-permute-start.26 = (bf16[512,2048]{1,0:T(8,128)(2,1)}, bf16[512,2048]{1,0:T(8,128)(2,1)}, u32[]{:S(2)}, u32[]{:S(2)}) collective-permute-start(bf16[512,2048]{1,0:T(8,128)(2,1)} %pad_maximum_fusion.14), channel_id=1, source_target_pairs={{0,1},{1,0},{2,3},{3,2},{4,5},{5,4},{6,7},{7,6},{8,9},{9,8},{10,11... | collective-permute-start | bytes 6291464 | tf_op jit(solution)/shard_map/ppermute | solution.py:700
  205.6 72.9 %collective-permute-start.32 = (bf16[512,2048]{1,0:T(8,128)(2,1)}, bf16[512,2048]{1,0:T(8,128)(2,1)}, u32[]{:S(2)}, u32[]{:S(2)}) collective-permute-start(bf16[512,2048]{1,0:T(8,128)(2,1)} %collective-permute-done.23), channel_id=1, source_target_pairs={{0,8},{8,0},{16,24},{24,16},{1,9},{9,1},{17,25},{25,17},{2,10},{10... | collective-permute-start | bytes 6291464 | tf_op jit(solution)/shard_map/ppermute | solution.py:694
  259.7 54.9 %collective-permute-start.27 = (bf16[512,2048]{1,0:T(8,128)(2,1)}, bf16[512,2048]{1,0:T(8,128)(2,1)}, u32[]{:S(2)}, u32[]{:S(2)}) collective-permute-start(bf16[512,2048]{1,0:T(8,128)(2,1)} %collective-permute-done.24), channel_id=1, source_target_pairs={{2,4},{3,5},{4,6},{5,7},{10,12},{11,13},{12,14},{13,15},{18,20},{1... | collective-permute-start | bytes 6291464 | tf_op jit(solution)/shard_map/ppermute | solution.py:725
  261.7 53.6 %collective-permute-start.28 = (bf16[512,2048]{1,0:T(8,128)(2,1)}, bf16[512,2048]{1,0:T(8,128)(2,1)}, u32[]{:S(2)}, u32[]{:S(2)}) collective-permute-start(bf16[512,2048]{1,0:T(8,128)(2,1)} %collective-permute-done.25), channel_id=1, source_target_pairs={{2,0},{3,1},{4,2},{5,3},{10,8},{11,9},{12,10},{13,11},{18,16},{19,... | collective-permute-start | bytes 6291464 | tf_op jit(solution)/shard_map/ppermute | solution.py:726
  319.2 69.2 %collective-permute-start.35 = (bf16[768,2048]{1,0:T(8,128)(2,1)}, bf16[768,2048]{1,0:T(8,128)(2,1)}, u32[]{:S(2)}, u32[]{:S(2)}) collective-permute-start(bf16[768,2048]{1,0:T(8,128)(2,1)} %slice.430), channel_id=1, source_target_pairs={{0,1},{1,0},{2,3},{3,2},{4,5},{5,4},{6,7},{7,6},{8,9},{9,8},{10,11... | collective-permute-start | bytes 9437192 | tf_op jit(solution)/shard_map/ppermute | solution.py:700
  324.1 50.9 %collective-permute-start.34 = (bf16[512,2048]{1,0:T(8,128)(2,1)}, bf16[512,2048]{1,0:T(8,128)(2,1)}, u32[]{:S(2)}, u32[]{:S(2)}) collective-permute-start(bf16[512,2048]{1,0:T(8,128)(2,1)} %collective-permute-done.28), channel_id=1, source_target_pairs={{2,0},{3,1},{10,8},{11,9},{18,16},{19,17},{26,24},{27,25}} | collective-permute-start | bytes 6291464 | tf_op jit(solution)/shard_map/ppermute | solution.py:726
  409.7 74.1 %collective-permute-start.36 = (bf16[512,2048]{1,0:T(8,128)(2,1)}, bf16[512,2048]{1,0:T(8,128)(2,1)}, u32[]{:S(2)}, u32[]{:S(2)}) collective-permute-start(bf16[512,2048]{1,0:T(8,128)(2,1)} %get-tuple-element.325), channel_id=1, source_target_pairs={{0,1},{1,0},{2,3},{3,2},{4,5},{5,4},{6,7},{7,6},{8,9},{9,8},{10,11... | collective-permute-start | bytes 6291464 | tf_op jit(solution)/shard_map/ppermute | solution.py:700
  431.3 52.5 %collective-permute-start.38 = (bf16[256,2048]{1,0:T(8,128)(2,1)S(1)}, bf16[256,2048]{1,0:T(8,128)(2,1)S(1)}, u32[]{:S(2)}, u32[]{:S(2)}) collective-permute-start(bf16[256,2048]{1,0:T(8,128)(2,1)S(1)} %get-tuple-element.476), channel_id=1, source_target_pairs={{0,4},{1,5},{2,6},{3,7},{4,0},{5,1},{6,2},{7,3},{8,12},{9,13},{10,... | collective-permute-start | bytes 3145736 | tf_op jit(solution)/shard_map/ppermute | solution.py:704
  485.1 55.3 %collective-permute-start.41 = (bf16[512,2048]{1,0:T(8,128)(2,1)S(1)}, bf16[512,2048]{1,0:T(8,128)(2,1)}, u32[]{:S(2)}, u32[]{:S(2)}) collective-permute-start(bf16[512,2048]{1,0:T(8,128)(2,1)S(1)} %copy-done.47), channel_id=1, source_target_pairs={{0,1},{1,0},{2,3},{3,2},{4,5},{5,4},{6,7},{7,6},{8,9},{9,8},{10,11... | collective-permute-start | bytes 6291464 | tf_op jit(solution)/shard_map/ppermute | solution.py:700
  489.9 50.5 %collective-permute-start.42 = (bf16[256,2048]{1,0:T(8,128)(2,1)}, bf16[256,2048]{1,0:T(8,128)(2,1)}, u32[]{:S(2)}, u32[]{:S(2)}) collective-permute-start(bf16[256,2048]{1,0:T(8,128)(2,1)} %get-tuple-element.472), channel_id=1, source_target_pairs={{0,6},{1,7},{2,4},{3,5},{4,2},{5,3},{6,0},{7,1},{8,14},{9,15},{10,... | collective-permute-start | bytes 3145736 | tf_op jit(solution)/shard_map/ppermute | solution.py:704
  567.9 69.3 %collective-permute-start.43 = (bf16[1024,1024]{1,0:T(8,128)(2,1)}, bf16[1024,1024]{1,0:T(8,128)(2,1)}, u32[]{:S(2)}, u32[]{:S(2)}) collective-permute-start(bf16[1024,1024]{1,0:T(8,128)(2,1)} %half_product.11), channel_id=1, source_target_pairs={{0,1},{1,0},{2,3},{3,2},{4,5},{5,4},{6,7},{7,6},{8,9},{9,8},{10,11... | collective-permute-start | bytes 6291464 | tf_op jit(solution)/shard_map/ppermute | solution.py:700
  569.2 68.0 %collective-permute-start.48 = (bf16[512,2048]{1,0:T(8,128)(2,1)}, bf16[512,2048]{1,0:T(8,128)(2,1)}, u32[]{:S(2)}, u32[]{:S(2)}) collective-permute-start(bf16[512,2048]{1,0:T(8,128)(2,1)} %get-tuple-element.373), channel_id=1, source_target_pairs={{0,8},{8,0},{16,24},{24,16},{1,9},{9,1},{17,25},{25,17},{2,10},{10... | collective-permute-start | bytes 6291464 | tf_op jit(solution)/shard_map/ppermute | solution.py:694
  589.0 48.2 %collective-permute-start.45 = (bf16[256,2048]{1,0:T(8,128)(2,1)}, bf16[256,2048]{1,0:T(8,128)(2,1)S(1)}, u32[]{:S(2)}, u32[]{:S(2)}) collective-permute-start(bf16[256,2048]{1,0:T(8,128)(2,1)} %get-tuple-element.470), channel_id=1, source_target_pairs={{0,4},{1,5},{2,6},{3,7},{4,0},{5,1},{6,2},{7,3},{8,12},{9,13},{10,... | collective-permute-start | bytes 3145736 | tf_op jit(solution)/shard_map/ppermute | solution.py:704
  651.3 60.8 %collective-permute-start.49 = (bf16[1024,1024]{1,0:T(8,128)(2,1)S(1)}, bf16[1024,1024]{1,0:T(8,128)(2,1)S(1)}, u32[]{:S(2)}, u32[]{:S(2)}) collective-permute-start(bf16[1024,1024]{1,0:T(8,128)(2,1)S(1)} %copy-done.48), channel_id=1, source_target_pairs={{0,1},{1,0},{2,3},{3,2},{4,5},{5,4},{6,7},{7,6},{8,9},{9,8},{10,11... | collective-permute-start | bytes 6291464 | tf_op jit(solution)/shard_map/ppermute | solution.py:700
  651.5 60.7 %collective-permute-start.55 = (bf16[512,2048]{1,0:T(8,128)(2,1)S(1)}, bf16[512,2048]{1,0:T(8,128)(2,1)}, u32[]{:S(2)}, u32[]{:S(2)}) collective-permute-start(bf16[512,2048]{1,0:T(8,128)(2,1)S(1)} %copy-done.89), channel_id=1, source_target_pairs={{0,8},{8,0},{16,24},{24,16},{1,9},{9,1},{17,25},{25,17},{2,10},{10... | collective-permute-start | bytes 6291464 | tf_op jit(solution)/shard_map/ppermute | solution.py:694
  651.9 60.3 %collective-permute-start.56 = (bf16[512,2048]{1,0:T(8,128)(2,1)S(1)}, bf16[512,2048]{1,0:T(8,128)(2,1)}, u32[]{:S(2)}, u32[]{:S(2)}) collective-permute-start(bf16[512,2048]{1,0:T(8,128)(2,1)S(1)} %copy-done.90), channel_id=1, source_target_pairs={{0,8},{8,0},{16,24},{24,16},{1,9},{9,1},{17,25},{25,17},{2,10},{10... | collective-permute-start | bytes 6291464 | tf_op jit(solution)/shard_map/ppermute | solution.py:694
  728.3 55.3 %collective-permute-start.61 = (bf16[256,2048]{1,0:T(8,128)(2,1)}, bf16[256,2048]{1,0:T(8,128)(2,1)S(1)}, u32[]{:S(2)}, u32[]{:S(2)}) collective-permute-start(bf16[256,2048]{1,0:T(8,128)(2,1)} %slice.656), channel_id=1, source_target_pairs={{0,16},{8,24},{16,0},{24,8},{1,17},{9,25},{17,1},{25,9},{2,18},{10... | collective-permute-start | bytes 3145736 | tf_op jit(solution)/shard_map/ppermute | solution.py:697
  735.5 49.7 %collective-permute-start.60 = (bf16[256,2048]{1,0:T(8,128)(2,1)}, bf16[256,2048]{1,0:T(8,128)(2,1)S(1)}, u32[]{:S(2)}, u32[]{:S(2)}) collective-permute-start(bf16[256,2048]{1,0:T(8,128)(2,1)} %slice.657), channel_id=1, source_target_pairs={{0,16},{8,24},{16,0},{24,8},{1,17},{9,25},{17,1},{25,9},{2,18},{10... | collective-permute-start | bytes 3145736 | tf_op jit(solution)/shard_map/ppermute | solution.py:697
  846.7 47.0 %collective-permute-start.67 = (bf16[2,256,2048]{2,1,0:T(8,128)(2,1)}, bf16[2,256,2048]{2,1,0:T(8,128)(2,1)}, u32[]{:S(2)}, u32[]{:S(2)}) collective-permute-start(bf16[2,256,2048]{2,1,0:T(8,128)(2,1)} %get-tuple-element.449), channel_id=1, source_target_pairs={{0,16},{8,24},{16,0},{24,8},{1,17},{9,25},{17,1},{25,9},{2,18},{10... | collective-permute-start | bytes 6291464 | tf_op jit(solution)/shard_map/ppermute | solution.py:697
  (149 other events, 2630.0 us)

commit v4 on v3

--- a/solution.py
+++ b/solution.py
@@ -78,7 +78,11 @@
     return weight.astype(jnp.float32) / 256.0
 
 
-SMALL_COST = pl.CostEstimate(flops=1, bytes_accessed=1, transcendentals=0)
+def cost_of(work):
+    return pl.CostEstimate(
+        flops=int(work * 1.15e9), bytes_accessed=int(work * 3.69e6), transcendentals=0
+    )
+
 VMEM_BYTES = 56 * 1024 * 1024
 
 
@@ -163,84 +167,89 @@
             for height, arrays in zip(heights, groups)
         ],
         compiler_params=kernel_params(),
-        cost_estimate=SMALL_COST,
+        cost_estimate=cost_of(0.3),
         name="take_blocks",
     )(order, *flat)
 
 
-def rows_kernel(order_ref, left_ref, even_ref, odd_ref, near_ref, far_ref):
-    width = even_ref.shape[0]
-    half = near_ref.shape[0]
-    for at, right_ref in enumerate((even_ref, odd_ref)):
-        span = slice(at * width, (at + 1) * width)
-        result = product_nt(left_ref[...], right_ref[...])
-        near_ref[:, span] = result[:half].astype(near_ref.dtype)
-        far_ref[:, span] = result[half:].astype(far_ref.dtype)
-
-
-def product_rows(left_side, right_side, order, width, far_type):
-    tokens, depth = left_side.shape
+def rows_kernel(order_ref, left_refs, right_refs, near_ref, far_ref):
+    half = left_refs[0].shape[0] // 2
+    for at, left_ref in enumerate(left_refs):
+        rows = slice(at * half, (at + 1) * half)
+        for place, right_ref in enumerate(right_refs[at]):
+            width = right_ref.shape[0]
+            span = slice(place * width, (place + 1) * width)
+            result = product_nt(left_ref[...], right_ref[...])
+            near_ref[rows, span] = result[:half].astype(near_ref.dtype)
+            far_ref[rows, span] = result[half:].astype(far_ref.dtype)
+
+
+def product_rows(lefts, rights, order, width, far_type, work=0.7):
+    tokens, depth = lefts[0].shape
     half = tokens // 2
     count = order.shape[0]
     if width % 128:
-        ((result,),) = [take_blocks([[product_nt(left_side, right_side)]], order, width)]
-        return (result[:half], result[half:].astype(far_type))
-    out_block = pl.BlockSpec((half, 2 * width), lambda at, order_ref: (0, at))
+        near, far = [], []
+        for left_side, right_side in zip(lefts, rights):
+            (result,) = take_blocks([[product_nt(left_side, right_side)]], order, width)
+            near.append(result[:half])
+            far.append(result[half:].astype(far_type))
+        return (jnp.concatenate(near, 0), jnp.concatenate(far, 0))
+    height = len(lefts) * half
+    out_block = pl.BlockSpec((height, 2 * width), lambda at, order_ref: (0, at))
+    right_blocks = [
+        pl.BlockSpec((width, depth), lambda at, order_ref: (order_ref[2 * at], 0)),
+        pl.BlockSpec((width, depth), lambda at, order_ref: (order_ref[2 * at + 1], 0)),
+    ]
     return pl.pallas_call(
         rows_kernel,
         grid_spec=pltpu.PrefetchScalarGridSpec(
             num_scalar_prefetch=1,
             grid=(count // 2,),
             in_specs=[
-                pl.BlockSpec((tokens, depth), lambda at, order_ref: (0, 0)),
-                pl.BlockSpec((width, depth), lambda at, order_ref: (order_ref[2 * at], 0)),
-                pl.BlockSpec((width, depth), lambda at, order_ref: (order_ref[2 * at + 1], 0)),
+                [pl.BlockSpec((tokens, depth), lambda at, order_ref: (0, 0))] * len(lefts),
+                [right_blocks] * len(lefts),
             ],
             out_specs=[out_block, out_block],
         ),
         out_shape=[
-            shaped((half, count * width), jnp.float32),
-            shaped((half, count * width), far_type),
+            shaped((height, count * width), jnp.float32),
+            shaped((height, count * width), far_type),
         ],
         compiler_params=kernel_params(),
-        cost_estimate=SMALL_COST,
+        cost_estimate=cost_of(work),
         name="product_rows",
-    )(order, left_side, right_side, right_side)
-
-
-def grad_kernel(left_refs, right_refs, extra_refs, out_ref):
+    )(order, lefts, [[right_side, right_side] for right_side in rights])
+
+
+def grad_kernel(left_refs, right_refs, out_ref):
     start = 0
     for left_ref, right_ref in zip(left_refs, right_refs):
         span = slice(start, start + right_ref.shape[1])
         start = span.stop
-        result = product_tn(left_ref[...], right_ref[...])
-        if extra_refs:
-            result = result + extra_refs[0][:, span].astype(jnp.float32)
-        out_ref[:, span] = result.astype(out_ref.dtype)
-
-
-def half_product(lefts, rights, part, extra=None):
+        out_ref[:, span] = product_tn(left_ref[...], right_ref[...]).astype(out_ref.dtype)
+
+
+def half_product(lefts, rights, part):
     tokens, width = lefts[0].shape
     columns = rights[0].shape[1]
     tile = 512
     col_tile = columns if len(rights) > 1 else 512
     steps = width // 2 // tile
-    out_block = pl.BlockSpec((tile, len(rights) * col_tile), lambda at, to: (at, to))
-    extras = [] if extra is None else [extra]
+    out_type = jnp.bfloat16 if part else jnp.float32
     return pl.pallas_call(
         grad_kernel,
         grid=(steps, columns // col_tile),
         in_specs=[
             [pl.BlockSpec((tokens, tile), lambda at, to: (0, part * steps + at))] * len(lefts),
             [pl.BlockSpec((tokens, col_tile), lambda at, to: (0, to))] * len(rights),
-            [out_block] * len(extras),
-        ],
-        out_specs=out_block,
-        out_shape=shaped((width // 2, len(rights) * columns), jnp.bfloat16),
+        ],
+        out_specs=pl.BlockSpec((tile, len(rights) * col_tile), lambda at, to: (at, to)),
+        out_shape=shaped((width // 2, len(rights) * columns), out_type),
         compiler_params=kernel_params(),
-        cost_estimate=SMALL_COST,
+        cost_estimate=cost_of(0.55),
         name="half_product",
-    )(lefts, rights, extras)
+    )(lefts, rights)
 
 
 MIX_STEP = 64
@@ -311,7 +320,7 @@
             shaped((tok_count, width), jnp.float32),
         ],
         compiler_params=kernel_params(),
-        cost_estimate=SMALL_COST,
+        cost_estimate=cost_of(0.9),
         name="mix_forward",
     )(history, mix_weight, mixing, norm_rows)
 
@@ -320,7 +329,9 @@
     hist_ref,
     cot_ref,
     tok_ref,
-    back_refs,
+    near_refs,
+    arrived_refs,
+    across_refs,
     kept_ref,
     coef_ref,
     inner_ref,
@@ -351,7 +362,8 @@
         cot_low = out_cot.astype(jnp.bfloat16).astype(jnp.float32)
         sums_ref[8:9] += jnp.sum(cot_low, 0, keepdims=True)
         for index in range(4):
-            back = back_refs[index][rows, :]
+            back = near_refs[index][rows, :] + arrived_refs[index][rows, :].astype(jnp.float32)
+            back = back + across_refs[index][rows, :].astype(jnp.float32)
             normed = kept_ref[index, rows, :]
             sums_ref[index : index + 1] += jnp.sum(back * normed, 0, keepdims=True)
             sums_ref[4 + index : 5 + index] += jnp.sum(back, 0, keepdims=True)
@@ -394,12 +406,19 @@
 
 
 def mix_backward(
-    history, cot, tok_weight, backs, kept, coef, inner, scale, mix_weight, mixing, norm_rows
+    history, cot, tok_weight, sums, across, kept, coef, inner, scale, mix_weight, mixing, norm_rows
 ):
     hist_count, tok_count, width = history.shape
     token_block = pl.BlockSpec((MIX_STEP, width), lambda at: (at, 0))
     narrow = pl.BlockSpec((MIX_STEP, MIXW), lambda at: (at, 0))
     hist_block = pl.BlockSpec((hist_count, MIX_STEP, width), lambda at: (0, at, 0))
+    pair_steps = 2 * tok_count // MIX_STEP
+    pair_blocks = [
+        pl.BlockSpec((MIX_STEP, width), lambda at, start=place * pair_steps: (start + at, 0))
+        for _, _, place in sums
+    ]
+    nears = [near for near, _, _ in sums]
+    arrived = [values for _, values, _ in sums]
     return pl.pallas_call(
         mix_backward_kernel,
         grid=(tok_count // MIX_STEP,),
@@ -407,6 +426,8 @@
             hist_block,
             token_block,
             pl.BlockSpec((MIX_STEP, 1), lambda at: (at, 0)),
+            pair_blocks,
+            pair_blocks,
             [token_block] * 4,
             pl.BlockSpec((4, MIX_STEP, width), lambda at: (0, at, 0)),
             narrow,
@@ -434,9 +455,9 @@
             pltpu.VMEM((MIX_STEP, MIXW), jnp.float32),
         ],
         compiler_params=kernel_params(),
-        cost_estimate=SMALL_COST,
+        cost_estimate=cost_of(19),
         name="mix_backward",
-    )(history, cot, tok_weight, backs, kept, coef, inner, scale, mix_weight, mixing, norm_rows)
+    )(history, cot, tok_weight, nears, arrived, across, kept, coef, inner, scale, mix_weight, mixing, norm_rows)
 
 
 def mlp_up_kernel(normed_ref, up_ref, bias_ref, act_ref, slope_ref):
@@ -465,7 +486,7 @@
         out_specs=[act_block, act_block],
         out_shape=[shaped((tokens, hidden), jnp.bfloat16), shaped((tokens, hidden), jnp.float32)],
         compiler_params=kernel_params(),
-        cost_estimate=SMALL_COST,
+        cost_estimate=cost_of(0.85),
         name="mlp_up",
     )(normed, up_weight, bias)
 
@@ -501,7 +522,7 @@
         out_specs=[act_block, row_block],
         out_shape=[shaped((tokens, hidden), jnp.bfloat16), shaped((1, hidden), jnp.float32)],
         compiler_params=kernel_params(),
-        cost_estimate=SMALL_COST,
+        cost_estimate=cost_of(0.8),
         name="mlp_back",
     )(cot, down_weight, slope)
 
@@ -591,7 +612,7 @@
         out_specs=[head_block, [head_block] * 3, whole_block((8, width))],
         out_shape=[out, [out] * 3, shaped((8, width), jnp.float32)],
         compiler_params=kernel_params(),
-        cost_estimate=SMALL_COST,
+        cost_estimate=cost_of(1.35),
         name="attention_inner",
     )(ends, normed, weights, bias, rope, cot)
 
@@ -624,7 +645,7 @@
         out_shape=[shaped(moment.shape, jnp.float32)] * 2
         + [shaped((count, rows, rows), jnp.float32)],
         compiler_params=kernel_params(),
-        cost_estimate=SMALL_COST,
+        cost_estimate=cost_of(0.5),
         name="finish_gradient",
     )(parts, moment)
 
@@ -676,7 +697,7 @@
         out_specs=[stack_block, stack_block],
         out_shape=[shaped(mom.shape, jnp.float32), shaped(mom.shape, jnp.bfloat16)],
         compiler_params=kernel_params(),
-        cost_estimate=SMALL_COST,
+        cost_estimate=cost_of(12),
         name="newton_update",
     )(gram, mom, master)
 
@@ -760,8 +781,7 @@
         first = jnp.where(odd_core == 1, other, own)
         return jnp.concatenate([first, jnp.where(odd_core == 1, own, other)], 0)
 
-    def gather_copies(self, values, across):
-        other = self.swap_core(values)
+    def gather_copies(self, values, across, other):
         other_across = self.swap_core(across)
         odd_core = self.member % 2 == 1
         high_y = self.member >= 2
@@ -855,11 +875,15 @@
     slots = jnp.stack(links.slots()).astype(jnp.int32)
     plain = links.slots_of(0, members)
 
-    def scatter_z(summed, turns):
-        return [links.swap_z(summed[turn * rows : (turn + 1) * rows], turn) for turn in turns]
-
-    def spread(left_side, right_side):
-        return product_rows(left_side, right_side, plain, rows, jnp.bfloat16)
+    def slot_sums(own, arrived, turns):
+        sums = []
+        for turn in turns:
+            total = own[turn * rows : (turn + 1) * rows] + wide(arrived[turn])
+            sums.append(total if turn == 0 else low(total))
+        return sums
+
+    def spread(lefts, rights):
+        return product_rows(lefts, rights, plain, rows, jnp.bfloat16)
 
     up_own = columns_of(mlp_weight[0], member, mlp_cols, 1)
     param_pieces = lax.all_to_all(
@@ -931,14 +955,14 @@
     full_up = jnp.concatenate(up_near + [far_up, far_up_one, far_third], 0)
     up_bias = lax.dynamic_index_in_dim(param_vals, 13 + member, 0)
     act_low, slope = mlp_up(group_normed[3], full_up, up_bias)
-    down_sent = half_product([group_cot], [act_low], 1)
-    attn_line, far_fourth, act_low, slope, down_sent, down_near, full_up = fence(
-        attn_line, far_fourth, act_low, slope, down_sent, down_near, full_up
+    attn_line, far_fourth, act_low, slope, down_near, full_up = fence(
+        attn_line, far_fourth, act_low, slope, down_near, full_up
     )
 
     for _ in range(2, depth - 1):
         attn_line = links.hop(attn_line)
     far_last = links.swap_x(down_near[depth - 1])
+    down_sent = half_product([group_cot], [act_low], 1)
     down_first = links.swap_x(down_sent[:rows])
     last_core = links.swap_core(normed_own[1])
     last_far = links.swap_core(last_y)
@@ -952,6 +976,8 @@
     full_down = jnp.concatenate(down_near + [far_down, far_fourth, far_last], 0)
     up_grad, up_sum = mlp_back(group_cot, full_down, slope)
     up_sent = half_product([group_normed[3]], [up_grad], 1)
+    down_own_sum = half_product([group_cot], [act_low], 0)
+    three_near, three_sent = spread([up_grad], [full_up])
     last_parts = (normed_own[1], last_y, last_core, last_far)
     group_normed[0] = jnp.concatenate([values[:tok_count] for values in last_parts], 0)
     group_normed[1] = jnp.concatenate([values[tok_count:] for values in last_parts], 0)
@@ -959,11 +985,18 @@
     attn_near = [links.near(attn_line, turn) for turn in range(depth)]
     half_depth = depth // 2
     up_sent = cut(up_sent, (half_depth * rows, half_depth * rows))
-    attn_near, down_rest, up_grad, up_sum, up_sent, full_down, cot_cols, group_normed = fence(
-        attn_near, down_rest, up_grad, up_sum, up_sent, full_down, cot_cols, group_normed
-    )
-
-    up_first = links.swap_x(up_sent[0])
+    (
+        attn_near, down_rest, up_grad, up_sum, up_sent, full_down, cot_cols, group_normed,
+        down_own_sum, three_near, three_sent,
+    ) = fence(
+        attn_near, down_rest, up_grad, up_sum, up_sent, full_down, cot_cols, group_normed,
+        down_own_sum, three_near, three_sent,
+    )
+
+    up_last = links.swap_x(up_sent[1])
+    down_arrived = [down_first] + cut(down_rest, (rows,) * (depth - 1))
+    down_summed = slot_sums(down_own_sum, down_arrived, range(depth))
+    down_parts = [links.swap_z(down_summed[turn], turn) for turn in range(1, depth - 1)]
     full_attn = [
         jnp.concatenate(
             [
@@ -977,23 +1010,45 @@
     ]
     order = [links.slots_of(links.partner(at) * col_blocks, col_blocks) for at in range(group)]
     context_sum = jnp.concatenate(
-        product_rows(cot_cols, full_attn[3], jnp.concatenate(order), rows, jnp.float32), 0
+        product_rows([cot_cols], [full_attn[3]], jnp.concatenate(order), rows, jnp.float32), 0
     )
     context_sum = [context_sum[:, at * attn_cols : (at + 1) * attn_cols] for at in range(group)]
     sent = low(jnp.concatenate(context_sum[2:], 1))
-    arrived = links.swap_core(turn_core(sent))
-    context_y = links.swap_y(turn_y(low(context_sum[1] + wide(arrived[:, attn_cols:]))))
-    context_grad = low(context_sum[0] + wide(arrived[:, :attn_cols]) + wide(context_y))
-    down_summed = half_product(
-        [group_cot], [act_low], 0, jnp.concatenate([down_first, down_rest], 0)
-    )
-    down_parts = scatter_z(down_summed, range(1, depth - 1))
-    up_first, down_summed, down_parts, full_attn, context_grad, up_sent = fence(
-        up_first, down_summed, down_parts, full_attn, context_grad, up_sent
-    )
-
-    up_rest = links.swap_x(up_sent[1])
-    down_parts = [down_summed[:rows]] + down_parts + scatter_z(down_summed, [depth - 1])
+    sent = turn_core(sent)
+    context_sent = context_sum[1] + wide(links.swap_core(sent[:, attn_cols:]))
+    context_sent = turn_y(low(context_sent))
+    context_own = context_sum[0] + wide(links.swap_core(sent[:, :attn_cols]))
+    three_arrived = links.swap_core(three_sent)
+    up_own_sum = half_product([group_normed[3]], [up_grad], 0)
+    (
+        up_last, down_summed, down_parts, full_attn, context_sent, context_own, up_sent, up_own_sum,
+        three_arrived,
+    ) = fence(
+        up_last, down_summed, down_parts, full_attn, context_sent, context_own, up_sent, up_own_sum,
+        three_arrived,
+    )
+
+    def halves(near, arrived):
+        summed = near + wide(arrived)
+        return (summed[:tok_count], low(summed[tok_count:]))
+
+    up_first = links.swap_x(up_sent[0])
+    down_parts = [down_summed[0]] + down_parts + [links.swap_z(down_summed[-1], depth - 1)]
+    context_y = links.swap_y(context_sent)
+    half_depth = depth // 2
+    last_turns = range(half_depth, depth)
+    up_arrived = [None] * half_depth + cut(up_last, (rows,) * half_depth)
+    up_summed = [None] * half_depth + slot_sums(up_own_sum, up_arrived, last_turns)
+    three_sent = low(three_near[tok_count:] + wide(three_arrived[tok_count:]))
+    context_grad = low(context_own + wide(context_y))
+    (
+        up_first, down_parts, context_grad, up_summed, up_own_sum, three_sent,
+    ) = fence(
+        up_first, down_parts, context_grad, up_summed, up_own_sum, three_sent,
+    )
+
+    up_parts = [links.swap_z(up_summed[turn], turn) for turn in list(last_turns)[:-1]]
+    three_y = links.swap_y(three_sent)
     attn_bias = lax.dynamic_slice(param_vals, (8, member * attn_cols), (3, attn_cols))
     context_low, proj_grads, proj_sums = attention_inner(
         jnp.cumsum(group_lengths, 1),
@@ -1006,23 +1061,54 @@
     two_sent = half_product(
         [group_normed[2], group_normed[0]], [proj_grads[2], proj_grads[0]], 1
     )
-    three_near, three_sent = spread(up_grad, full_up)
+    token_near, token_sent = spread(
+        [proj_grads[at] for at in (2, 0, 1)], [full_attn[at] for at in (2, 0, 1)]
+    )
     context_turned = turn_y(context_low)
     (
-        up_rest, down_parts, context_low, context_turned, proj_grads, proj_sums, two_sent,
-        three_near, three_sent,
+        up_parts, up_summed, context_low, context_turned, proj_grads, proj_sums, two_sent,
+        token_near, token_sent, three_y, full_attn, up_first, up_own_sum, act_low, full_down,
     ) = fence(
-        up_rest, down_parts, context_low, context_turned, proj_grads, proj_sums, two_sent,
-        three_near, three_sent,
+        up_parts, up_summed, context_low, context_turned, proj_grads, proj_sums, two_sent,
+        token_near, token_sent, three_y, full_attn, up_first, up_own_sum, act_low, full_down,
     )
 
     two_x = links.swap_x(two_sent)
-    up_summed = half_product(
-        [group_normed[3]], [up_grad], 0, jnp.concatenate([up_first, up_rest], 0)
-    )
-    up_parts = scatter_z(up_summed, range(1, depth - 1))
+    up_arrived = cut(up_first, (rows,) * half_depth)
+    up_summed = slot_sums(up_own_sum, up_arrived, range(half_depth)) + up_summed[half_depth:]
+    up_parts = [up_summed[0]] + up_parts
+    up_parts += [
+        links.swap_z(up_summed[turn], turn) for turn in [depth - 1] + list(range(1, half_depth))
+    ]
+    token_arrived = links.swap_core(token_sent)
+    mlp_near, mlp_sent = product_rows([act_low], [full_down], plain, rows, jnp.float32, 9)
     context_near = jnp.concatenate([context_low, links.swap_y(context_turned)], 1)
-    context_far = links.swap_core(turn_core(context_near))
+    context_sent = turn_core(context_near)
+    two_own_sum = half_product(
+        [group_normed[2], group_normed[0]], [proj_grads[2], proj_grads[0]], 0
+    )
+    one_sent = half_product([group_normed[1]], [proj_grads[1]], 1)
+    (
+        two_x, up_parts, context_near, context_sent, two_own_sum, one_sent, token_near,
+        token_arrived, proj_grads, mlp_near, mlp_sent,
+    ) = fence(
+        two_x, up_parts, context_near, context_sent, two_own_sum, one_sent, token_near,
+        token_arrived, proj_grads, mlp_near, mlp_sent,
+    )
+
+    one_x = links.swap_x(one_sent)
+    two_summed = slot_sums(two_own_sum, cut(two_x, (rows,) * depth), range(depth))
+    two_parts = [two_summed[0]]
+    two_parts += [
+        links.swap_z(two_summed[turn], turn) for turn in list(range(2, depth)) + [1]
+    ]
+    token_sent = []
+    for at in range(3):
+        span = slice((2 * at + 1) * tok_count, (2 * at + 2) * tok_count)
+        token_sent.append(low(token_near[span] + wide(token_arrived[span])))
+    two_y = links.swap_y(token_sent[0])
+    zero_y = links.swap_y(token_sent[1])
+    context_far = links.swap_core(context_sent)
     order = []
     for owner in links.slots():
         place = (owner // col_blocks) ^ member
@@ -1033,53 +1119,62 @@
         jnp.stack(order).astype(jnp.int32),
         rows,
     )
-    one_sent = half_product([group_normed[1], group_context], [proj_grads[1], cot_cols], 1)
-    three_arrived = links.swap_core(three_sent)
-    token_parts = [spread(proj_grads[at], full_attn[at]) for at in range(3)]
-    two_x, up_summed, up_parts, group_context, one_sent, token_parts, three_arrived = fence(
-        two_x, up_summed, up_parts, group_context, one_sent, token_parts, three_arrived
-    )
-
-    def across_y(near, arrived):
-        summed = near + wide(arrived)
-        return summed[:tok_count] + wide(links.swap_y(low(summed[tok_count:])))
-
-    one_x = links.swap_x(one_sent)
-    up_parts = [up_summed[:rows]] + up_parts + scatter_z(up_summed, [depth - 1])
-    two_summed = half_product(
-        [group_normed[2], group_normed[0]], [proj_grads[2], proj_grads[0]], 0, two_x
-    )
-    two_parts = scatter_z(two_summed, [1])
-    back_three = across_y(three_near, three_arrived)
-    token_arrived = [links.swap_core(far) for _, far in token_parts]
-    back_two = across_y(token_parts[2][0], token_arrived[2])
-    one_x, up_parts, two_summed, two_parts, back_three, back_two, token_arrived = fence(
-        one_x, up_parts, two_summed, two_parts, back_three, back_two, token_arrived
-    )
-
-    two_parts = [two_summed[:rows]] + two_parts + scatter_z(two_summed, range(2, depth))
+    out_weight_sent = half_product([group_context], [cot_cols], 1)
+    one_own_sum = half_product([group_normed[1]], [proj_grads[1]], 0)
     mlp_grad, mlp_mom, mlp_gram = finish_gradient([up_parts, down_parts], mlp_moment)
-    one_summed = half_product(
-        [group_normed[1], group_context], [proj_grads[1], cot_cols], 0, one_x
-    )
-    one_parts = scatter_z(one_summed, [1])
+    (
+        one_x, two_parts, zero_y, two_y, group_context, out_weight_sent, one_own_sum, mlp_mom,
+        mlp_gram, token_sent,
+    ) = fence(
+        one_x, two_parts, zero_y, two_y, group_context, out_weight_sent, one_own_sum, mlp_mom,
+        mlp_gram, token_sent,
+    )
+
+    out_x = links.swap_x(out_weight_sent)
+    one_summed = slot_sums(one_own_sum, cut(one_x, (rows,) * depth), range(depth))
+    one_parts = [one_summed[0]]
+    one_parts += [links.swap_z(one_summed[turn], turn) for turn in range(1, depth)]
+    one_y = links.swap_y(token_sent[2])
     mlp_gram = links.sum_stack(mlp_gram)
-    back_zero = across_y(token_parts[0][0], token_arrived[0])
-    back_one = across_y(token_parts[1][0], token_arrived[1])
-    two_parts, one_summed, one_parts, back_zero, back_one, mlp_mom, mlp_gram = fence(
-        two_parts, one_summed, one_parts, back_zero, back_one, mlp_mom, mlp_gram
-    )
-
-    one_parts = [one_summed[:rows]] + one_parts + scatter_z(one_summed, range(2, depth))
+    out_own_sum = half_product([group_context], [cot_cols], 0)
+    attn_out = jnp.dot(group_context, full_attn[3], preferred_element_type=jnp.float32)
+
+    def with_attn(part, addend):
+        own = columns_of(part, member, attn_cols, 1) + addend
+        return lax.dynamic_update_slice_in_dim(part, own, member * attn_cols, 1)
+
+    out_sent = low(with_attn(mlp_sent, attn_out[near_tok:]))
+    out_near = with_attn(mlp_near, attn_out[:near_tok])
+    out_own, out_sent = halves(out_near, links.swap_core(out_sent))
+    out_x, one_parts, mlp_gram, out_own_sum, out_own, out_sent, zero_y, one_y, two_y, three_y = fence(
+        out_x, one_parts, mlp_gram, out_own_sum, out_own, out_sent, zero_y, one_y, two_y, three_y
+    )
+
+    out_summed = slot_sums(out_own_sum, cut(out_x, (rows,) * depth), range(depth))
+    out_parts = [out_summed[0]]
+    out_parts += [links.swap_z(out_summed[turn], turn) for turn in range(1, depth)]
+    out_y = links.swap_y(out_sent)
     mlp_new, mlp_low = newton_update(
         mlp_gram, mlp_mom, mlp_master, LR_MUON * 0.2 * math.sqrt(FF)
     )
-    mlp_across = links.swap_y(mlp_low)
+    out_parts, out_y, mlp_low, zero_y, one_y, two_y, three_y = fence(
+        out_parts, out_y, mlp_low, zero_y, one_y, two_y, three_y
+    )
+
+    attn_parts = [
+        [values[:, attn_cols:] for values in two_parts],
+        one_parts,
+        [values[:, :attn_cols] for values in two_parts],
+        out_parts,
+    ]
+    attn_grad, attn_mom, attn_gram = finish_gradient(attn_parts, attn_moment)
+    attn_gram = links.sum_stack(attn_gram)
     history_grad, sums, mix_weight_grad, mixing_grad = mix_backward(
         history,
         out_grad,
         tok_weight[:, None],
-        [back_zero, back_one, back_two, back_three],
+        [(token_near, token_arrived, at) for at in (1, 2, 0)] + [(three_near, three_arrived, 0)],
+        [zero_y, one_y, two_y, three_y],
         kept,
         coef,
         inner,
@@ -1088,28 +1183,9 @@
         mixing,
         param_vals[:8],
     )
-    one_parts, mlp_low, mlp_across, sums, mix_weight_grad, mixing_grad = fence(
-        one_parts, mlp_low, mlp_across, sums, mix_weight_grad, mixing_grad
-    )
-
-    attn_parts = [
-        [values[:, :attn_cols] for values in two_parts],
-        [values[:, attn_cols:] for values in two_parts],
-        [values[:, :attn_cols] for values in one_parts],
-        [values[:, attn_cols:] for values in one_parts],
-    ]
-    attn_parts = [attn_parts[1], attn_parts[2], attn_parts[0], attn_parts[3]]
-    attn_grad, attn_mom, attn_gram = finish_gradient(attn_parts, attn_moment)
-    attn_gram = links.sum_stack(attn_gram)
-    mlp_near, mlp_sent = product_rows(act_low, full_down, plain, rows, jnp.float32)
-    attn_out = jnp.dot(group_context, full_attn[3], preferred_element_type=jnp.float32)
-
-    def with_attn(part, addend):
-        own = columns_of(part, member, attn_cols, 1) + addend
-        return lax.dynamic_update_slice_in_dim(part, own, member * attn_cols, 1)
-
-    out_sent = low(with_attn(mlp_sent, attn_out[near_tok:]))
-    out_near = with_attn(mlp_near, attn_out[:near_tok])
+    mlp_across = links.swap_y(mlp_low)
+    mlp_other = links.swap_core(mlp_low)
+    layer_out = low(stream_three + out_own + wide(out_y) + (param_vals[11] + param_vals[12]))
 
     def placed(values, total):
         return lax.dynamic_update_slice_in_dim(
@@ -1133,17 +1209,16 @@
     mix_flat = jnp.pad(mixing_grad.reshape(-1), (0, mix_rows * rows - mix_size))
     mix_flat = jnp.broadcast_to(mix_flat.reshape(1, mix_rows, rows), (members, mix_rows, rows))
     small_sent = jnp.concatenate([param_pieces_grad, mix_flat], 1)
-    attn_gram, small_sent, attn_mom, out_sent, out_near = fence(
-        attn_gram, small_sent, attn_mom, out_sent, out_near
+    attn_gram, small_sent, attn_mom, mlp_across, mlp_other = fence(
+        attn_gram, small_sent, attn_mom, mlp_across, mlp_other
     )
 
     attn_new, attn_low = newton_update(
         attn_gram, attn_mom, attn_master, LR_MUON * 0.2 * math.sqrt(model_width)
     )
-    attn_copy = links.gather_copies(attn_low, links.swap_y(attn_low))
-    out_own = across_y(out_near, links.swap_core(out_sent))
-    layer_out = low(stream_three + out_own + (param_vals[11] + param_vals[12]))
-    mlp_copy = links.gather_copies(mlp_low, mlp_across)
+    attn_copy = links.gather_copies(attn_low, links.swap_y(attn_low), links.swap_core(attn_low))
+    mlp_copy = links.gather_copies(mlp_low, mlp_across, mlp_other)
+    small_sent, attn_low = fence(small_sent, attn_low)
     small = lax.all_to_all(small_sent, "fsdp", 0, 0, tiled=True)
     small = links.sum_group(jnp.sum(small, 0))
     param_part = small[:param_rows]

time: 1040 us -> 924 us (0.89)
  waiting for transfers between devices: 366 us -> 244 us
  starting transfers between devices: 116 us -> 133 us
    ppermute x16, waiting for transfers between devices: 138 us -> 51.4 us  [swap_y(): return lax.ppermute(values, 'dp', [(at, at ^ 2) for at in range(4)])]
    convert_element_type x7 -> x14, other arithmetic: 9.33 us -> 33.6 us  [low(): return values.astype(jnp.bfloat16)]
    ppermute x12 -> x15, waiting for transfers between devices: 93.1 us -> 69.4 us  [swap_z(): return lax.ppermute(values, 'fsdp', pairs)]
    slice x17 -> x3, local copies, waits for them, and re-layouts: 17.2 us -> 0.14 us  [halves(): return (summed[:tok_count], low(summed[tok_count:]))]
    ppermute x9, waiting for transfers between devices: 79 us -> 64.3 us  [hop(): lax.ppermute(fall[-1], 'fsdp', down_pairs)]
    add x10 -> x3, other arithmetic: 22.2 us -> 7.78 us  [the longest x1 3.69 us: body(): context_own = context_sum[0] + wide(links.swap_core(sent[:, :attn_cols]))]
    all_to_all x1, waiting for transfers between devices: 0.01 us -> 13 us  [body(): small = lax.all_to_all(small_sent, 'fsdp', 0, 0, tiled=True)]
    ppermute x12 -> x13, waiting for transfers between devices: 48.5 us -> 36.7 us  [swap_x(): lax.ppermute(values, 'fsdp', [(at, at ^ 1) for at in range(self.members)])]
  transfers between devices with their start and end apart: 82 -> 85, of which waited for: 29 -> 29; matrix products, arithmetic and copies ran while one was open for 17% -> 18% of each run, Pallas kernels for 27% -> 31%
where the time goes in v4:
time: 924 us; the launch traced here: 912 us
  Pallas kernels  319 us (35%)
  waiting for transfers between devices  244 us (26%)
  starting transfers between devices  133 us (14%)
  other arithmetic  111 us (12%)
  local copies, waits for them, and re-layouts  102 us (11%)
    pallas_call x10, Pallas kernels, half_product(): pl.pallas_call(grad_kernel, grid=(steps, columns // col_tile), in_specs=[...  73.7 us
    ppermute x15, waiting for transfers between devices, swap_z(): return lax.ppermute(values, 'fsdp', pairs)  69.4 us
    ppermute x9, waiting for transfers between devices, hop(): lax.ppermute(fall[-1], 'fsdp', down_pairs)  64.3 us
    ppermute x16, waiting for transfers between devices, swap_y(): return lax.ppermute(values, 'dp', [(at, at ^ 2) for at in range(4)])  51.4 us
    pallas_call x4, Pallas kernels, product_rows(): pl.pallas_call(rows_kernel, grid_spec=pltpu.PrefetchScalarGridSpec(num_sc...  49.4 us
    pallas_call x2, Pallas kernels, newton_update(): pl.pallas_call(functools.partial(newton_kernel, rate=rate), grid=(count /...  41.9 us
    ppermute x21, starting transfers between devices, swap_core(): return lax.ppermute(values, 'dp', [(at, at ^ 1) for at in range(4)])  41.5 us
    unnamed x200, local copies, waits for them, and re-layouts  40.7 us
  transfers between devices with their start and end apart: 85, of which 29 were waited for; matrix products, arithmetic and copies ran while one was open for 18% of the time, Pallas kernels for 31%

profile of v4, /device:TPU:1, one launch (start us, length us, event | category | flops | bytes accessed | tf_op | source)
XLA Modules:
  0.0 912.5 jit_solution(10394662438229258588)
XLA Ops:
  46.9 18.4 %mix_forward.1 = (bf16[256,2048]{1,0:T(8,128)(2,1)}, bf16[256,2048]{1,0:T(8,128)(2,1)}, bf16[256,2048]{1,0:T(8,128)(2,1)}, bf16[256,2048]{1,0:T(8,128)(2,1)}, f3...) custom-call(bf16[9,256,2048]{2,1,0:T(8,128)(2,1)} %hist_ref.3, ...), custom_call_target="tpu_custom_call" | custom-call | flops 1035000000 | bytes 3321000 | tf_op jit(solution)/shard_map/mix_forward/pallas_call | solution.py:297
  86.2 14.5 %collective-permute-done.10 = bf16[256,2048]{1,0:T(8,128)(2,1)S(1)} collective-permute-done((bf16[256,2048]{1,0:T(8,128)(2,1)S(1)}, bf16[256,2048]{1,0:T(8,128)(2,1)S(1)}, u32[]{:S(2)}, u32[]{:S(2)}) %collective-permute-start.10) | collective-permute-done | bytes 1048608 | tf_op jit(solution)/shard_map/ppermute | solution.py:747
  105.2 18.0 %collective-permute-done.12 = bf16[256,2048]{1,0:T(8,128)(2,1)} collective-permute-done((bf16[256,2048]{1,0:T(8,128)(2,1)S(1)}, bf16[256,2048]{1,0:T(8,128)(2,1)}, u32[]{:S(2)}, u32[]{:S(2)}) %collective-permute-start.12) | collective-permute-done | bytes 1048608 | tf_op jit(solution)/shard_map/ppermute | solution.py:747
  142.0 22.2 %collective-permute-done.18 = bf16[256,2048]{1,0:T(8,128)(2,1)S(1)} collective-permute-done((bf16[256,2048]{1,0:T(8,128)(2,1)}, bf16[256,2048]{1,0:T(8,128)(2,1)S(1)}, u32[]{:S(2)}, u32[]{:S(2)}) %collective-permute-start.18) | collective-permute-done | bytes 1048608 | tf_op jit(solution)/shard_map/ppermute | solution.py:747
  222.9 17.4 %mlp_up.1 = (bf16[1024,2048]{1,0:T(8,128)(2,1)}, f32[1024,2048]{1,0:T(8,128)}) custom-call(bf16[1024,2048]{1,0:T(8,128)(2,1)} %pad_maximum_fusion.2.normed_ref.left_refs_0_, bf16[2048,2048]{1,0:T(8,128)(2,1)} %constant_dynamic-update-slice_fusion.up_ref.right_refs_0__0_.right_refs_0__1_, f32[1,2048]{1,0:T(1,128)} %get-tuple-element.628.bias_ref), custom_call_target="tpu_custom_call" | custom-call | flops 977500032 | bytes 3136500 | tf_op jit(solution)/shard_map/mlp_up/pallas_call | solution.py:478
  265.1 10.8 %half_product.10 = bf16[1024,2048]{1,0:T(8,128)(2,1)} custom-call(bf16[1024,2048]{1,0:T(8,128)(2,1)} %pad_maximum_fusion.1.left_refs_0_.cot_ref.refs_0_, bf16[1024,2048]{1,0:T(8,128)(2,1)} %get-tuple-element.411.right_refs_0_.left_refs_0_), custom_call_target="tpu_custom_call" | custom-call | flops 632499968 | bytes 2029500 | tf_op jit(solution)/shard_map/half_product/pallas_call | solution.py:240
  282.8 11.9 %half_product.12 = f32[1024,2048]{1,0:T(8,128)} custom-call(bf16[1024,2048]{1,0:T(8,128)(2,1)} %pad_maximum_fusion.1.left_refs_0_.cot_ref.refs_0_, bf16[1024,2048]{1,0:T(8,128)(2,1)} %get-tuple-element.411.right_refs_0_.left_refs_0_), custom_call_target="tpu_custom_call" | custom-call | flops 632499968 | bytes 2029500 | tf_op jit(solution)/shard_map/half_product/pallas_call | solution.py:240
  321.0 15.9 %mlp_back.1 = (bf16[1024,2048]{1,0:T(8,128)(2,1)}, f32[1,2048]{1,0:T(1,128)}) custom-call(bf16[1024,2048]{1,0:T(8,128)(2,1)} %pad_maximum_fusion.1.left_refs_0_.cot_ref.refs_0_, bf16[2048,2048]{1,0:T(8,128)(2,1)} %constant_dynamic-update-slice_fusion.6.down_ref.right_refs_0__0_.right_refs_0__1_, f32[1024,2048]{1,0:T(8,128)} %get-tuple-element.341.slope_ref), custom_call_target="tpu_custom_call" | custom-call | flops 920000000 | bytes 2952000 | tf_op jit(solution)/shard_map/mlp_back/pallas_call | solution.py:514
  337.0 10.8 %half_product.11 = bf16[1024,2048]{1,0:T(8,128)(2,1)} custom-call(bf16[1024,2048]{1,0:T(8,128)(2,1)} %pad_maximum_fusion.2.normed_ref.left_refs_0_, bf16[1024,2048]{1,0:T(8,128)(2,1)} %get-tuple-element.364.right_refs_0_.left_refs_0_), custom_call_target="tpu_custom_call" | custom-call | flops 632499968 | bytes 2029500 | tf_op jit(solution)/shard_map/half_product/pallas_call | solution.py:240
  347.7 14.3 %product_rows.4 = (f32[512,2048]{1,0:T(8,128)}, bf16[512,2048]{1,0:T(8,128)(2,1)}) custom-call(s32[8]{0:T(128)} %stack.142.order_ref, bf16[1024,2048]{1,0:T(8,128)(2,1)} %get-tuple-element.364.right_refs_0_.left_refs_0_, bf16[2048,2048]{1,0:T(8,128)(2,1)} %constant_dynamic-update-slice_fusion.up_ref.right_refs_0__0_.right_refs_0__1_, ...), custom_call_target="tpu_custom_call" | custom-call | flops 805000000 | bytes 2583000 | tf_op jit(solution)/shard_map/product_rows/pallas_call | solution.py:204
  423.8 12.3 %half_product.13 = f32[1024,2048]{1,0:T(8,128)} custom-call(bf16[1024,2048]{1,0:T(8,128)(2,1)} %pad_maximum_fusion.2.normed_ref.left_refs_0_, bf16[1024,2048]{1,0:T(8,128)(2,1)} %get-tuple-element.364.right_refs_0_.left_refs_0_), custom_call_target="tpu_custom_call" | custom-call | flops 632499968 | bytes 2029500 | tf_op jit(solution)/shard_map/half_product/pallas_call | solution.py:240
  440.0 30.2 %collective-permute-done.38.part_refs_1__2_ = bf16[256,2048]{1,0:T(8,128)(2,1)S(1)} collective-permute-done((bf16[256,2048]{1,0:T(8,128)(2,1)}, bf16[256,2048]{1,0:T(8,128)(2,1)S(1)}, u32[]{:S(2)}, u32[]{:S(2)}) %collective-permute-start.38) | collective-permute-done | bytes 1048608 | tf_op jit(solution)/shard_map/ppermute | solution.py:725
  476.8 19.8 %collective-permute-done.44 = bf16[1024,512]{1,0:T(8,128)(2,1)S(1)} collective-permute-done((bf16[1024,512]{1,0:T(8,128)(2,1)S(1)}, bf16[1024,512]{1,0:T(8,128)(2,1)S(1)}, u32[]{:S(2)}, u32[]{:S(2)}) %collective-permute-start.44) | collective-permute-done | bytes 1048608 | tf_op jit(solution)/shard_map/ppermute | solution.py:718
  498.3 18.8 %collective-permute-done.42 = bf16[512,2048]{1,0:T(8,128)(2,1)S(1)} collective-permute-done((bf16[512,2048]{1,0:T(8,128)(2,1)S(1)}, bf16[512,2048]{1,0:T(8,128)(2,1)S(1)}, u32[]{:S(2)}, u32[]{:S(2)}) %collective-permute-start.42) | collective-permute-done | bytes 2097184 | tf_op jit(solution)/shard_map/ppermute | solution.py:721
  524.9 27.0 %attention_inner.1 = (bf16[1024,512]{1,0:T(8,128)(2,1)}, bf16[1024,512]{1,0:T(8,128)(2,1)}, bf16[1024,512]{1,0:T(8,128)(2,1)}, bf16[1024,512]{1,0:T(8,128)(2,1)}, f32[8,512]{1,0:T(8,128)}) custom-call(s32[4,3]{1,0:T(4,128)} %reduce_window_sum.18.ends_ref, bf16[1024,2048]{1,0:T(8,128)(2,1)} %pad_maximum_fusion.4.normed_refs_0_.left_refs_1_, ...), custom_call_target="tpu_custom_call" | custom-call | flops 1552499968 | bytes 4981500 | tf_op jit(solution)/shard_map/attention_inner/pallas_call | solution.py:601
  557.7 13.4 %product_rows.6 = (f32[1536,2048]{1,0:T(8,128)}, bf16[1536,2048]{1,0:T(8,128)(2,1)}) custom-call(s32[8]{0:T(128)} %stack.142.order_ref, bf16[1024,512]{1,0:T(8,128)(2,1)} %get-tuple-element.406.right_refs_0_.left_refs_0_, bf16[1024,512]{1,0:T(8,128)(2,1)} %get-tuple-element.407.right_refs_1_.left_refs_1_, ...), custom_call_target="tpu_custom_call" | custom-call | flops 805000000 | bytes 2583000 | tf_op jit(solution)/shard_map/product_rows/pallas_call | solution.py:204
  583.7 14.5 %product_rows.7 = (f32[512,2048]{1,0:T(8,128)}, f32[512,2048]{1,0:T(8,128)}) custom-call(s32[8]{0:T(128)} %stack.142.order_ref, bf16[1024,2048]{1,0:T(8,128)(2,1)} %get-tuple-element.411.right_refs_0_.left_refs_0_, bf16[2048,2048]{1,0:T(8,128)(2,1)} %constant_dynamic-update-slice_fusion.6.down_ref.right_refs_0__0_.right_refs_0__1_, ...), custom_call_target="tpu_custom_call" | custom-call | flops 10350000128 | bytes 33210000 | tf_op jit(solution)/shard_map/product_rows/pallas_call | solution.py:204
  612.4 12.4 %collective-permute-done.49.part_refs_0__3_ = bf16[256,2048]{1,0:T(8,128)(2,1)} collective-permute-done((bf16[256,2048]{1,0:T(8,128)(2,1)}, bf16[256,2048]{1,0:T(8,128)(2,1)}, u32[]{:S(2)}, u32[]{:S(2)}) %collective-permute-start.49) | collective-permute-done | bytes 1048608 | tf_op jit(solution)/shard_map/ppermute | solution.py:725
  675.0 14.3 %collective-permute-done.53 = bf16[256,1024]{1,0:T(8,128)(2,1)} collective-permute-done((bf16[256,1024]{1,0:T(8,128)(2,1)S(1)}, bf16[256,1024]{1,0:T(8,128)(2,1)}, u32[]{:S(2)}, u32[]{:S(2)}) %collective-permute-start.53) | collective-permute-done | bytes 524320 | tf_op jit(solution)/shard_map/ppermute | solution.py:725
  715.0 14.2 %collective-permute-done.64 = f32[1,256,256]{2,1,0:T(8,128)S(1)} collective-permute-done((f32[1,256,256]{2,1,0:T(8,128)S(1)}, f32[1,256,256]{2,1,0:T(8,128)S(1)}, u32[]{:S(2)}, u32[]{:S(2)}) %collective-permute-start.64) | collective-permute-done | bytes 262176 | tf_op jit(solution)/shard_map/ppermute | solution.py:718
  752.7 19.1 %newton_update.2 = (f32[2,256,2048]{2,1,0:T(8,128)}, bf16[2,256,2048]{2,1,0:T(8,128)(2,1)}) custom-call(f32[2,256,256]{2,1,0:T(8,128)} %pad_maximum_fusion.19.gram_ref, f32[2,256,2048]{2,1,0:T(8,128)} %get-tuple-element.246.mom_ref, f32[2,256,2048]{2,1,0:T(8,128)} %master_ref.2), custom_call_target="tpu_custom_call" | custom-call | flops 13799999488 | bytes 44280000 | tf_op jit(solution)/shard_map/newton_update/pallas_call | solution.py:689
  802.7 34.4 %mix_backward.1 = (bf16[9,256,2048]{2,1,0:T(8,128)(2,1)}, f32[16,2048]{1,0:T(8,128)}, f32[36,2048]{1,0:T(8,128)}, f32[37,36]{1,0:T(8,128)}) custom-call(bf16[9,256,2048]{2,1,0:T(8,128)(2,1)} %hist_ref.3, bf16[256,2048]{1,0:T(8,128)(2,1)} %cot_ref.1, f32[256,1]{1,0:T(8,128)} %copy.51.tok_ref, ...), custom_call_target="tpu_custom_call" | custom-call | flops 21849999360 | bytes 70110000 | tf_op jit(solution)/shard_map/mix_backward/pallas_call | solution.py:422
  846.0 22.7 %newton_update.3 = (f32[4,256,512]{2,1,0:T(8,128)}, bf16[4,256,512]{2,1,0:T(8,128)(2,1)}) custom-call(f32[4,256,256]{2,1,0:T(8,128)} %pad_maximum_fusion.18.gram_ref, f32[4,256,512]{2,1,0:T(8,128)} %get-tuple-element.242.mom_ref, f32[4,256,512]{2,1,0:T(8,128)} %master_ref.3), custom_call_target="tpu_custom_call" | custom-call | flops 13799999488 | bytes 44280000 | tf_op jit(solution)/shard_map/newton_update/pallas_call | solution.py:689
  873.3 13.0 %all-to-all-done.1 = f32[8,59,256]{2,1,0:T(8,128)S(1)} async-done(((f32[8,59,256]{2,1,0:T(8,128)}), f32[8,59,256]{2,1,0:T(8,128)S(1)}, u32[]{:S(2)}, u32[]{:S(2)}) %all-to-all-start.1) | async-done | bytes 483360 | tf_op jit(solution)/shard_map/all_to_all | solution.py:1222
  (519 shorter events, 490.0 us)
Async XLA Ops:
  131.8 47.2 %collective-permute-start.23 = (bf16[512,2048]{1,0:T(8,128)(2,1)}, bf16[512,2048]{1,0:T(8,128)(2,1)}, u32[]{:S(2)}, u32[]{:S(2)}) collective-permute-start(bf16[512,2048]{1,0:T(8,128)(2,1)} %get-tuple-element.297), channel_id=1, source_target_pairs={{0,16},{8,24},{16,0},{24,8},{1,17},{9,25},{17,1},{25,9},{2,18},{10... | collective-permute-start | bytes 6291464 | tf_op jit(solution)/shard_map/ppermute | solution.py:718
  173.1 108.5 %collective-permute-start.31 = (bf16[512,2048]{1,0:T(8,128)(2,1)}, bf16[512,2048]{1,0:T(8,128)(2,1)}, u32[]{:S(2)}, u32[]{:S(2)}) collective-permute-start(bf16[512,2048]{1,0:T(8,128)(2,1)} %get-tuple-element.297), channel_id=1, source_target_pairs={{0,8},{8,0},{16,24},{24,16},{1,9},{9,1},{17,25},{25,17},{2,10},{10... | collective-permute-start | bytes 6291464 | tf_op jit(solution)/shard_map/ppermute | solution.py:715
  191.1 55.9 %collective-permute-start.25 = (bf16[512,2048]{1,0:T(8,128)(2,1)S(1)}, bf16[512,2048]{1,0:T(8,128)(2,1)}, u32[]{:S(2)}, u32[]{:S(2)}) collective-permute-start(bf16[512,2048]{1,0:T(8,128)(2,1)S(1)} %pad_maximum_fusion.11), channel_id=1, source_target_pairs={{2,0},{3,1},{4,2},{5,3},{6,4},{7,5},{10,8},{11,9},{12,10},{13,11},... | collective-permute-start | bytes 6291464 | tf_op jit(solution)/shard_map/ppermute | solution.py:747
  192.4 54.6 %collective-permute-start.24 = (bf16[512,2048]{1,0:T(8,128)(2,1)S(1)}, bf16[512,2048]{1,0:T(8,128)(2,1)}, u32[]{:S(2)}, u32[]{:S(2)}) collective-permute-start(bf16[512,2048]{1,0:T(8,128)(2,1)S(1)} %pad_maximum_fusion.11), channel_id=1, source_target_pairs={{0,2},{1,3},{2,4},{3,5},{4,6},{5,7},{8,10},{9,11},{10,12},{11,13},... | collective-permute-start | bytes 6291464 | tf_op jit(solution)/shard_map/ppermute | solution.py:746
  204.8 96.4 %collective-permute-start.32 = (bf16[512,2048]{1,0:T(8,128)(2,1)}, bf16[512,2048]{1,0:T(8,128)(2,1)}, u32[]{:S(2)}, u32[]{:S(2)}) collective-permute-start(bf16[512,2048]{1,0:T(8,128)(2,1)} %collective-permute-done.23), channel_id=1, source_target_pairs={{0,8},{8,0},{16,24},{24,16},{1,9},{9,1},{17,25},{25,17},{2,10},{10... | collective-permute-start | bytes 6291464 | tf_op jit(solution)/shard_map/ppermute | solution.py:715
  247.0 60.0 %collective-permute-start.27 = (bf16[512,2048]{1,0:T(8,128)(2,1)}, bf16[512,2048]{1,0:T(8,128)(2,1)}, u32[]{:S(2)}, u32[]{:S(2)}) collective-permute-start(bf16[512,2048]{1,0:T(8,128)(2,1)} %collective-permute-done.24), channel_id=1, source_target_pairs={{2,4},{3,5},{4,6},{5,7},{10,12},{11,13},{12,14},{13,15},{18,20},{1... | collective-permute-start | bytes 6291464 | tf_op jit(solution)/shard_map/ppermute | solution.py:746
  249.0 58.0 %collective-permute-start.28 = (bf16[512,2048]{1,0:T(8,128)(2,1)}, bf16[512,2048]{1,0:T(8,128)(2,1)}, u32[]{:S(2)}, u32[]{:S(2)}) collective-permute-start(bf16[512,2048]{1,0:T(8,128)(2,1)} %collective-permute-done.25), channel_id=1, source_target_pairs={{2,0},{3,1},{4,2},{5,3},{10,8},{11,9},{12,10},{13,11},{18,16},{19,... | collective-permute-start | bytes 6291464 | tf_op jit(solution)/shard_map/ppermute | solution.py:747
  312.1 61.0 %collective-permute-start.33 = (bf16[512,2048]{1,0:T(8,128)(2,1)}, bf16[512,2048]{1,0:T(8,128)(2,1)}, u32[]{:S(2)}, u32[]{:S(2)}) collective-permute-start(bf16[512,2048]{1,0:T(8,128)(2,1)} %collective-permute-done.27), channel_id=1, source_target_pairs={{4,6},{5,7},{12,14},{13,15},{20,22},{21,23},{28,30},{29,31}} | collective-permute-start | bytes 6291464 | tf_op jit(solution)/shard_map/ppermute | solution.py:746
  314.2 59.0 %collective-permute-start.34 = (bf16[512,2048]{1,0:T(8,128)(2,1)}, bf16[512,2048]{1,0:T(8,128)(2,1)}, u32[]{:S(2)}, u32[]{:S(2)}) collective-permute-start(bf16[512,2048]{1,0:T(8,128)(2,1)} %collective-permute-done.28), channel_id=1, source_target_pairs={{2,0},{3,1},{10,8},{11,9},{18,16},{19,17},{26,24},{27,25}} | collective-permute-start | bytes 6291464 | tf_op jit(solution)/shard_map/ppermute | solution.py:747
  317.5 64.1 %collective-permute-start.35 = (bf16[768,2048]{1,0:T(8,128)(2,1)}, bf16[768,2048]{1,0:T(8,128)(2,1)}, u32[]{:S(2)}, u32[]{:S(2)}) collective-permute-start(bf16[768,2048]{1,0:T(8,128)(2,1)} %slice.471), channel_id=1, source_target_pairs={{0,1},{1,0},{2,3},{3,2},{4,5},{5,4},{6,7},{7,6},{8,9},{9,8},{10,11... | collective-permute-start | bytes 9437192 | tf_op jit(solution)/shard_map/ppermute | solution.py:721
  409.9 61.1 %collective-permute-start.41 = (bf16[512,2048]{1,0:T(8,128)(2,1)}, bf16[512,2048]{1,0:T(8,128)(2,1)S(1)}, u32[]{:S(2)}, u32[]{:S(2)}) collective-permute-start(bf16[512,2048]{1,0:T(8,128)(2,1)} %get-tuple-element.365), channel_id=1, source_target_pairs={{0,8},{8,0},{16,24},{24,16},{1,9},{9,1},{17,25},{25,17},{2,10},{10... | collective-permute-start | bytes 6291464 | tf_op jit(solution)/shard_map/ppermute | solution.py:715
  409.9 61.1 %collective-permute-start.36 = (bf16[512,2048]{1,0:T(8,128)(2,1)S(1)}, bf16[512,2048]{1,0:T(8,128)(2,1)S(1)}, u32[]{:S(2)}, u32[]{:S(2)}) collective-permute-start(bf16[512,2048]{1,0:T(8,128)(2,1)S(1)} %copy-done.40), channel_id=1, source_target_pairs={{0,1},{1,0},{2,3},{3,2},{4,5},{5,4},{6,7},{7,6},{8,9},{9,8},{10,11... | collective-permute-start | bytes 6291464 | tf_op jit(solution)/shard_map/ppermute | solution.py:721
  418.2 52.0 %collective-permute-start.38 = (bf16[256,2048]{1,0:T(8,128)(2,1)}, bf16[256,2048]{1,0:T(8,128)(2,1)S(1)}, u32[]{:S(2)}, u32[]{:S(2)}) collective-permute-start(bf16[256,2048]{1,0:T(8,128)(2,1)} %get-tuple-element.508), channel_id=1, source_target_pairs={{0,4},{1,5},{2,6},{3,7},{4,0},{5,1},{6,2},{7,3},{8,12},{9,13},{10,... | collective-permute-start | bytes 3145736 | tf_op jit(solution)/shard_map/ppermute | solution.py:725
  423.8 47.1 %collective-permute-start.37 = (bf16[256,2048]{1,0:T(8,128)(2,1)}, bf16[256,2048]{1,0:T(8,128)(2,1)}, u32[]{:S(2)}, u32[]{:S(2)}) collective-permute-start(bf16[256,2048]{1,0:T(8,128)(2,1)} %get-tuple-element.509), channel_id=1, source_target_pairs={{0,2},{1,3},{2,0},{3,1},{4,6},{5,7},{6,4},{7,5},{8,10},{9,11},{10,... | collective-permute-start | bytes 3145736 | tf_op jit(solution)/shard_map/ppermute | solution.py:725
  518.4 53.9 %collective-permute-start.46 = (bf16[256,2048]{1,0:T(8,128)(2,1)}, bf16[256,2048]{1,0:T(8,128)(2,1)S(1)}, u32[]{:S(2)}, u32[]{:S(2)}) collective-permute-start(bf16[256,2048]{1,0:T(8,128)(2,1)} %add_convert_fusion.5), channel_id=1, source_target_pairs={{0,16},{8,24},{16,0},{24,8},{1,17},{9,25},{17,1},{25,9},{2,18},{10... | collective-permute-start | bytes 3145736 | tf_op jit(solution)/shard_map/ppermute | solution.py:718
  518.5 53.8 %collective-permute-start.45 = (bf16[256,2048]{1,0:T(8,128)(2,1)}, bf16[256,2048]{1,0:T(8,128)(2,1)}, u32[]{:S(2)}, u32[]{:S(2)}) collective-permute-start(bf16[256,2048]{1,0:T(8,128)(2,1)} %get-tuple-element.377), channel_id=1, source_target_pairs={{0,4},{1,5},{2,6},{3,7},{4,0},{5,1},{6,2},{7,3},{8,12},{9,13},{10,... | collective-permute-start | bytes 3145736 | tf_op jit(solution)/shard_map/ppermute | solution.py:725
  573.3 52.4 %collective-permute-start.51 = (bf16[1536,2048]{1,0:T(8,128)(2,1)}, bf16[1536,2048]{1,0:T(8,128)(2,1)S(1)}, u32[]{:S(2)}, u32[]{:S(2)}) collective-permute-start(bf16[1536,2048]{1,0:T(8,128)(2,1)} %get-tuple-element.410), channel_id=1, source_target_pairs={{0,8},{8,0},{16,24},{24,16},{1,9},{9,1},{17,25},{25,17},{2,10},{10... | collective-permute-start | bytes 18874376 | tf_op jit(solution)/shard_map/ppermute | solution.py:715
  578.7 46.9 %collective-permute-start.47 = (bf16[1024,1024]{1,0:T(8,128)(2,1)}, bf16[1024,1024]{1,0:T(8,128)(2,1)}, u32[]{:S(2)}, u32[]{:S(2)}) collective-permute-start(bf16[1024,1024]{1,0:T(8,128)(2,1)} %half_product.14), channel_id=1, source_target_pairs={{0,1},{1,0},{2,3},{3,2},{4,5},{5,4},{6,7},{7,6},{8,9},{9,8},{10,11... | collective-permute-start | bytes 6291464 | tf_op jit(solution)/shard_map/ppermute | solution.py:721
  627.1 62.2 %collective-permute-start.52 = (bf16[1024,512]{1,0:T(8,128)(2,1)}, bf16[1024,512]{1,0:T(8,128)(2,1)}, u32[]{:S(2)}, u32[]{:S(2)}) collective-permute-start(bf16[1024,512]{1,0:T(8,128)(2,1)} %half_product.16), channel_id=1, source_target_pairs={{0,1},{1,0},{2,3},{3,2},{4,5},{5,4},{6,7},{7,6},{8,9},{9,8},{10,11... | collective-permute-start | bytes 3145736 | tf_op jit(solution)/shard_map/ppermute | solution.py:721
  636.3 53.1 %collective-permute-start.57 = (bf16[256,2048]{1,0:T(8,128)(2,1)}, bf16[256,2048]{1,0:T(8,128)(2,1)}, u32[]{:S(2)}, u32[]{:S(2)}) collective-permute-start(bf16[256,2048]{1,0:T(8,128)(2,1)} %get-tuple-element.505), channel_id=1, source_target_pairs={{0,16},{8,24},{16,0},{24,8},{1,17},{9,25},{17,1},{25,9},{2,18},{10... | collective-permute-start | bytes 3145736 | tf_op jit(solution)/shard_map/ppermute | solution.py:718
  637.1 52.3 %collective-permute-start.56 = (bf16[256,2048]{1,0:T(8,128)(2,1)}, bf16[256,2048]{1,0:T(8,128)(2,1)}, u32[]{:S(2)}, u32[]{:S(2)}) collective-permute-start(bf16[256,2048]{1,0:T(8,128)(2,1)} %get-tuple-element.506), channel_id=1, source_target_pairs={{0,16},{8,24},{16,0},{24,8},{1,17},{9,25},{17,1},{25,9},{2,18},{10... | collective-permute-start | bytes 3145736 | tf_op jit(solution)/shard_map/ppermute | solution.py:718
  698.4 48.1 %collective-permute-start.59 = (bf16[1024,512]{1,0:T(8,128)(2,1)}, bf16[1024,512]{1,0:T(8,128)(2,1)S(1)}, u32[]{:S(2)}, u32[]{:S(2)}) collective-permute-start(bf16[1024,512]{1,0:T(8,128)(2,1)} %half_product.17), channel_id=1, source_target_pairs={{0,1},{1,0},{2,3},{3,2},{4,5},{5,4},{6,7},{7,6},{8,9},{9,8},{10,11... | collective-permute-start | bytes 3145736 | tf_op jit(solution)/shard_map/ppermute | solution.py:721
  790.0 56.1 %collective-permute-start.76 = (bf16[2,256,2048]{2,1,0:T(8,128)(2,1)S(1)}, bf16[2,256,2048]{2,1,0:T(8,128)(2,1)}, u32[]{:S(2)}, u32[]{:S(2)}) collective-permute-start(bf16[2,256,2048]{2,1,0:T(8,128)(2,1)S(1)} %copy-done.37), channel_id=1, source_target_pairs={{0,8},{8,0},{16,24},{24,16},{1,9},{9,1},{17,25},{25,17},{2,10},{10... | collective-permute-start | bytes 6291464 | tf_op jit(solution)/shard_map/ppermute | solution.py:715
  790.7 55.3 %collective-permute-start.75 = (bf16[2,256,2048]{2,1,0:T(8,128)(2,1)S(1)}, bf16[2,256,2048]{2,1,0:T(8,128)(2,1)}, u32[]{:S(2)}, u32[]{:S(2)}) collective-permute-start(bf16[2,256,2048]{2,1,0:T(8,128)(2,1)S(1)} %copy-done.37), channel_id=1, source_target_pairs={{0,16},{8,24},{16,0},{24,8},{1,17},{9,25},{17,1},{25,9},{2,18},{10... | collective-permute-start | bytes 6291464 | tf_op jit(solution)/shard_map/ppermute | solution.py:718
  (150 other events, 2595.8 us)

commit v5 on v4

--- a/solution.py
+++ b/solution.py
@@ -682,20 +682,23 @@
         copy_ref[at] = fresh.astype(jnp.bfloat16)
 
 
-def newton_update(gram, mom, master, rate):
+def newton_update(gram, mom, master, rate, first=0, pairs=None):
     count, rows, width = mom.shape
     step = 2
-    stack_block = pl.BlockSpec((step, rows, width), lambda at: (at, 0, 0))
+    pairs = count // step if pairs is None else pairs
+    shape = (pairs * step, rows, width)
+    stack_in = pl.BlockSpec((step, rows, width), lambda at: (first + at, 0, 0))
+    stack_out = pl.BlockSpec((step, rows, width), lambda at: (at, 0, 0))
     return pl.pallas_call(
         functools.partial(newton_kernel, rate=rate),
-        grid=(count // step,),
+        grid=(pairs,),
         in_specs=[
-            pl.BlockSpec((step, rows, rows), lambda at: (at, 0, 0)),
-            stack_block,
-            stack_block,
-        ],
-        out_specs=[stack_block, stack_block],
-        out_shape=[shaped(mom.shape, jnp.float32), shaped(mom.shape, jnp.bfloat16)],
+            pl.BlockSpec((step, rows, rows), lambda at: (first + at, 0, 0)),
+            stack_in,
+            stack_in,
+        ],
+        out_specs=[stack_out, stack_out],
+        out_shape=[shaped(shape, jnp.float32), shaped(shape, jnp.bfloat16)],
         compiler_params=kernel_params(),
         cost_estimate=cost_of(12),
         name="newton_update",
@@ -1213,10 +1216,17 @@
         attn_gram, small_sent, attn_mom, mlp_across, mlp_other
     )
 
-    attn_new, attn_low = newton_update(
-        attn_gram, attn_mom, attn_master, LR_MUON * 0.2 * math.sqrt(model_width)
-    )
-    attn_copy = links.gather_copies(attn_low, links.swap_y(attn_low), links.swap_core(attn_low))
+    attn_new, attn_copy = [], []
+    for pair in range(2):
+        fresh, attn_low = newton_update(
+            attn_gram, attn_mom, attn_master, LR_MUON * 0.2 * math.sqrt(model_width), pair, 1
+        )
+        attn_new.append(fresh)
+        attn_copy.append(
+            links.gather_copies(attn_low, links.swap_y(attn_low), links.swap_core(attn_low))
+        )
+    attn_new = jnp.concatenate(attn_new, 0)
+    attn_copy = jnp.concatenate(attn_copy, 0)
     mlp_copy = links.gather_copies(mlp_low, mlp_across, mlp_other)
     small_sent, attn_low = fence(small_sent, attn_low)
     small = lax.all_to_all(small_sent, "fsdp", 0, 0, tiled=True)

time: 924 us -> 912 us (0.987)
  waiting for transfers between devices: 244 us -> 234 us
    all_to_all x1, waiting for transfers between devices: 13 us -> 0.01 us  [body(): small = lax.all_to_all(small_sent, 'fsdp', 0, 0, tiled=True)]
    ppermute x16 -> x17, waiting for transfers between devices: 51.4 us -> 55.1 us  [swap_y(): return lax.ppermute(values, 'dp', [(at, at ^ 2) for at in range(4)])]
    pallas_call x2 -> x3, Pallas kernels: 41.9 us -> 44.6 us  [newton_update(): pl.pallas_call(functools.partial(newton_kernel, rate=rate), grid=(pairs,)...]
    ppermute x21 -> x23, starting transfers between devices: 41.5 us -> 41.5 us  [swap_core(): return lax.ppermute(values, 'dp', [(at, at ^ 1) for at in range(4)])]
    unnamed x200 -> x206, local copies, waits for them, and re-layouts: 40.7 us -> 40.7 us
  transfers between devices with their start and end apart: 85 -> 88, of which waited for: 29 -> 29; matrix products, arithmetic and copies ran while one was open for 18% -> 19% of each run, Pallas kernels for 31% -> 33%
where the time goes in v5:
time: 912 us; the launch traced here: 900 us
  Pallas kernels  322 us (35%)
  waiting for transfers between devices  234 us (26%)
  starting transfers between devices  126 us (14%)
  other arithmetic  113 us (12%)
  local copies, waits for them, and re-layouts  102 us (11%)
    pallas_call x10, Pallas kernels, half_product(): pl.pallas_call(grad_kernel, grid=(steps, columns // col_tile), in_specs=[...  73.7 us
    ppermute x15, waiting for transfers between devices, swap_z(): return lax.ppermute(values, 'fsdp', pairs)  69.3 us
    ppermute x9, waiting for transfers between devices, hop(): lax.ppermute(fall[-1], 'fsdp', down_pairs)  64.4 us
    ppermute x17, waiting for transfers between devices, swap_y(): return lax.ppermute(values, 'dp', [(at, at ^ 2) for at in range(4)])  55.1 us
    pallas_call x4, Pallas kernels, product_rows(): pl.pallas_call(rows_kernel, grid_spec=pltpu.PrefetchScalarGridSpec(num_sc...  49.5 us
    pallas_call x3, Pallas kernels, newton_update(): pl.pallas_call(functools.partial(newton_kernel, rate=rate), grid=(pairs,)...  44.6 us
    ppermute x23, starting transfers between devices, swap_core(): return lax.ppermute(values, 'dp', [(at, at ^ 1) for at in range(4)])  41.5 us
    unnamed x206, local copies, waits for them, and re-layouts  40.7 us
  transfers between devices with their start and end apart: 88, of which 29 were waited for; matrix products, arithmetic and copies ran while one was open for 19% of the time, Pallas kernels for 33%

profile of v5, /device:TPU:1, one launch (start us, length us, event | category | flops | bytes accessed | tf_op | source)
XLA Modules:
  0.0 900.4 jit_solution(12945026924295017260)
XLA Ops:
  46.9 18.4 %mix_forward.1 = (bf16[256,2048]{1,0:T(8,128)(2,1)}, bf16[256,2048]{1,0:T(8,128)(2,1)}, bf16[256,2048]{1,0:T(8,128)(2,1)}, bf16[256,2048]{1,0:T(8,128)(2,1)}, f3...) custom-call(bf16[9,256,2048]{2,1,0:T(8,128)(2,1)} %hist_ref.3, ...), custom_call_target="tpu_custom_call" | custom-call | flops 1035000000 | bytes 3321000 | tf_op jit(solution)/shard_map/mix_forward/pallas_call | solution.py:297
  86.2 14.5 %collective-permute-done.10 = bf16[256,2048]{1,0:T(8,128)(2,1)S(1)} collective-permute-done((bf16[256,2048]{1,0:T(8,128)(2,1)S(1)}, bf16[256,2048]{1,0:T(8,128)(2,1)S(1)}, u32[]{:S(2)}, u32[]{:S(2)}) %collective-permute-start.10) | collective-permute-done | bytes 1048608 | tf_op jit(solution)/shard_map/ppermute | solution.py:750
  105.2 18.0 %collective-permute-done.12 = bf16[256,2048]{1,0:T(8,128)(2,1)} collective-permute-done((bf16[256,2048]{1,0:T(8,128)(2,1)S(1)}, bf16[256,2048]{1,0:T(8,128)(2,1)}, u32[]{:S(2)}, u32[]{:S(2)}) %collective-permute-start.12) | collective-permute-done | bytes 1048608 | tf_op jit(solution)/shard_map/ppermute | solution.py:750
  142.0 22.2 %collective-permute-done.18 = bf16[256,2048]{1,0:T(8,128)(2,1)S(1)} collective-permute-done((bf16[256,2048]{1,0:T(8,128)(2,1)}, bf16[256,2048]{1,0:T(8,128)(2,1)S(1)}, u32[]{:S(2)}, u32[]{:S(2)}) %collective-permute-start.18) | collective-permute-done | bytes 1048608 | tf_op jit(solution)/shard_map/ppermute | solution.py:750
  222.9 17.4 %mlp_up.1 = (bf16[1024,2048]{1,0:T(8,128)(2,1)}, f32[1024,2048]{1,0:T(8,128)}) custom-call(bf16[1024,2048]{1,0:T(8,128)(2,1)} %pad_maximum_fusion.2.normed_ref.left_refs_0_, bf16[2048,2048]{1,0:T(8,128)(2,1)} %constant_dynamic-update-slice_fusion.up_ref.right_refs_0__0_.right_refs_0__1_, f32[1,2048]{1,0:T(1,128)} %get-tuple-element.636.bias_ref), custom_call_target="tpu_custom_call" | custom-call | flops 977500032 | bytes 3136500 | tf_op jit(solution)/shard_map/mlp_up/pallas_call | solution.py:478
  256.0 10.8 %half_product.10 = bf16[1024,2048]{1,0:T(8,128)(2,1)} custom-call(bf16[1024,2048]{1,0:T(8,128)(2,1)} %pad_maximum_fusion.1.left_refs_0_.cot_ref.refs_0_, bf16[1024,2048]{1,0:T(8,128)(2,1)} %get-tuple-element.413.right_refs_0_.left_refs_0_), custom_call_target="tpu_custom_call" | custom-call | flops 632499968 | bytes 2029500 | tf_op jit(solution)/shard_map/half_product/pallas_call | solution.py:240
  273.6 11.9 %half_product.12 = f32[1024,2048]{1,0:T(8,128)} custom-call(bf16[1024,2048]{1,0:T(8,128)(2,1)} %pad_maximum_fusion.1.left_refs_0_.cot_ref.refs_0_, bf16[1024,2048]{1,0:T(8,128)(2,1)} %get-tuple-element.413.right_refs_0_.left_refs_0_), custom_call_target="tpu_custom_call" | custom-call | flops 632499968 | bytes 2029500 | tf_op jit(solution)/shard_map/half_product/pallas_call | solution.py:240
  311.9 15.9 %mlp_back.1 = (bf16[1024,2048]{1,0:T(8,128)(2,1)}, f32[1,2048]{1,0:T(1,128)}) custom-call(bf16[1024,2048]{1,0:T(8,128)(2,1)} %pad_maximum_fusion.1.left_refs_0_.cot_ref.refs_0_, bf16[2048,2048]{1,0:T(8,128)(2,1)} %constant_dynamic-update-slice_fusion.6.down_ref.right_refs_0__0_.right_refs_0__1_, f32[1024,2048]{1,0:T(8,128)} %get-tuple-element.343.slope_ref), custom_call_target="tpu_custom_call" | custom-call | flops 920000000 | bytes 2952000 | tf_op jit(solution)/shard_map/mlp_back/pallas_call | solution.py:514
  327.8 10.8 %half_product.11 = bf16[1024,2048]{1,0:T(8,128)(2,1)} custom-call(bf16[1024,2048]{1,0:T(8,128)(2,1)} %pad_maximum_fusion.2.normed_ref.left_refs_0_, bf16[1024,2048]{1,0:T(8,128)(2,1)} %get-tuple-element.366.right_refs_0_.left_refs_0_), custom_call_target="tpu_custom_call" | custom-call | flops 632499968 | bytes 2029500 | tf_op jit(solution)/shard_map/half_product/pallas_call | solution.py:240
  338.6 14.3 %product_rows.4 = (f32[512,2048]{1,0:T(8,128)}, bf16[512,2048]{1,0:T(8,128)(2,1)}) custom-call(s32[8]{0:T(128)} %stack.142.order_ref, bf16[1024,2048]{1,0:T(8,128)(2,1)} %get-tuple-element.366.right_refs_0_.left_refs_0_, bf16[2048,2048]{1,0:T(8,128)(2,1)} %constant_dynamic-update-slice_fusion.up_ref.right_refs_0__0_.right_refs_0__1_, ...), custom_call_target="tpu_custom_call" | custom-call | flops 805000000 | bytes 2583000 | tf_op jit(solution)/shard_map/product_rows/pallas_call | solution.py:204
  414.9 12.3 %half_product.13 = f32[1024,2048]{1,0:T(8,128)} custom-call(bf16[1024,2048]{1,0:T(8,128)(2,1)} %pad_maximum_fusion.2.normed_ref.left_refs_0_, bf16[1024,2048]{1,0:T(8,128)(2,1)} %get-tuple-element.366.right_refs_0_.left_refs_0_), custom_call_target="tpu_custom_call" | custom-call | flops 632499968 | bytes 2029500 | tf_op jit(solution)/shard_map/half_product/pallas_call | solution.py:240
  431.1 29.9 %collective-permute-done.38.part_refs_1__2_ = bf16[256,2048]{1,0:T(8,128)(2,1)S(1)} collective-permute-done((bf16[256,2048]{1,0:T(8,128)(2,1)}, bf16[256,2048]{1,0:T(8,128)(2,1)S(1)}, u32[]{:S(2)}, u32[]{:S(2)}) %collective-permute-start.38) | collective-permute-done | bytes 1048608 | tf_op jit(solution)/shard_map/ppermute | solution.py:728
  467.9 19.7 %collective-permute-done.44 = bf16[1024,512]{1,0:T(8,128)(2,1)S(1)} collective-permute-done((bf16[1024,512]{1,0:T(8,128)(2,1)S(1)}, bf16[1024,512]{1,0:T(8,128)(2,1)S(1)}, u32[]{:S(2)}, u32[]{:S(2)}) %collective-permute-start.44) | collective-permute-done | bytes 1048608 | tf_op jit(solution)/shard_map/ppermute | solution.py:721
  489.4 18.8 %collective-permute-done.42 = bf16[512,2048]{1,0:T(8,128)(2,1)S(1)} collective-permute-done((bf16[512,2048]{1,0:T(8,128)(2,1)S(1)}, bf16[512,2048]{1,0:T(8,128)(2,1)S(1)}, u32[]{:S(2)}, u32[]{:S(2)}) %collective-permute-start.42) | collective-permute-done | bytes 2097184 | tf_op jit(solution)/shard_map/ppermute | solution.py:724
  516.0 27.1 %attention_inner.1 = (bf16[1024,512]{1,0:T(8,128)(2,1)}, bf16[1024,512]{1,0:T(8,128)(2,1)}, bf16[1024,512]{1,0:T(8,128)(2,1)}, bf16[1024,512]{1,0:T(8,128)(2,1)}, f32[8,512]{1,0:T(8,128)}) custom-call(s32[4,3]{1,0:T(4,128)} %reduce_window_sum.18.ends_ref, bf16[1024,2048]{1,0:T(8,128)(2,1)} %pad_maximum_fusion.4.normed_refs_0_.left_refs_1_, ...), custom_call_target="tpu_custom_call" | custom-call | flops 1552499968 | bytes 4981500 | tf_op jit(solution)/shard_map/attention_inner/pallas_call | solution.py:601
  548.8 13.4 %product_rows.6 = (f32[1536,2048]{1,0:T(8,128)}, bf16[1536,2048]{1,0:T(8,128)(2,1)}) custom-call(s32[8]{0:T(128)} %stack.142.order_ref, bf16[1024,512]{1,0:T(8,128)(2,1)} %get-tuple-element.408.right_refs_0_.left_refs_0_, bf16[1024,512]{1,0:T(8,128)(2,1)} %get-tuple-element.409.right_refs_1_.left_refs_1_, ...), custom_call_target="tpu_custom_call" | custom-call | flops 805000000 | bytes 2583000 | tf_op jit(solution)/shard_map/product_rows/pallas_call | solution.py:204
  574.8 14.5 %product_rows.7 = (f32[512,2048]{1,0:T(8,128)}, f32[512,2048]{1,0:T(8,128)}) custom-call(s32[8]{0:T(128)} %stack.142.order_ref, bf16[1024,2048]{1,0:T(8,128)(2,1)} %get-tuple-element.413.right_refs_0_.left_refs_0_, bf16[2048,2048]{1,0:T(8,128)(2,1)} %constant_dynamic-update-slice_fusion.6.down_ref.right_refs_0__0_.right_refs_0__1_, ...), custom_call_target="tpu_custom_call" | custom-call | flops 10350000128 | bytes 33210000 | tf_op jit(solution)/shard_map/product_rows/pallas_call | solution.py:204
  603.6 12.4 %collective-permute-done.49.part_refs_0__3_ = bf16[256,2048]{1,0:T(8,128)(2,1)} collective-permute-done((bf16[256,2048]{1,0:T(8,128)(2,1)}, bf16[256,2048]{1,0:T(8,128)(2,1)}, u32[]{:S(2)}, u32[]{:S(2)}) %collective-permute-start.49) | collective-permute-done | bytes 1048608 | tf_op jit(solution)/shard_map/ppermute | solution.py:728
  666.1 14.3 %collective-permute-done.53 = bf16[256,1024]{1,0:T(8,128)(2,1)} collective-permute-done((bf16[256,1024]{1,0:T(8,128)(2,1)S(1)}, bf16[256,1024]{1,0:T(8,128)(2,1)}, u32[]{:S(2)}, u32[]{:S(2)}) %collective-permute-start.53) | collective-permute-done | bytes 524320 | tf_op jit(solution)/shard_map/ppermute | solution.py:728
  706.2 14.1 %collective-permute-done.64 = f32[1,256,256]{2,1,0:T(8,128)S(1)} collective-permute-done((f32[1,256,256]{2,1,0:T(8,128)S(1)}, f32[1,256,256]{2,1,0:T(8,128)S(1)}, u32[]{:S(2)}, u32[]{:S(2)}) %collective-permute-start.64) | collective-permute-done | bytes 262176 | tf_op jit(solution)/shard_map/ppermute | solution.py:721
  743.8 19.1 %newton_update.3 = (f32[2,256,2048]{2,1,0:T(8,128)}, bf16[2,256,2048]{2,1,0:T(8,128)(2,1)}) custom-call(f32[2,256,256]{2,1,0:T(8,128)} %pad_maximum_fusion.19.gram_ref, f32[2,256,2048]{2,1,0:T(8,128)} %get-tuple-element.248.mom_ref, f32[2,256,2048]{2,1,0:T(8,128)} %master_ref.3), custom_call_target="tpu_custom_call" | custom-call | flops 13799999488 | bytes 44280000 | tf_op jit(solution)/shard_map/newton_update/pallas_call | solution.py:692
  793.9 34.4 %mix_backward.1 = (bf16[9,256,2048]{2,1,0:T(8,128)(2,1)}, f32[16,2048]{1,0:T(8,128)}, f32[36,2048]{1,0:T(8,128)}, f32[37,36]{1,0:T(8,128)}) custom-call(bf16[9,256,2048]{2,1,0:T(8,128)(2,1)} %hist_ref.3, bf16[256,2048]{1,0:T(8,128)(2,1)} %cot_ref.1, f32[256,1]{1,0:T(8,128)} %copy.51.tok_ref, ...), custom_call_target="tpu_custom_call" | custom-call | flops 21849999360 | bytes 70110000 | tf_op jit(solution)/shard_map/mix_backward/pallas_call | solution.py:422
  837.4 12.7 %newton_update.5 = (f32[2,256,512]{2,1,0:T(8,128)}, bf16[2,256,512]{2,1,0:T(8,128)(2,1)}) custom-call(f32[4,256,256]{2,1,0:T(8,128)} %pad_maximum_fusion.18.gram_ref, f32[4,256,512]{2,1,0:T(8,128)} %get-tuple-element.244.mom_ref, f32[4,256,512]{2,1,0:T(8,128)} %master_ref.5), custom_call_target="tpu_custom_call" | custom-call | flops 13799999488 | bytes 44280000 | tf_op jit(solution)/shard_map/newton_update/pallas_call | solution.py:692
  853.8 12.8 %newton_update.4 = (f32[2,256,512]{2,1,0:T(8,128)}, bf16[2,256,512]{2,1,0:T(8,128)(2,1)}) custom-call(f32[4,256,256]{2,1,0:T(8,128)} %pad_maximum_fusion.18.gram_ref, f32[4,256,512]{2,1,0:T(8,128)} %get-tuple-element.244.mom_ref, f32[4,256,512]{2,1,0:T(8,128)} %master_ref.5), custom_call_target="tpu_custom_call" | custom-call | flops 13799999488 | bytes 44280000 | tf_op jit(solution)/shard_map/newton_update/pallas_call | solution.py:692
  (534 shorter events, 488.5 us)
Async XLA Ops:
  131.8 47.2 %collective-permute-start.23 = (bf16[512,2048]{1,0:T(8,128)(2,1)}, bf16[512,2048]{1,0:T(8,128)(2,1)}, u32[]{:S(2)}, u32[]{:S(2)}) collective-permute-start(bf16[512,2048]{1,0:T(8,128)(2,1)} %get-tuple-element.299), channel_id=1, source_target_pairs={{0,16},{8,24},{16,0},{24,8},{1,17},{9,25},{17,1},{25,9},{2,18},{10... | collective-permute-start | bytes 6291464 | tf_op jit(solution)/shard_map/ppermute | solution.py:721
  173.0 99.4 %collective-permute-start.31 = (bf16[512,2048]{1,0:T(8,128)(2,1)}, bf16[512,2048]{1,0:T(8,128)(2,1)}, u32[]{:S(2)}, u32[]{:S(2)}) collective-permute-start(bf16[512,2048]{1,0:T(8,128)(2,1)} %get-tuple-element.299), channel_id=1, source_target_pairs={{0,8},{8,0},{16,24},{24,16},{1,9},{9,1},{17,25},{25,17},{2,10},{10... | collective-permute-start | bytes 6291464 | tf_op jit(solution)/shard_map/ppermute | solution.py:718
  191.1 56.0 %collective-permute-start.25 = (bf16[512,2048]{1,0:T(8,128)(2,1)S(1)}, bf16[512,2048]{1,0:T(8,128)(2,1)}, u32[]{:S(2)}, u32[]{:S(2)}) collective-permute-start(bf16[512,2048]{1,0:T(8,128)(2,1)S(1)} %pad_maximum_fusion.10), channel_id=1, source_target_pairs={{2,0},{3,1},{4,2},{5,3},{6,4},{7,5},{10,8},{11,9},{12,10},{13,11},... | collective-permute-start | bytes 6291464 | tf_op jit(solution)/shard_map/ppermute | solution.py:750
  192.4 54.7 %collective-permute-start.24 = (bf16[512,2048]{1,0:T(8,128)(2,1)S(1)}, bf16[512,2048]{1,0:T(8,128)(2,1)}, u32[]{:S(2)}, u32[]{:S(2)}) collective-permute-start(bf16[512,2048]{1,0:T(8,128)(2,1)S(1)} %pad_maximum_fusion.10), channel_id=1, source_target_pairs={{0,2},{1,3},{2,4},{3,5},{4,6},{5,7},{8,10},{9,11},{10,12},{11,13},... | collective-permute-start | bytes 6291464 | tf_op jit(solution)/shard_map/ppermute | solution.py:749
  204.9 87.2 %collective-permute-start.32 = (bf16[512,2048]{1,0:T(8,128)(2,1)}, bf16[512,2048]{1,0:T(8,128)(2,1)}, u32[]{:S(2)}, u32[]{:S(2)}) collective-permute-start(bf16[512,2048]{1,0:T(8,128)(2,1)} %collective-permute-done.23), channel_id=1, source_target_pairs={{0,8},{8,0},{16,24},{24,16},{1,9},{9,1},{17,25},{25,17},{2,10},{10... | collective-permute-start | bytes 6291464 | tf_op jit(solution)/shard_map/ppermute | solution.py:718
  247.0 50.9 %collective-permute-start.27 = (bf16[512,2048]{1,0:T(8,128)(2,1)}, bf16[512,2048]{1,0:T(8,128)(2,1)}, u32[]{:S(2)}, u32[]{:S(2)}) collective-permute-start(bf16[512,2048]{1,0:T(8,128)(2,1)} %collective-permute-done.24), channel_id=1, source_target_pairs={{2,4},{3,5},{4,6},{5,7},{10,12},{11,13},{12,14},{13,15},{18,20},{1... | collective-permute-start | bytes 6291464 | tf_op jit(solution)/shard_map/ppermute | solution.py:749
  249.1 48.9 %collective-permute-start.28 = (bf16[512,2048]{1,0:T(8,128)(2,1)}, bf16[512,2048]{1,0:T(8,128)(2,1)}, u32[]{:S(2)}, u32[]{:S(2)}) collective-permute-start(bf16[512,2048]{1,0:T(8,128)(2,1)} %collective-permute-done.25), channel_id=1, source_target_pairs={{2,0},{3,1},{4,2},{5,3},{10,8},{11,9},{12,10},{13,11},{18,16},{19,... | collective-permute-start | bytes 6291464 | tf_op jit(solution)/shard_map/ppermute | solution.py:750
  303.1 61.0 %collective-permute-start.33 = (bf16[512,2048]{1,0:T(8,128)(2,1)}, bf16[512,2048]{1,0:T(8,128)(2,1)}, u32[]{:S(2)}, u32[]{:S(2)}) collective-permute-start(bf16[512,2048]{1,0:T(8,128)(2,1)} %collective-permute-done.27), channel_id=1, source_target_pairs={{4,6},{5,7},{12,14},{13,15},{20,22},{21,23},{28,30},{29,31}} | collective-permute-start | bytes 6291464 | tf_op jit(solution)/shard_map/ppermute | solution.py:749
  305.1 59.0 %collective-permute-start.34 = (bf16[512,2048]{1,0:T(8,128)(2,1)}, bf16[512,2048]{1,0:T(8,128)(2,1)}, u32[]{:S(2)}, u32[]{:S(2)}) collective-permute-start(bf16[512,2048]{1,0:T(8,128)(2,1)} %collective-permute-done.28), channel_id=1, source_target_pairs={{2,0},{3,1},{10,8},{11,9},{18,16},{19,17},{26,24},{27,25}} | collective-permute-start | bytes 6291464 | tf_op jit(solution)/shard_map/ppermute | solution.py:750
  308.4 64.1 %collective-permute-start.35 = (bf16[768,2048]{1,0:T(8,128)(2,1)}, bf16[768,2048]{1,0:T(8,128)(2,1)}, u32[]{:S(2)}, u32[]{:S(2)}) collective-permute-start(bf16[768,2048]{1,0:T(8,128)(2,1)} %slice.471), channel_id=1, source_target_pairs={{0,1},{1,0},{2,3},{3,2},{4,5},{5,4},{6,7},{7,6},{8,9},{9,8},{10,11... | collective-permute-start | bytes 9437192 | tf_op jit(solution)/shard_map/ppermute | solution.py:724
  400.9 61.2 %collective-permute-start.41 = (bf16[512,2048]{1,0:T(8,128)(2,1)}, bf16[512,2048]{1,0:T(8,128)(2,1)S(1)}, u32[]{:S(2)}, u32[]{:S(2)}) collective-permute-start(bf16[512,2048]{1,0:T(8,128)(2,1)} %get-tuple-element.367), channel_id=1, source_target_pairs={{0,8},{8,0},{16,24},{24,16},{1,9},{9,1},{17,25},{25,17},{2,10},{10... | collective-permute-start | bytes 6291464 | tf_op jit(solution)/shard_map/ppermute | solution.py:718
  400.9 61.2 %collective-permute-start.36 = (bf16[512,2048]{1,0:T(8,128)(2,1)S(1)}, bf16[512,2048]{1,0:T(8,128)(2,1)S(1)}, u32[]{:S(2)}, u32[]{:S(2)}) collective-permute-start(bf16[512,2048]{1,0:T(8,128)(2,1)S(1)} %copy-done.40), channel_id=1, source_target_pairs={{0,1},{1,0},{2,3},{3,2},{4,5},{5,4},{6,7},{7,6},{8,9},{9,8},{10,11... | collective-permute-start | bytes 6291464 | tf_op jit(solution)/shard_map/ppermute | solution.py:724
  409.1 51.9 %collective-permute-start.38 = (bf16[256,2048]{1,0:T(8,128)(2,1)}, bf16[256,2048]{1,0:T(8,128)(2,1)S(1)}, u32[]{:S(2)}, u32[]{:S(2)}) collective-permute-start(bf16[256,2048]{1,0:T(8,128)(2,1)} %get-tuple-element.512), channel_id=1, source_target_pairs={{0,4},{1,5},{2,6},{3,7},{4,0},{5,1},{6,2},{7,3},{8,12},{9,13},{10,... | collective-permute-start | bytes 3145736 | tf_op jit(solution)/shard_map/ppermute | solution.py:728
  414.9 47.2 %collective-permute-start.37 = (bf16[256,2048]{1,0:T(8,128)(2,1)}, bf16[256,2048]{1,0:T(8,128)(2,1)}, u32[]{:S(2)}, u32[]{:S(2)}) collective-permute-start(bf16[256,2048]{1,0:T(8,128)(2,1)} %get-tuple-element.513), channel_id=1, source_target_pairs={{0,2},{1,3},{2,0},{3,1},{4,6},{5,7},{6,4},{7,5},{8,10},{9,11},{10,... | collective-permute-start | bytes 3145736 | tf_op jit(solution)/shard_map/ppermute | solution.py:728
  509.5 53.9 %collective-permute-start.46 = (bf16[256,2048]{1,0:T(8,128)(2,1)}, bf16[256,2048]{1,0:T(8,128)(2,1)S(1)}, u32[]{:S(2)}, u32[]{:S(2)}) collective-permute-start(bf16[256,2048]{1,0:T(8,128)(2,1)} %add_convert_fusion.5), channel_id=1, source_target_pairs={{0,16},{8,24},{16,0},{24,8},{1,17},{9,25},{17,1},{25,9},{2,18},{10... | collective-permute-start | bytes 3145736 | tf_op jit(solution)/shard_map/ppermute | solution.py:721
  509.5 53.8 %collective-permute-start.45 = (bf16[256,2048]{1,0:T(8,128)(2,1)}, bf16[256,2048]{1,0:T(8,128)(2,1)}, u32[]{:S(2)}, u32[]{:S(2)}) collective-permute-start(bf16[256,2048]{1,0:T(8,128)(2,1)} %get-tuple-element.379), channel_id=1, source_target_pairs={{0,4},{1,5},{2,6},{3,7},{4,0},{5,1},{6,2},{7,3},{8,12},{9,13},{10,... | collective-permute-start | bytes 3145736 | tf_op jit(solution)/shard_map/ppermute | solution.py:728
  564.4 52.4 %collective-permute-start.51 = (bf16[1536,2048]{1,0:T(8,128)(2,1)}, bf16[1536,2048]{1,0:T(8,128)(2,1)S(1)}, u32[]{:S(2)}, u32[]{:S(2)}) collective-permute-start(bf16[1536,2048]{1,0:T(8,128)(2,1)} %get-tuple-element.412), channel_id=1, source_target_pairs={{0,8},{8,0},{16,24},{24,16},{1,9},{9,1},{17,25},{25,17},{2,10},{10... | collective-permute-start | bytes 18874376 | tf_op jit(solution)/shard_map/ppermute | solution.py:718
  569.8 46.9 %collective-permute-start.47 = (bf16[1024,1024]{1,0:T(8,128)(2,1)}, bf16[1024,1024]{1,0:T(8,128)(2,1)}, u32[]{:S(2)}, u32[]{:S(2)}) collective-permute-start(bf16[1024,1024]{1,0:T(8,128)(2,1)} %half_product.14), channel_id=1, source_target_pairs={{0,1},{1,0},{2,3},{3,2},{4,5},{5,4},{6,7},{7,6},{8,9},{9,8},{10,11... | collective-permute-start | bytes 6291464 | tf_op jit(solution)/shard_map/ppermute | solution.py:724
  618.2 62.2 %collective-permute-start.52 = (bf16[1024,512]{1,0:T(8,128)(2,1)}, bf16[1024,512]{1,0:T(8,128)(2,1)}, u32[]{:S(2)}, u32[]{:S(2)}) collective-permute-start(bf16[1024,512]{1,0:T(8,128)(2,1)} %half_product.16), channel_id=1, source_target_pairs={{0,1},{1,0},{2,3},{3,2},{4,5},{5,4},{6,7},{7,6},{8,9},{9,8},{10,11... | collective-permute-start | bytes 3145736 | tf_op jit(solution)/shard_map/ppermute | solution.py:724
  627.4 53.0 %collective-permute-start.57 = (bf16[256,2048]{1,0:T(8,128)(2,1)}, bf16[256,2048]{1,0:T(8,128)(2,1)}, u32[]{:S(2)}, u32[]{:S(2)}) collective-permute-start(bf16[256,2048]{1,0:T(8,128)(2,1)} %get-tuple-element.509), channel_id=1, source_target_pairs={{0,16},{8,24},{16,0},{24,8},{1,17},{9,25},{17,1},{25,9},{2,18},{10... | collective-permute-start | bytes 3145736 | tf_op jit(solution)/shard_map/ppermute | solution.py:721
  628.2 52.2 %collective-permute-start.56 = (bf16[256,2048]{1,0:T(8,128)(2,1)}, bf16[256,2048]{1,0:T(8,128)(2,1)}, u32[]{:S(2)}, u32[]{:S(2)}) collective-permute-start(bf16[256,2048]{1,0:T(8,128)(2,1)} %get-tuple-element.510), channel_id=1, source_target_pairs={{0,16},{8,24},{16,0},{24,8},{1,17},{9,25},{17,1},{25,9},{2,18},{10... | collective-permute-start | bytes 3145736 | tf_op jit(solution)/shard_map/ppermute | solution.py:721
  689.4 48.1 %collective-permute-start.59 = (bf16[1024,512]{1,0:T(8,128)(2,1)}, bf16[1024,512]{1,0:T(8,128)(2,1)S(1)}, u32[]{:S(2)}, u32[]{:S(2)}) collective-permute-start(bf16[1024,512]{1,0:T(8,128)(2,1)} %half_product.17), channel_id=1, source_target_pairs={{0,1},{1,0},{2,3},{3,2},{4,5},{5,4},{6,7},{7,6},{8,9},{9,8},{10,11... | collective-permute-start | bytes 3145736 | tf_op jit(solution)/shard_map/ppermute | solution.py:724
  781.1 56.3 %collective-permute-start.76 = (bf16[2,256,2048]{2,1,0:T(8,128)(2,1)S(1)}, bf16[2,256,2048]{2,1,0:T(8,128)(2,1)}, u32[]{:S(2)}, u32[]{:S(2)}) collective-permute-start(bf16[2,256,2048]{2,1,0:T(8,128)(2,1)S(1)} %copy-done.37), channel_id=1, source_target_pairs={{0,8},{8,0},{16,24},{24,16},{1,9},{9,1},{17,25},{25,17},{2,10},{10... | collective-permute-start | bytes 6291464 | tf_op jit(solution)/shard_map/ppermute | solution.py:718
  781.8 55.5 %collective-permute-start.75 = (bf16[2,256,2048]{2,1,0:T(8,128)(2,1)S(1)}, bf16[2,256,2048]{2,1,0:T(8,128)(2,1)}, u32[]{:S(2)}, u32[]{:S(2)}) collective-permute-start(bf16[2,256,2048]{2,1,0:T(8,128)(2,1)S(1)} %copy-done.37), channel_id=1, source_target_pairs={{0,16},{8,24},{16,0},{24,8},{1,17},{9,25},{17,1},{25,9},{2,18},{10... | collective-permute-start | bytes 6291464 | tf_op jit(solution)/shard_map/ppermute | solution.py:721
  (156 other events, 2548.3 us)

commit v6 on v5

--- a/solution.py
+++ b/solution.py
@@ -1021,14 +1021,11 @@
     context_sent = context_sum[1] + wide(links.swap_core(sent[:, attn_cols:]))
     context_sent = turn_y(low(context_sent))
     context_own = context_sum[0] + wide(links.swap_core(sent[:, :attn_cols]))
-    three_arrived = links.swap_core(three_sent)
     up_own_sum = half_product([group_normed[3]], [up_grad], 0)
     (
         up_last, down_summed, down_parts, full_attn, context_sent, context_own, up_sent, up_own_sum,
-        three_arrived,
     ) = fence(
         up_last, down_summed, down_parts, full_attn, context_sent, context_own, up_sent, up_own_sum,
-        three_arrived,
     )
 
     def halves(near, arrived):
@@ -1042,16 +1039,17 @@
     last_turns = range(half_depth, depth)
     up_arrived = [None] * half_depth + cut(up_last, (rows,) * half_depth)
     up_summed = [None] * half_depth + slot_sums(up_own_sum, up_arrived, last_turns)
-    three_sent = low(three_near[tok_count:] + wide(three_arrived[tok_count:]))
+    three_arrived = links.swap_core(three_sent)
     context_grad = low(context_own + wide(context_y))
     (
-        up_first, down_parts, context_grad, up_summed, up_own_sum, three_sent,
+        up_first, down_parts, context_grad, up_summed, up_own_sum, three_arrived,
     ) = fence(
-        up_first, down_parts, context_grad, up_summed, up_own_sum, three_sent,
+        up_first, down_parts, context_grad, up_summed, up_own_sum, three_arrived,
     )
 
     up_parts = [links.swap_z(up_summed[turn], turn) for turn in list(last_turns)[:-1]]
-    three_y = links.swap_y(three_sent)
+    three_y = low(three_near[tok_count:] + wide(three_arrived[tok_count:]))
+    three_y = links.swap_y(three_y)
     attn_bias = lax.dynamic_slice(param_vals, (8, member * attn_cols), (3, attn_cols))
     context_low, proj_grads, proj_sums = attention_inner(
         jnp.cumsum(group_lengths, 1),

time: 912 us -> 913 us (level)
    unnamed x206 -> x202, local copies, waits for them, and re-layouts: 40.7 us -> 39.5 us
  transfers between devices with their start and end apart: 88 -> 88, of which waited for: 29 -> 28; matrix products, arithmetic and copies ran while one was open for 19% -> 19% of each run, Pallas kernels for 33% -> 33%
where the time goes in v6:
time: 913 us; the launch traced here: 901 us
  Pallas kernels  321 us (35%)
  waiting for transfers between devices  234 us (26%)
  starting transfers between devices  127 us (14%)
  other arithmetic  114 us (12%)
  local copies, waits for them, and re-layouts  100 us (11%)
    pallas_call x10, Pallas kernels, half_product(): pl.pallas_call(grad_kernel, grid=(steps, columns // col_tile), in_specs=[...  73.6 us
    ppermute x15, waiting for transfers between devices, swap_z(): return lax.ppermute(values, 'fsdp', pairs)  69.8 us
    ppermute x9, waiting for transfers between devices, hop(): lax.ppermute(fall[-1], 'fsdp', down_pairs)  64.4 us
    ppermute x17, waiting for transfers between devices, swap_y(): return lax.ppermute(values, 'dp', [(at, at ^ 2) for at in range(4)])  54.2 us
    pallas_call x4, Pallas kernels, product_rows(): pl.pallas_call(rows_kernel, grid_spec=pltpu.PrefetchScalarGridSpec(num_sc...  49.5 us
    pallas_call x3, Pallas kernels, newton_update(): pl.pallas_call(functools.partial(newton_kernel, rate=rate), grid=(pairs,)...  44.5 us
    ppermute x23, starting transfers between devices, swap_core(): return lax.ppermute(values, 'dp', [(at, at ^ 1) for at in range(4)])  42.8 us
    unnamed x202, local copies, waits for them, and re-layouts  39.5 us
  transfers between devices with their start and end apart: 88, of which 28 were waited for; matrix products, arithmetic and copies ran while one was open for 19% of the time, Pallas kernels for 33%

profile of v6, /device:TPU:1, one launch (start us, length us, event | category | flops | bytes accessed | tf_op | source)
XLA Modules:
  0.0 901.3 jit_solution(718804249496775839)
XLA Ops:
  46.9 18.4 %mix_forward.1 = (bf16[256,2048]{1,0:T(8,128)(2,1)}, bf16[256,2048]{1,0:T(8,128)(2,1)}, bf16[256,2048]{1,0:T(8,128)(2,1)}, bf16[256,2048]{1,0:T(8,128)(2,1)}, f3...) custom-call(bf16[9,256,2048]{2,1,0:T(8,128)(2,1)} %hist_ref.3, ...), custom_call_target="tpu_custom_call" | custom-call | flops 1035000000 | bytes 3321000 | tf_op jit(solution)/shard_map/mix_forward/pallas_call | solution.py:297
  86.2 14.5 %collective-permute-done.10 = bf16[256,2048]{1,0:T(8,128)(2,1)S(1)} collective-permute-done((bf16[256,2048]{1,0:T(8,128)(2,1)S(1)}, bf16[256,2048]{1,0:T(8,128)(2,1)S(1)}, u32[]{:S(2)}, u32[]{:S(2)}) %collective-permute-start.10) | collective-permute-done | bytes 1048608 | tf_op jit(solution)/shard_map/ppermute | solution.py:750
  105.1 18.0 %collective-permute-done.12 = bf16[256,2048]{1,0:T(8,128)(2,1)} collective-permute-done((bf16[256,2048]{1,0:T(8,128)(2,1)S(1)}, bf16[256,2048]{1,0:T(8,128)(2,1)}, u32[]{:S(2)}, u32[]{:S(2)}) %collective-permute-start.12) | collective-permute-done | bytes 1048608 | tf_op jit(solution)/shard_map/ppermute | solution.py:750
  142.0 22.2 %collective-permute-done.18 = bf16[256,2048]{1,0:T(8,128)(2,1)S(1)} collective-permute-done((bf16[256,2048]{1,0:T(8,128)(2,1)}, bf16[256,2048]{1,0:T(8,128)(2,1)S(1)}, u32[]{:S(2)}, u32[]{:S(2)}) %collective-permute-start.18) | collective-permute-done | bytes 1048608 | tf_op jit(solution)/shard_map/ppermute | solution.py:750
  222.9 17.4 %mlp_up.1 = (bf16[1024,2048]{1,0:T(8,128)(2,1)}, f32[1024,2048]{1,0:T(8,128)}) custom-call(bf16[1024,2048]{1,0:T(8,128)(2,1)} %pad_maximum_fusion.2.normed_ref.left_refs_0_, bf16[2048,2048]{1,0:T(8,128)(2,1)} %constant_dynamic-update-slice_fusion.up_ref.right_refs_0__0_.right_refs_0__1_, f32[1,2048]{1,0:T(1,128)} %get-tuple-element.634.bias_ref), custom_call_target="tpu_custom_call" | custom-call | flops 977500032 | bytes 3136500 | tf_op jit(solution)/shard_map/mlp_up/pallas_call | solution.py:478
  256.0 10.8 %half_product.10 = bf16[1024,2048]{1,0:T(8,128)(2,1)} custom-call(bf16[1024,2048]{1,0:T(8,128)(2,1)} %pad_maximum_fusion.1.left_refs_0_.cot_ref.refs_0_, bf16[1024,2048]{1,0:T(8,128)(2,1)} %get-tuple-element.411.right_refs_0_.left_refs_0_), custom_call_target="tpu_custom_call" | custom-call | flops 632499968 | bytes 2029500 | tf_op jit(solution)/shard_map/half_product/pallas_call | solution.py:240
  273.7 11.9 %half_product.12 = f32[1024,2048]{1,0:T(8,128)} custom-call(bf16[1024,2048]{1,0:T(8,128)(2,1)} %pad_maximum_fusion.1.left_refs_0_.cot_ref.refs_0_, bf16[1024,2048]{1,0:T(8,128)(2,1)} %get-tuple-element.411.right_refs_0_.left_refs_0_), custom_call_target="tpu_custom_call" | custom-call | flops 632499968 | bytes 2029500 | tf_op jit(solution)/shard_map/half_product/pallas_call | solution.py:240
  312.0 15.9 %mlp_back.1 = (bf16[1024,2048]{1,0:T(8,128)(2,1)}, f32[1,2048]{1,0:T(1,128)}) custom-call(bf16[1024,2048]{1,0:T(8,128)(2,1)} %pad_maximum_fusion.1.left_refs_0_.cot_ref.refs_0_, bf16[2048,2048]{1,0:T(8,128)(2,1)} %constant_dynamic-update-slice_fusion.6.down_ref.right_refs_0__0_.right_refs_0__1_, f32[1024,2048]{1,0:T(8,128)} %get-tuple-element.342.slope_ref), custom_call_target="tpu_custom_call" | custom-call | flops 920000000 | bytes 2952000 | tf_op jit(solution)/shard_map/mlp_back/pallas_call | solution.py:514
  327.9 10.8 %half_product.11 = bf16[1024,2048]{1,0:T(8,128)(2,1)} custom-call(bf16[1024,2048]{1,0:T(8,128)(2,1)} %pad_maximum_fusion.2.normed_ref.left_refs_0_, bf16[1024,2048]{1,0:T(8,128)(2,1)} %get-tuple-element.365.right_refs_0_.left_refs_0_), custom_call_target="tpu_custom_call" | custom-call | flops 632499968 | bytes 2029500 | tf_op jit(solution)/shard_map/half_product/pallas_call | solution.py:240
  338.7 14.3 %product_rows.4 = (f32[512,2048]{1,0:T(8,128)}, bf16[512,2048]{1,0:T(8,128)(2,1)}) custom-call(s32[8]{0:T(128)} %stack.142.order_ref, bf16[1024,2048]{1,0:T(8,128)(2,1)} %get-tuple-element.365.right_refs_0_.left_refs_0_, bf16[2048,2048]{1,0:T(8,128)(2,1)} %constant_dynamic-update-slice_fusion.up_ref.right_refs_0__0_.right_refs_0__1_, ...), custom_call_target="tpu_custom_call" | custom-call | flops 805000000 | bytes 2583000 | tf_op jit(solution)/shard_map/product_rows/pallas_call | solution.py:204
  416.1 12.3 %half_product.13 = f32[1024,2048]{1,0:T(8,128)} custom-call(bf16[1024,2048]{1,0:T(8,128)(2,1)} %pad_maximum_fusion.2.normed_ref.left_refs_0_, bf16[1024,2048]{1,0:T(8,128)(2,1)} %get-tuple-element.365.right_refs_0_.left_refs_0_), custom_call_target="tpu_custom_call" | custom-call | flops 632499968 | bytes 2029500 | tf_op jit(solution)/shard_map/half_product/pallas_call | solution.py:240
  433.1 29.0 %collective-permute-done.38.part_refs_1__2_ = bf16[256,2048]{1,0:T(8,128)(2,1)S(1)} collective-permute-done((bf16[256,2048]{1,0:T(8,128)(2,1)S(1)}, bf16[256,2048]{1,0:T(8,128)(2,1)S(1)}, u32[]{:S(2)}, u32[]{:S(2)}) %collective-permute-start.38) | collective-permute-done | bytes 1048608 | tf_op jit(solution)/shard_map/ppermute | solution.py:728
  467.7 17.8 %collective-permute-done.43 = bf16[1024,512]{1,0:T(8,128)(2,1)S(1)} collective-permute-done((bf16[1024,512]{1,0:T(8,128)(2,1)S(1)}, bf16[1024,512]{1,0:T(8,128)(2,1)S(1)}, u32[]{:S(2)}, u32[]{:S(2)}) %collective-permute-start.43) | collective-permute-done | bytes 1048608 | tf_op jit(solution)/shard_map/ppermute | solution.py:721
  488.1 19.3 %collective-permute-done.41 = bf16[512,2048]{1,0:T(8,128)(2,1)S(1)} collective-permute-done((bf16[512,2048]{1,0:T(8,128)(2,1)S(1)}, bf16[512,2048]{1,0:T(8,128)(2,1)S(1)}, u32[]{:S(2)}, u32[]{:S(2)}) %collective-permute-start.41) | collective-permute-done | bytes 2097184 | tf_op jit(solution)/shard_map/ppermute | solution.py:724
  516.1 27.1 %attention_inner.1 = (bf16[1024,512]{1,0:T(8,128)(2,1)}, bf16[1024,512]{1,0:T(8,128)(2,1)}, bf16[1024,512]{1,0:T(8,128)(2,1)}, bf16[1024,512]{1,0:T(8,128)(2,1)}, f32[8,512]{1,0:T(8,128)}) custom-call(s32[4,3]{1,0:T(4,128)} %reduce_window_sum.18.ends_ref, bf16[1024,2048]{1,0:T(8,128)(2,1)} %pad_maximum_fusion.4.normed_refs_0_.left_refs_1_, ...), custom_call_target="tpu_custom_call" | custom-call | flops 1552499968 | bytes 4981500 | tf_op jit(solution)/shard_map/attention_inner/pallas_call | solution.py:601
  548.9 13.4 %product_rows.6 = (f32[1536,2048]{1,0:T(8,128)}, bf16[1536,2048]{1,0:T(8,128)(2,1)}) custom-call(s32[8]{0:T(128)} %stack.142.order_ref, bf16[1024,512]{1,0:T(8,128)(2,1)} %get-tuple-element.406.right_refs_0_.left_refs_0_, bf16[1024,512]{1,0:T(8,128)(2,1)} %get-tuple-element.407.right_refs_1_.left_refs_1_, ...), custom_call_target="tpu_custom_call" | custom-call | flops 805000000 | bytes 2583000 | tf_op jit(solution)/shard_map/product_rows/pallas_call | solution.py:204
  574.4 14.5 %product_rows.7 = (f32[512,2048]{1,0:T(8,128)}, f32[512,2048]{1,0:T(8,128)}) custom-call(s32[8]{0:T(128)} %stack.142.order_ref, bf16[1024,2048]{1,0:T(8,128)(2,1)} %get-tuple-element.411.right_refs_0_.left_refs_0_, bf16[2048,2048]{1,0:T(8,128)(2,1)} %constant_dynamic-update-slice_fusion.6.down_ref.right_refs_0__0_.right_refs_0__1_, ...), custom_call_target="tpu_custom_call" | custom-call | flops 10350000128 | bytes 33210000 | tf_op jit(solution)/shard_map/product_rows/pallas_call | solution.py:204
  603.1 13.4 %collective-permute-done.49.part_refs_0__3_ = bf16[256,2048]{1,0:T(8,128)(2,1)} collective-permute-done((bf16[256,2048]{1,0:T(8,128)(2,1)}, bf16[256,2048]{1,0:T(8,128)(2,1)}, u32[]{:S(2)}, u32[]{:S(2)}) %collective-permute-start.49) | collective-permute-done | bytes 1048608 | tf_op jit(solution)/shard_map/ppermute | solution.py:728
  667.1 15.0 %collective-permute-done.53 = bf16[256,1024]{1,0:T(8,128)(2,1)} collective-permute-done((bf16[256,1024]{1,0:T(8,128)(2,1)S(1)}, bf16[256,1024]{1,0:T(8,128)(2,1)}, u32[]{:S(2)}, u32[]{:S(2)}) %collective-permute-start.53) | collective-permute-done | bytes 524320 | tf_op jit(solution)/shard_map/ppermute | solution.py:728
  707.2 13.2 %collective-permute-done.64 = f32[1,256,256]{2,1,0:T(8,128)S(1)} collective-permute-done((f32[1,256,256]{2,1,0:T(8,128)S(1)}, f32[1,256,256]{2,1,0:T(8,128)S(1)}, u32[]{:S(2)}, u32[]{:S(2)}) %collective-permute-start.64) | collective-permute-done | bytes 262176 | tf_op jit(solution)/shard_map/ppermute | solution.py:721
  743.4 19.1 %newton_update.3 = (f32[2,256,2048]{2,1,0:T(8,128)}, bf16[2,256,2048]{2,1,0:T(8,128)(2,1)}) custom-call(f32[2,256,256]{2,1,0:T(8,128)} %pad_maximum_fusion.19.gram_ref, f32[2,256,2048]{2,1,0:T(8,128)} %get-tuple-element.247.mom_ref, f32[2,256,2048]{2,1,0:T(8,128)} %master_ref.3), custom_call_target="tpu_custom_call" | custom-call | flops 13799999488 | bytes 44280000 | tf_op jit(solution)/shard_map/newton_update/pallas_call | solution.py:692
  793.6 34.4 %mix_backward.1 = (bf16[9,256,2048]{2,1,0:T(8,128)(2,1)}, f32[16,2048]{1,0:T(8,128)}, f32[36,2048]{1,0:T(8,128)}, f32[37,36]{1,0:T(8,128)}) custom-call(bf16[9,256,2048]{2,1,0:T(8,128)(2,1)} %hist_ref.3, bf16[256,2048]{1,0:T(8,128)(2,1)} %cot_ref.1, f32[256,1]{1,0:T(8,128)} %copy.51.tok_ref, ...), custom_call_target="tpu_custom_call" | custom-call | flops 21849999360 | bytes 70110000 | tf_op jit(solution)/shard_map/mix_backward/pallas_call | solution.py:422
  836.9 12.6 %newton_update.5 = (f32[2,256,512]{2,1,0:T(8,128)}, bf16[2,256,512]{2,1,0:T(8,128)(2,1)}) custom-call(f32[4,256,256]{2,1,0:T(8,128)} %pad_maximum_fusion.18.gram_ref, f32[4,256,512]{2,1,0:T(8,128)} %get-tuple-element.243.mom_ref, f32[4,256,512]{2,1,0:T(8,128)} %master_ref.5), custom_call_target="tpu_custom_call" | custom-call | flops 13799999488 | bytes 44280000 | tf_op jit(solution)/shard_map/newton_update/pallas_call | solution.py:692
  854.8 12.8 %newton_update.4 = (f32[2,256,512]{2,1,0:T(8,128)}, bf16[2,256,512]{2,1,0:T(8,128)(2,1)}) custom-call(f32[4,256,256]{2,1,0:T(8,128)} %pad_maximum_fusion.18.gram_ref, f32[4,256,512]{2,1,0:T(8,128)} %get-tuple-element.243.mom_ref, f32[4,256,512]{2,1,0:T(8,128)} %master_ref.5), custom_call_target="tpu_custom_call" | custom-call | flops 13799999488 | bytes 44280000 | tf_op jit(solution)/shard_map/newton_update/pallas_call | solution.py:692
  (529 shorter events, 490.9 us)
Async XLA Ops:
  131.8 47.2 %collective-permute-start.23 = (bf16[512,2048]{1,0:T(8,128)(2,1)}, bf16[512,2048]{1,0:T(8,128)(2,1)}, u32[]{:S(2)}, u32[]{:S(2)}) collective-permute-start(bf16[512,2048]{1,0:T(8,128)(2,1)} %get-tuple-element.298), channel_id=1, source_target_pairs={{0,16},{8,24},{16,0},{24,8},{1,17},{9,25},{17,1},{25,9},{2,18},{10... | collective-permute-start | bytes 6291464 | tf_op jit(solution)/shard_map/ppermute | solution.py:721
  173.0 99.5 %collective-permute-start.31 = (bf16[512,2048]{1,0:T(8,128)(2,1)}, bf16[512,2048]{1,0:T(8,128)(2,1)}, u32[]{:S(2)}, u32[]{:S(2)}) collective-permute-start(bf16[512,2048]{1,0:T(8,128)(2,1)} %get-tuple-element.298), channel_id=1, source_target_pairs={{0,8},{8,0},{16,24},{24,16},{1,9},{9,1},{17,25},{25,17},{2,10},{10... | collective-permute-start | bytes 6291464 | tf_op jit(solution)/shard_map/ppermute | solution.py:718
  191.1 55.9 %collective-permute-start.25 = (bf16[512,2048]{1,0:T(8,128)(2,1)S(1)}, bf16[512,2048]{1,0:T(8,128)(2,1)}, u32[]{:S(2)}, u32[]{:S(2)}) collective-permute-start(bf16[512,2048]{1,0:T(8,128)(2,1)S(1)} %pad_maximum_fusion.10), channel_id=1, source_target_pairs={{2,0},{3,1},{4,2},{5,3},{6,4},{7,5},{10,8},{11,9},{12,10},{13,11},... | collective-permute-start | bytes 6291464 | tf_op jit(solution)/shard_map/ppermute | solution.py:750
  192.4 54.7 %collective-permute-start.24 = (bf16[512,2048]{1,0:T(8,128)(2,1)S(1)}, bf16[512,2048]{1,0:T(8,128)(2,1)}, u32[]{:S(2)}, u32[]{:S(2)}) collective-permute-start(bf16[512,2048]{1,0:T(8,128)(2,1)S(1)} %pad_maximum_fusion.10), channel_id=1, source_target_pairs={{0,2},{1,3},{2,4},{3,5},{4,6},{5,7},{8,10},{9,11},{10,12},{11,13},... | collective-permute-start | bytes 6291464 | tf_op jit(solution)/shard_map/ppermute | solution.py:749
  204.9 87.3 %collective-permute-start.32 = (bf16[512,2048]{1,0:T(8,128)(2,1)}, bf16[512,2048]{1,0:T(8,128)(2,1)}, u32[]{:S(2)}, u32[]{:S(2)}) collective-permute-start(bf16[512,2048]{1,0:T(8,128)(2,1)} %collective-permute-done.23), channel_id=1, source_target_pairs={{0,8},{8,0},{16,24},{24,16},{1,9},{9,1},{17,25},{25,17},{2,10},{10... | collective-permute-start | bytes 6291464 | tf_op jit(solution)/shard_map/ppermute | solution.py:718
  247.0 51.0 %collective-permute-start.27 = (bf16[512,2048]{1,0:T(8,128)(2,1)}, bf16[512,2048]{1,0:T(8,128)(2,1)}, u32[]{:S(2)}, u32[]{:S(2)}) collective-permute-start(bf16[512,2048]{1,0:T(8,128)(2,1)} %collective-permute-done.24), channel_id=1, source_target_pairs={{2,4},{3,5},{4,6},{5,7},{10,12},{11,13},{12,14},{13,15},{18,20},{1... | collective-permute-start | bytes 6291464 | tf_op jit(solution)/shard_map/ppermute | solution.py:749
  249.1 49.0 %collective-permute-start.28 = (bf16[512,2048]{1,0:T(8,128)(2,1)}, bf16[512,2048]{1,0:T(8,128)(2,1)}, u32[]{:S(2)}, u32[]{:S(2)}) collective-permute-start(bf16[512,2048]{1,0:T(8,128)(2,1)} %collective-permute-done.25), channel_id=1, source_target_pairs={{2,0},{3,1},{4,2},{5,3},{10,8},{11,9},{12,10},{13,11},{18,16},{19,... | collective-permute-start | bytes 6291464 | tf_op jit(solution)/shard_map/ppermute | solution.py:750
  303.2 61.0 %collective-permute-start.33 = (bf16[512,2048]{1,0:T(8,128)(2,1)}, bf16[512,2048]{1,0:T(8,128)(2,1)}, u32[]{:S(2)}, u32[]{:S(2)}) collective-permute-start(bf16[512,2048]{1,0:T(8,128)(2,1)} %collective-permute-done.27), channel_id=1, source_target_pairs={{4,6},{5,7},{12,14},{13,15},{20,22},{21,23},{28,30},{29,31}} | collective-permute-start | bytes 6291464 | tf_op jit(solution)/shard_map/ppermute | solution.py:749
  305.2 59.0 %collective-permute-start.34 = (bf16[512,2048]{1,0:T(8,128)(2,1)}, bf16[512,2048]{1,0:T(8,128)(2,1)}, u32[]{:S(2)}, u32[]{:S(2)}) collective-permute-start(bf16[512,2048]{1,0:T(8,128)(2,1)} %collective-permute-done.28), channel_id=1, source_target_pairs={{2,0},{3,1},{10,8},{11,9},{18,16},{19,17},{26,24},{27,25}} | collective-permute-start | bytes 6291464 | tf_op jit(solution)/shard_map/ppermute | solution.py:750
  308.5 64.2 %collective-permute-start.35 = (bf16[768,2048]{1,0:T(8,128)(2,1)}, bf16[768,2048]{1,0:T(8,128)(2,1)}, u32[]{:S(2)}, u32[]{:S(2)}) collective-permute-start(bf16[768,2048]{1,0:T(8,128)(2,1)} %slice.471), channel_id=1, source_target_pairs={{0,1},{1,0},{2,3},{3,2},{4,5},{5,4},{6,7},{7,6},{8,9},{9,8},{10,11... | collective-permute-start | bytes 9437192 | tf_op jit(solution)/shard_map/ppermute | solution.py:724
  372.7 89.4 %collective-permute-start.36 = (bf16[512,2048]{1,0:T(8,128)(2,1)}, bf16[512,2048]{1,0:T(8,128)(2,1)}, u32[]{:S(2)}, u32[]{:S(2)}) collective-permute-start(bf16[512,2048]{1,0:T(8,128)(2,1)} %get-tuple-element.352), channel_id=1, source_target_pairs={{0,1},{1,0},{2,3},{3,2},{4,5},{5,4},{6,7},{7,6},{8,9},{9,8},{10,11... | collective-permute-start | bytes 6291464 | tf_op jit(solution)/shard_map/ppermute | solution.py:724
  409.9 52.2 %collective-permute-start.38 = (bf16[256,2048]{1,0:T(8,128)(2,1)S(1)}, bf16[256,2048]{1,0:T(8,128)(2,1)S(1)}, u32[]{:S(2)}, u32[]{:S(2)}) collective-permute-start(bf16[256,2048]{1,0:T(8,128)(2,1)S(1)} %get-tuple-element.510), channel_id=1, source_target_pairs={{0,4},{1,5},{2,6},{3,7},{4,0},{5,1},{6,2},{7,3},{8,12},{9,13},{10,... | collective-permute-start | bytes 3145736 | tf_op jit(solution)/shard_map/ppermute | solution.py:728
  428.4 58.5 %collective-permute-start.44 = (bf16[512,2048]{1,0:T(8,128)(2,1)}, bf16[512,2048]{1,0:T(8,128)(2,1)S(1)}, u32[]{:S(2)}, u32[]{:S(2)}) collective-permute-start(bf16[512,2048]{1,0:T(8,128)(2,1)} %get-tuple-element.375), channel_id=1, source_target_pairs={{0,8},{8,0},{16,24},{24,16},{1,9},{9,1},{17,25},{25,17},{2,10},{10... | collective-permute-start | bytes 6291464 | tf_op jit(solution)/shard_map/ppermute | solution.py:718
  509.1 54.4 %collective-permute-start.46 = (bf16[256,2048]{1,0:T(8,128)(2,1)}, bf16[256,2048]{1,0:T(8,128)(2,1)S(1)}, u32[]{:S(2)}, u32[]{:S(2)}) collective-permute-start(bf16[256,2048]{1,0:T(8,128)(2,1)} %add_convert_fusion.5), channel_id=1, source_target_pairs={{0,16},{8,24},{16,0},{24,8},{1,17},{9,25},{17,1},{25,9},{2,18},{10... | collective-permute-start | bytes 3145736 | tf_op jit(solution)/shard_map/ppermute | solution.py:721
  509.1 54.4 %collective-permute-start.45 = (bf16[256,2048]{1,0:T(8,128)(2,1)}, bf16[256,2048]{1,0:T(8,128)(2,1)}, u32[]{:S(2)}, u32[]{:S(2)}) collective-permute-start(bf16[256,2048]{1,0:T(8,128)(2,1)} %get-tuple-element.376), channel_id=1, source_target_pairs={{0,4},{1,5},{2,6},{3,7},{4,0},{5,1},{6,2},{7,3},{8,12},{9,13},{10,... | collective-permute-start | bytes 3145736 | tf_op jit(solution)/shard_map/ppermute | solution.py:728
  564.5 52.0 %collective-permute-start.51 = (bf16[1536,2048]{1,0:T(8,128)(2,1)}, bf16[1536,2048]{1,0:T(8,128)(2,1)S(1)}, u32[]{:S(2)}, u32[]{:S(2)}) collective-permute-start(bf16[1536,2048]{1,0:T(8,128)(2,1)} %get-tuple-element.410), channel_id=1, source_target_pairs={{0,8},{8,0},{16,24},{24,16},{1,9},{9,1},{17,25},{25,17},{2,10},{10... | collective-permute-start | bytes 18874376 | tf_op jit(solution)/shard_map/ppermute | solution.py:718
  569.2 47.3 %collective-permute-start.47 = (bf16[1024,1024]{1,0:T(8,128)(2,1)}, bf16[1024,1024]{1,0:T(8,128)(2,1)}, u32[]{:S(2)}, u32[]{:S(2)}) collective-permute-start(bf16[1024,1024]{1,0:T(8,128)(2,1)} %half_product.14), channel_id=1, source_target_pairs={{0,1},{1,0},{2,3},{3,2},{4,5},{5,4},{6,7},{7,6},{8,9},{9,8},{10,11... | collective-permute-start | bytes 6291464 | tf_op jit(solution)/shard_map/ppermute | solution.py:724
  617.6 64.5 %collective-permute-start.52 = (bf16[1024,512]{1,0:T(8,128)(2,1)}, bf16[1024,512]{1,0:T(8,128)(2,1)}, u32[]{:S(2)}, u32[]{:S(2)}) collective-permute-start(bf16[1024,512]{1,0:T(8,128)(2,1)} %half_product.16), channel_id=1, source_target_pairs={{0,1},{1,0},{2,3},{3,2},{4,5},{5,4},{6,7},{7,6},{8,9},{9,8},{10,11... | collective-permute-start | bytes 3145736 | tf_op jit(solution)/shard_map/ppermute | solution.py:724
  627.4 54.6 %collective-permute-start.57 = (bf16[256,2048]{1,0:T(8,128)(2,1)}, bf16[256,2048]{1,0:T(8,128)(2,1)}, u32[]{:S(2)}, u32[]{:S(2)}) collective-permute-start(bf16[256,2048]{1,0:T(8,128)(2,1)} %get-tuple-element.507), channel_id=1, source_target_pairs={{0,16},{8,24},{16,0},{24,8},{1,17},{9,25},{17,1},{25,9},{2,18},{10... | collective-permute-start | bytes 3145736 | tf_op jit(solution)/shard_map/ppermute | solution.py:721
  628.1 54.0 %collective-permute-start.56 = (bf16[256,2048]{1,0:T(8,128)(2,1)}, bf16[256,2048]{1,0:T(8,128)(2,1)}, u32[]{:S(2)}, u32[]{:S(2)}) collective-permute-start(bf16[256,2048]{1,0:T(8,128)(2,1)} %get-tuple-element.508), channel_id=1, source_target_pairs={{0,16},{8,24},{16,0},{24,8},{1,17},{9,25},{17,1},{25,9},{2,18},{10... | collective-permute-start | bytes 3145736 | tf_op jit(solution)/shard_map/ppermute | solution.py:721
  690.4 48.1 %collective-permute-start.59 = (bf16[1024,512]{1,0:T(8,128)(2,1)}, bf16[1024,512]{1,0:T(8,128)(2,1)S(1)}, u32[]{:S(2)}, u32[]{:S(2)}) collective-permute-start(bf16[1024,512]{1,0:T(8,128)(2,1)} %half_product.17), channel_id=1, source_target_pairs={{0,1},{1,0},{2,3},{3,2},{4,5},{5,4},{6,7},{7,6},{8,9},{9,8},{10,11... | collective-permute-start | bytes 3145736 | tf_op jit(solution)/shard_map/ppermute | solution.py:724
  690.9 47.6 %collective-permute-start.67 = (bf16[256,2048]{1,0:T(8,128)(2,1)S(1)}, bf16[256,2048]{1,0:T(8,128)(2,1)S(1)}, u32[]{:S(2)}, u32[]{:S(2)}) collective-permute-start(bf16[256,2048]{1,0:T(8,128)(2,1)S(1)} %copy-done.48), channel_id=1, source_target_pairs={{0,16},{8,24},{16,0},{24,8},{1,17},{9,25},{17,1},{25,9},{2,18},{10... | collective-permute-start | bytes 3145736 | tf_op jit(solution)/shard_map/ppermute | solution.py:721
  782.1 54.8 %collective-permute-start.76 = (bf16[2,256,2048]{2,1,0:T(8,128)(2,1)S(1)}, bf16[2,256,2048]{2,1,0:T(8,128)(2,1)}, u32[]{:S(2)}, u32[]{:S(2)}) collective-permute-start(bf16[2,256,2048]{2,1,0:T(8,128)(2,1)S(1)} %copy-done.38), channel_id=1, source_target_pairs={{0,8},{8,0},{16,24},{24,16},{1,9},{9,1},{17,25},{25,17},{2,10},{10... | collective-permute-start | bytes 6291464 | tf_op jit(solution)/shard_map/ppermute | solution.py:718
  782.8 54.1 %collective-permute-start.75 = (bf16[2,256,2048]{2,1,0:T(8,128)(2,1)S(1)}, bf16[2,256,2048]{2,1,0:T(8,128)(2,1)}, u32[]{:S(2)}, u32[]{:S(2)}) collective-permute-start(bf16[2,256,2048]{2,1,0:T(8,128)(2,1)S(1)} %copy-done.38), channel_id=1, source_target_pairs={{0,16},{8,24},{16,0},{24,8},{1,17},{9,25},{17,1},{25,9},{2,18},{10... | collective-permute-start | bytes 6291464 | tf_op jit(solution)/shard_map/ppermute | solution.py:721
  (154 other events, 2507.8 us)
